TPU v7x, 32 devices: a whole 2x2x4 slice. The times are simulated.
32 devices in a mesh: gx: 16 (over z, y, x), gy: 2 (over core).
Axes of the slice: x: 2, y: 2, z: 4, core: 2. Of those that a mesh axis runs over, the one named last changes fastest.
Arguments:
- velocity: float32 [3, 128, 96, 256], P(None, 'gx', 'gy'), may hold values from -6 to 6
- pressure: float32 [128, 96, 256], P('gx', 'gy'), may hold values from -6 to 6
- viscosity: float32 [128, 96, 256], P('gx', 'gy'), may hold values from 0.12 to 0.6
- wind_profile: float32 [256], replicated, may hold values from 0.5 to 1.5
- panel_area: float32 [4096], P('gy'), may hold values from 0.5 to 2
- slot_cell: int32 [2, 4096], P('gy', 'gx'), may hold values from 0 to 98303
- slot_panel: int32 [2, 4096], P('gy'), may hold values from -1 to 2047, as said below
- panel_shapes: bfloat16 [4096, 2048], P('gy', 'gx'), may hold values from -0.09375 to 0.09375
- node_shapes: bfloat16 [1024, 2048], P(None, 'gx'), may hold values from -0.125 to 0.125
- damper_node: int32 [128], P('gy'), may hold values from 0 to 1022
- damper_viscous: float32 [128], P('gy'), may hold values from 0.2 to 2
- damper_hysteretic: float32 [128], P('gy'), may hold values from 0.2 to 2
- frequency: float32 [2048], P('gx'), may hold values from 0.2 to 1.8
- damping_ratio: float32 [2048], P('gx'), may hold values from 0.05 to 0.5
- modal_state: float32 [2, 2048], P(None, 'gx'), may hold values from -6 to 6
- damper_state: float32 [128], P('gy'), may hold values from -1 to 1
Outputs:
- velocity_next: float32 [3, 128, 96, 256], P(None, 'gx', 'gy')
- pressure_next: float32 [128, 96, 256], P('gx', 'gy')
- modal_next: float32 [2, 2048], P(None, 'gx')
- damper_next: float32 [128], P('gy')
Inputs may be any that keep to these rules, and one draw needn't show every extreme that they name: `slot_panel`: in every row each panel number 0 to 2047 stands in exactly one slot; every other slot holds -1.
All inputs are finite; a program needn't handle non-finite values.
Results may differ from a plain program's by a relative error of at most 0.0013.
Values may be sent and summed in bfloat16 or wider, within the bound.
No kernel may reach another device: no remote copies, remote signals or barrier semaphores. Data moves between devices by JAX's collectives and lax.ppermute only.
A program may use at most 64 MiB of HBM per device.

v0:
```python
import jax
import jax.numpy as jnp
from jax import lax
from jax.sharding import PartitionSpec as P

time_step = 0.1
sound_squared = 1.0
modal_step = 0.5
hysteresis_gain = 1.0
shape_beta = 0.5
shape_gamma = 0.5
spring_rate = 0.5


def padded_2(value, sides, width):
    for axis, dim in sides:
        size, length = (lax.axis_size(axis), value.shape[dim])
        up = [(i, (i + 1) % size) for i in range(size - 1)]
        down = [(j, i) for i, j in up]
        last = lax.slice_in_dim(value, length - width, length, axis=dim)
        first = lax.slice_in_dim(value, 0, width, axis=dim)
        before = lax.ppermute(last, axis, up)
        after = lax.ppermute(first, axis, down)
        value = jnp.concatenate([before, value, after], axis=dim)
    return value


def advance(padded, local_viscosity, wind_profile):
    centre_cells = padded[:, 1:-1, 1:-1, 1:-1]
    ahead_cells = padded[:, 2:, 1:-1, 1:-1]
    behind_cells = padded[:, :-2, 1:-1, 1:-1]
    right_cells = padded[:, 1:-1, 2:, 1:-1]
    left_cells = padded[:, 1:-1, :-2, 1:-1]
    above_cells = padded[:, 1:-1, 1:-1, 2:]
    below_cells = padded[:, 1:-1, 1:-1, :-2]
    slope_stream = 0.5 * (ahead_cells - behind_cells)
    slope_span = 0.5 * (right_cells - left_cells)
    slope_vertical = 0.5 * (above_cells - below_cells)
    laplacian = (
        ahead_cells
        + behind_cells
        + right_cells
        + left_cells
        + above_cells
        + below_cells
        - 6.0 * centre_cells
    )
    pressure_slope = jnp.stack([slope_stream[3], slope_span[3], slope_vertical[3]])
    velocity_new = centre_cells[:3] + time_step * (
        -wind_profile * slope_stream[:3] + local_viscosity * laplacian[:3] - pressure_slope
    )
    pressure_new = centre_cells[3] - time_step * sound_squared * (
        slope_stream[0] + slope_span[1] + slope_vertical[2]
    )
    return jnp.concatenate([velocity_new, pressure_new[None]], axis=0)


def vertical_pad(fields):
    return jnp.pad(fields, ((0, 0), (0, 0), (0, 0), (1, 1)))


def body(
    velocity,
    pressure,
    viscosity,
    wind_profile,
    panel_area,
    slot_cell,
    slot_panel,
    panel_shapes,
    node_shapes,
    damper_node,
    damper_viscous,
    damper_hysteretic,
    frequency,
    damping_ratio,
    modal_state,
    damper_state,
):
    fields = jnp.concatenate([velocity, pressure[None]], axis=0)
    for substep in range(2):
        padded = padded_2(fields, (("gx", 1), ("gy", 2)), 1)
        fields = advance(vertical_pad(padded), viscosity, wind_profile)
    velocity_next = fields[:3]
    pressure_next = fields[3]
    slot_count = slot_cell.shape[1]
    panel_count = panel_area.shape[0]
    flat_pressure = pressure_next.reshape(-1)
    sampled = flat_pressure[slot_cell[0]]
    panel_ids = slot_panel[0]
    own_ids = lax.dynamic_slice_in_dim(panel_ids, lax.axis_index("gx") * slot_count, slot_count)
    safe_ids = jnp.where(own_ids < 0, 0, own_ids)
    own_loads = (panel_area[safe_ids] * sampled).astype(jnp.bfloat16)
    target = jnp.where(own_ids < 0, panel_count, own_ids)
    partial_value = (
        jnp.zeros((panel_count + 1,), jnp.float32)
        .at[target]
        .set(own_loads.astype(jnp.float32))[:panel_count]
    )
    panel_loads = lax.psum(partial_value, "gx").astype(jnp.bfloat16)
    panel_part = jnp.dot(panel_loads, panel_shapes, preferred_element_type=jnp.float32)
    node_numbers = jnp.arange(node_shapes.shape[0], dtype=jnp.int32)
    upper_pick = (node_numbers[None, :] == damper_node[:, None] + 1).astype(jnp.float32)
    lower_pick = (node_numbers[None, :] == damper_node[:, None]).astype(jnp.float32)
    selector = (upper_pick - lower_pick).astype(jnp.bfloat16)
    drift_shapes = jnp.dot(selector, node_shapes, preferred_element_type=jnp.float32)
    panel_modal = lax.psum(panel_part, "gy")
    displacement = modal_state[0]
    modal_velocity = modal_state[1]
    hysteresis = damper_state
    for modal_turn in range(2):
        stretch, stretch_rate = lax.psum(
            (
                jnp.dot(drift_shapes, displacement, precision=lax.Precision.HIGHEST),
                jnp.dot(drift_shapes, modal_velocity, precision=lax.Precision.HIGHEST),
            ),
            "gx",
        )
        hysteresis = hysteresis + modal_step * (
            hysteresis_gain * stretch_rate
            - shape_beta * jnp.abs(stretch_rate) * hysteresis
            - shape_gamma * stretch_rate * jnp.abs(hysteresis)
        )
        damper_force = -(
            damper_viscous * stretch_rate + spring_rate * stretch + damper_hysteretic * hysteresis
        )
        generalized = jnp.dot(damper_force, drift_shapes, precision=lax.Precision.HIGHEST)
        modal_load = panel_modal + lax.psum(generalized, "gy")
        acceleration = (
            modal_load
            - 2.0 * damping_ratio * frequency * modal_velocity
            - frequency * frequency * displacement
        )
        modal_velocity = modal_velocity + modal_step * acceleration
        displacement = displacement + modal_step * modal_velocity
    return (velocity_next, pressure_next, jnp.stack([displacement, modal_velocity]), hysteresis)


def solution(mesh):
    placed = (
        P(None, "gx", "gy", None),
        P("gx", "gy", None),
        P("gx", "gy", None),
        P(),
        P("gy"),
        P("gy", "gx"),
        P("gy", None),
        P("gy", "gx"),
        P(None, "gx"),
        P("gy"),
        P("gy"),
        P("gy"),
        P("gx"),
        P("gx"),
        P(None, "gx"),
        P("gy"),
    )
    return jax.shard_map(
        body,
        mesh=mesh,
        in_specs=placed,
        out_specs=(P(None, "gx", "gy", None), P("gx", "gy", None), P(None, "gx"), P("gy")),
        check_vma=False,
    )
```

profile of v0, /device:TPU:0, one launch (start us, length us, event | category | flops | bytes accessed | tf_op | source)
XLA Modules:
  0.0 157.6 jit_solution(6759244853942315606)
XLA Ops:
  0.7 1.2 fusion.21
  1.9 4.9 %collective-permute-start.1 = (f32[4,1,48,256]{3,2,1,0:T(8,128)S(1)}, f32[4,1,48,256]{3,2,1,0:T(8,128)S(1)}, u32[]{:S(2)}, u32[]{:S(2)}) collective-permute-start(f32[4,1,48,256]{3,2,1,0:T(8,128)S(1)} %get-tuple-element.47), channel_id=1, source_target_pairs={{0,2},{2,4},{4,6},{6,8},{8,10},{10,12},{12,14},{14,16},{16,18},{18... | collective-permute-start | bytes 589832 | tf_op jit(solution)/shard_map/ppermute | solution.py:22
  6.7 1.3 collective-permute-start
  8.1 0.2 fusion.23
  8.3 0.1 convolution_bitcast_fusion.4
  8.5 0.7 compare_select_fusion.3
  9.2 0.1 convolution_bitcast_fusion.5
  9.3 1.5 collective-permute-done.1
  10.9 6.2 %collective-permute-done = f32[4,1,48,256]{3,2,1,0:T(8,128)S(1)} collective-permute-done((f32[4,1,48,256]{3,2,1,0:T(8,128)S(1)}, f32[4,1,48,256]{3,2,1,0:T(8,128)S(1)}, u32[]{:S(2)}, u32[]{:S(2)}) %collective-permute-start) | collective-permute-done | bytes 196640 | tf_op jit(solution)/shard_map/ppermute | solution.py:23
  17.0 0.1 pad_maximum_fusion.30
  17.1 1.3 collective-permute-start.3
  18.4 1.3 collective-permute-start.2
  19.7 1.8 %collective-permute-done.2 = f32[4,10,1,256]{3,2,1,0:T(1,128)S(1)} collective-permute-done((f32[4,10,1,256]{3,2,1,0:T(1,128)S(1)}, f32[4,10,1,256]{3,2,1,0:T(1,128)S(1)}, u32[]{:S(2)}, u32[]{:S(2)}) %collective-permute-start.2) | collective-permute-done | bytes 40992 | tf_op jit(solution)/shard_map/ppermute | solution.py:23
  21.5 3.5 %select_maximum_fusion.5 = f32[4,10,50,258]{3,2,1,0:T(8,128)S(1)} fusion(f32[4,10,1,256]{3,2,1,0:T(1,128)S(1)} %collective-permute-done.2, f32[4,10,1,256]{3,2,1,0:T(1,128)S(1)} %collective-permute-done.3, f32[4,1,48,256]{3,2,1,0:T(8,128)S(1)} %collective-permute-done, f32[4,1,48,256]{3,2,1,0:T(8,128)S(1)} %collective-permute-done.1, ...), kind=kLoop, calls=%fused_computation.10 | loop fusion | flops 7224000 | bytes 4112000 | tf_op jit(solution)/shard_map/concatenate | solution.py:24
  25.0 0.7 subtract_multiply_fusion.3
  25.7 1.2 subtract_multiply_fusion.5
  26.9 0.2 bitcast_subtract_fusion.1
  27.1 0.9 copy-done.9
  28.0 0.5 copy-done.6
  28.5 1.2 fusion.13
  29.8 3.4 %collective-permute-start.5 = (f32[4,1,48,256]{3,2,1,0:T(8,128)S(1)}, f32[4,1,48,256]{3,2,1,0:T(8,128)S(1)}, u32[]{:S(2)}, u32[]{:S(2)}) collective-permute-start(f32[4,1,48,256]{3,2,1,0:T(8,128)S(1)} %get-tuple-element.41), channel_id=1, source_target_pairs={{0,2},{2,4},{4,6},{6,8},{8,10},{10,12},{12,14},{14,16},{16,18},{18... | collective-permute-start | bytes 589832 | tf_op jit(solution)/shard_map/ppermute | solution.py:22
  33.2 1.3 collective-permute-start.4
  34.6 3.1 %collective-permute-done.5 = f32[4,1,48,256]{3,2,1,0:T(8,128)S(1)} collective-permute-done((f32[4,1,48,256]{3,2,1,0:T(8,128)S(1)}, f32[4,1,48,256]{3,2,1,0:T(8,128)S(1)}, u32[]{:S(2)}, u32[]{:S(2)}) %collective-permute-start.5) | collective-permute-done | bytes 196640 | tf_op jit(solution)/shard_map/ppermute | solution.py:22
  37.7 5.0 %collective-permute-done.4 = f32[4,1,48,256]{3,2,1,0:T(8,128)S(1)} collective-permute-done((f32[4,1,48,256]{3,2,1,0:T(8,128)S(1)}, f32[4,1,48,256]{3,2,1,0:T(8,128)S(1)}, u32[]{:S(2)}, u32[]{:S(2)}) %collective-permute-start.4) | collective-permute-done | bytes 196640 | tf_op jit(solution)/shard_map/ppermute | solution.py:23
  42.7 1.6 collective-permute-start.7
  44.3 1.3 collective-permute-start.6
  45.6 1.7 %gather_fusion = f32[256]{0:T(256)S(1)} fusion(f32[2048]{0:T(1024)S(1)} %copy-done.1, s32[1024]{0:T(1024)S(1)} %pad_clamp_fusion.1), kind=kCustom, calls=%fused_computation | custom fusion | bytes 3072 | tf_op jit(solution)/shard_map/gather | solution.py:93
  47.4 4.5 %select_maximum_fusion = f32[4,10,50,258]{3,2,1,0:T(8,128)S(1)} fusion(f32[4,10,1,256]{3,2,1,0:T(1,128)S(1)} %collective-permute-done.6, f32[4,10,1,256]{3,2,1,0:T(1,128)S(1)} %collective-permute-done.7, f32[4,1,48,256]{3,2,1,0:T(8,128)S(1)} %collective-permute-done.4, f32[4,1,48,256]{3,2,1,0:T(8,128)S(1)} %collective-permute-done.5, ...), kind=kLoop, calls=%fused_computation.5 | loop fusion | flops 7224000 | bytes 4112000 | tf_op jit(solution)/shard_map/concatenate | solution.py:24
  51.9 2.3 %subtract_multiply_fusion = (f32[4,8,48,256]{3,2,1,0:T(8,128)S(1)}, f32[4,8,48,256]{3,2,1,0:T(8,128)}, f32[4,8,48,256]{3,2,1,0:T(8,128)}) fusion(f32[4,10,50,258]{3,2,1,0:T(8,128)S(1)} %select_maximum_fusion), kind=kLoop, calls=%fused_computation.48 | loop fusion | flops 786432 | bytes 7864320 | tf_op jit(solution)/shard_map/mul | solution.py:38
  54.3 3.0 %subtract_multiply_fusion.2 = (f32[4,8,48,256]{3,2,1,0:T(8,128)S(1)}, f32[4,8,48,256]{3,2,1,0:T(8,128)}, f32[4,8,48,256]{3,2,1,0:T(8,128)}, f32[4,8,48,256]{3,2,...) fusion(f32[4,1,48,256]{3,2,1,0:T(8,128)S(1)} %collective-permute-done.4, ...), kind=kLoop, calls=%fused_computation.50 | loop fusion | flops 6291456 | bytes 11485184 | tf_op jit(solution)/shard_map/mul | solution.py:36
  57.3 2.3 %fusion.17 = f32[8,48,256]{2,1,0:T(8,128)S(1)} fusion(f32[4,8,48,256]{3,2,1,0:T(8,128)S(1)} %get-tuple-element.25, f32[4,8,48,256]{3,2,1,0:T(8,128)S(1)} %get-tuple-element.31, f32[4,8,48,256]{3,2,1,0:T(8,128)S(1)} %get-tuple-element.16, f32[8,48,256]{2,1,0:T(8,128)S(1)} %copy-done.3, f32[4,8,48,256]{3,2,1,0:T(8,128)} %copy-done.8, ...), kind=kLoop, calls=%fused_computation.92 | loop fusion | flops 786432 | bytes 3145728 | tf_op jit(solution)/shard_map/sub | solution.py:52
  59.7 0.2 copy.20
  59.9 0.5 copy-done.13
  60.4 1.7 %gather_fusion.1 = f32[256]{0:T(256)S(1)} fusion(f32[98304]{0:T(1024)S(1)} %bitcast.94, s32[1024]{0:T(1024)S(1)} %pad_clamp_fusion), kind=kCustom, calls=%fused_computation.1 | custom fusion | bytes 3072 | tf_op jit(solution)/shard_map/gather | solution.py:89
  62.1 1.4 scatter_custom_fusion
  63.6 42.6 %all-reduce.3 = (bf16[2048]{0:T(1024)(128)(2,1)S(1)}, f32[64]{0:T(128)S(1)}, f32[64]{0:T(128)S(1)}) all-reduce(f32[2048]{0:T(1024)S(1)} %slice.234, f32[64]{0:T(128)S(1)} %convolution_bitcast_fusion.4, f32[64]{0:T(128)S(1)} %convolution_bitcast_fusion.5), channel_id=1, replica_groups=mesh['gx'=16,'gy'=2] {'gx'}, use_global_device_ids=true, to_apply=%region_1.2 | all-reduce | flops 2176 | bytes 13312 | tf_op jit(solution)/shard_map/psum | solution.py:100
  106.2 0.2 convolution_bitcast_fusion.6
  106.4 0.1 convolution_bitcast_fusion.3
  106.5 2.5 %all-reduce.4 = (f32[128]{0:T(128)S(1)}, f32[128]{0:T(128)S(1)}) all-reduce(f32[128]{0:T(128)S(1)} %convolution_bitcast_fusion.6, f32[128]{0:T(128)S(1)} %convolution_bitcast_fusion.3), channel_id=1, replica_groups=mesh['gx'=16,'gy'=2] {'gy'}, use_global_device_ids=true, to_apply=%region_2.3 | all-reduce | flops 256 | bytes 2048 | tf_op jit(solution)/shard_map/psum | solution.py:107
  109.0 0.1 convolution_bitcast_fusion.2
  109.1 0.2 convolution_bitcast_fusion.1
  109.3 1.1 slice.229
  110.4 1.8 %slice.228 = f32[1,8,48,256]{3,2,1,0:T(8,128)} slice(f32[4,8,48,256]{3,2,1,0:T(8,128)} %copy-done.7), slice={[3:4], [0:8], [0:48], [0:256]} | slice | bytes 786432 | tf_op jit(solution)/shard_map/slice | solution.py:48
  112.1 36.6 %all-reduce.2 = (f32[64]{0:T(128)S(1)}, f32[64]{0:T(128)S(1)}) all-reduce(f32[64]{0:T(128)S(1)} %convolution_bitcast_fusion.2, f32[64]{0:T(128)S(1)} %convolution_bitcast_fusion.1), channel_id=1, replica_groups=mesh['gx'=16,'gy'=2] {'gx'}, use_global_device_ids=true, to_apply=%region_6.7 | all-reduce | flops 128 | bytes 1024 | tf_op jit(solution)/shard_map/psum | solution.py:112
  148.7 0.1 convolution_bitcast_fusion
  148.9 2.5 %psum.63 = f32[128]{0:T(128)S(1)} all-reduce(f32[128]{0:T(128)S(1)} %convolution_bitcast_fusion), channel_id=1, replica_groups=mesh['gx'=16,'gy'=2] {'gy'}, use_global_device_ids=true, to_apply=%region_8.9 | all-reduce | flops 128 | bytes 1024 | tf_op jit(solution)/shard_map/psum | solution.py:128
  151.3 0.6 pad_maximum_fusion.34
  151.9 5.7 %fusion.6 = f32[3,8,48,256]{3,2,1,0:T(8,128)} fusion(f32[3,8,48,256]{3,2,1,0:T(8,128)S(1)} %fusion.13, f32[4,8,48,256]{3,2,1,0:T(8,128)} %get-tuple-element.27, f32[1,8,48,256]{3,2,1,0:T(8,128)S(1)} %copy-done.5, f32[4,8,48,256]{3,2,1,0:T(8,128)} %get-tuple-element.26, f32[4,8,48,256]{3,2,1,0:T(8,128)} %get-tuple-element.32, ...), kind=kLoop, calls=%fused_computation.60 | loop fusion | flops 4718592 | bytes 12583936 | tf_op jit(solution)/shard_map/add | solution.py:49
  (64 shorter events, 0.4 us)
Async XLA Ops:
  0.6 105.5 %copy-start = (bf16[2048,128]{1,0:T(8,128)(2,1)S(1)}, bf16[2048,128]{1,0:T(8,128)(2,1)}, u32[]{:S(2)}) copy-start(bf16[2048,128]{1,0:T(8,128)(2,1)} %param.23) | copy-start | bytes 1572868
  0.6 16.4 %copy-start.2 = (f32[3,8,48,256]{3,2,1,0:T(8,128)S(1)}, f32[3,8,48,256]{3,2,1,0:T(8,128)}, u32[]{:S(2)}) copy-start(f32[3,8,48,256]{3,2,1,0:T(8,128)} %param.16) | copy-start | bytes 3538948
  0.7 16.4 %copy-start.3 = (f32[8,48,256]{2,1,0:T(8,128)S(1)}, f32[8,48,256]{2,1,0:T(8,128)}, u32[]{:S(2)}) copy-start(f32[8,48,256]{2,1,0:T(8,128)} %param.17) | copy-start | bytes 1179652
  0.7 7.4 %copy-start.24 = (s32[64]{0:T(128)S(1)}, s32[64]{0:T(128)}, u32[]{:S(2)}) copy-start(s32[64]{0:T(128)} %param.25) | copy-start | bytes 772
  0.7 7.4 %copy-start.23 = (bf16[1024,128]{1,0:T(8,128)(2,1)S(1)}, bf16[1024,128]{1,0:T(8,128)(2,1)}, u32[]{:S(2)}) copy-start(bf16[1024,128]{1,0:T(8,128)(2,1)} %param.24) | copy-start | bytes 786436
  0.7 7.6 %copy-start.14 = (f32[2,128]{1,0:T(2,128)S(1)}, f32[2,128]{1,0:T(2,128)}, u32[]{:S(2)}) copy-start(f32[2,128]{1,0:T(2,128)} %param.30) | copy-start | bytes 3076
  1.9 17.8 %copy-start.21 = (f32[256]{0:T(256)S(1)}, f32[256]{0:T(256)}, u32[]{:S(2)}) copy-start(f32[256]{0:T(256)} %param.19) | copy-start | bytes 3076
  1.9 9.0 %collective-permute-start.1 = (f32[4,1,48,256]{3,2,1,0:T(8,128)S(1)}, f32[4,1,48,256]{3,2,1,0:T(8,128)S(1)}, u32[]{:S(2)}, u32[]{:S(2)}) collective-permute-start(f32[4,1,48,256]{3,2,1,0:T(8,128)S(1)} %get-tuple-element.47), channel_id=1, source_target_pairs={{0,2},{2,4},{4,6},{6,8},{8,10},{10,12},{12,14},{14,16},{16,18},{18... | collective-permute-start | bytes 589832 | tf_op jit(solution)/shard_map/ppermute | solution.py:22
  6.7 10.3 %collective-permute-start = (f32[4,1,48,256]{3,2,1,0:T(8,128)S(1)}, f32[4,1,48,256]{3,2,1,0:T(8,128)S(1)}, u32[]{:S(2)}, u32[]{:S(2)}) collective-permute-start(f32[4,1,48,256]{3,2,1,0:T(8,128)S(1)} %get-tuple-element.48), channel_id=1, source_target_pairs={{2,0},{4,2},{6,4},{8,6},{10,8},{12,10},{14,12},{16,14},{18,16},{20... | collective-permute-start | bytes 589832 | tf_op jit(solution)/shard_map/ppermute | solution.py:23
  17.1 2.6 %collective-permute-start.3 = (f32[4,10,1,256]{3,2,1,0:T(1,128)S(1)}, f32[4,10,1,256]{3,2,1,0:T(1,128)S(1)}, u32[]{:S(2)}, u32[]{:S(2)}) collective-permute-start(f32[4,10,1,256]{3,2,1,0:T(1,128)S(1)} %get-tuple-element.39), channel_id=1, source_target_pairs={{0,1},{2,3},{4,5},{6,7},{8,9},{10,11},{12,13},{14,15},{16,17},{18,... | collective-permute-start | bytes 122888 | tf_op jit(solution)/shard_map/ppermute | solution.py:22
  18.4 3.1 %collective-permute-start.2 = (f32[4,10,1,256]{3,2,1,0:T(1,128)S(1)}, f32[4,10,1,256]{3,2,1,0:T(1,128)S(1)}, u32[]{:S(2)}, u32[]{:S(2)}) collective-permute-start(f32[4,10,1,256]{3,2,1,0:T(1,128)S(1)} %get-tuple-element.40), channel_id=1, source_target_pairs={{1,0},{3,2},{5,4},{7,6},{9,8},{11,10},{13,12},{15,14},{17,16},{19,... | collective-permute-start | bytes 122888 | tf_op jit(solution)/shard_map/ppermute | solution.py:23
  25.7 1.2 copy-start.8
  26.9 1.1 copy-start.9
  26.9 1.6 %copy-start.6 = (f32[4,8,48,256]{3,2,1,0:T(8,128)}, f32[4,8,48,256]{3,2,1,0:T(8,128)S(1)}, u32[]{:S(2)}) copy-start(f32[4,8,48,256]{3,2,1,0:T(8,128)S(1)} %get-tuple-element.22) | copy-start | bytes 4718596
  26.9 1.6 %copy-start.11 = (f32[8,48,256]{2,1,0:T(8,128)S(1)}, f32[8,48,256]{2,1,0:T(8,128)}, u32[]{:S(2)}) copy-start(f32[8,48,256]{2,1,0:T(8,128)} %param.18) | copy-start | bytes 1179652
  28.0 14.6 %copy-start.4 = (f32[1,8,48,256]{3,2,1,0:T(8,128)}, f32[1,8,48,256]{3,2,1,0:T(8,128)S(1)}, u32[]{:S(2)}) copy-start(f32[1,8,48,256]{3,2,1,0:T(8,128)S(1)} %get-tuple-element.43) | copy-start | bytes 1179652
  29.8 4.8 %copy-start.22 = (s32[1,256]{1,0:T(1,128)S(1)}, s32[1,256]{1,0:T(1,128)}, u32[]{:S(2)}) copy-start(s32[1,256]{1,0:T(1,128)} %param.21) | copy-start | bytes 3076
  29.8 15.8 %copy-start.1 = (f32[2048]{0:T(1024)S(1)}, f32[2048]{0:T(1024)}, u32[]{:S(2)}) copy-start(f32[2048]{0:T(1024)} %param.20) | copy-start | bytes 24580
  29.8 7.9 %collective-permute-start.5 = (f32[4,1,48,256]{3,2,1,0:T(8,128)S(1)}, f32[4,1,48,256]{3,2,1,0:T(8,128)S(1)}, u32[]{:S(2)}, u32[]{:S(2)}) collective-permute-start(f32[4,1,48,256]{3,2,1,0:T(8,128)S(1)} %get-tuple-element.41), channel_id=1, source_target_pairs={{0,2},{2,4},{4,6},{6,8},{8,10},{10,12},{12,14},{14,16},{16,18},{18... | collective-permute-start | bytes 589832 | tf_op jit(solution)/shard_map/ppermute | solution.py:22
  33.2 9.4 %collective-permute-start.4 = (f32[4,1,48,256]{3,2,1,0:T(8,128)S(1)}, f32[4,1,48,256]{3,2,1,0:T(8,128)S(1)}, u32[]{:S(2)}, u32[]{:S(2)}) collective-permute-start(f32[4,1,48,256]{3,2,1,0:T(8,128)S(1)} %get-tuple-element.42), channel_id=1, source_target_pairs={{2,0},{4,2},{6,4},{8,6},{10,8},{12,10},{14,12},{16,14},{18,16},{20... | collective-permute-start | bytes 589832 | tf_op jit(solution)/shard_map/ppermute | solution.py:23
  42.7 4.6 %collective-permute-start.7 = (f32[4,10,1,256]{3,2,1,0:T(1,128)S(1)}, f32[4,10,1,256]{3,2,1,0:T(1,128)S(1)}, u32[]{:S(2)}, u32[]{:S(2)}) collective-permute-start(f32[4,10,1,256]{3,2,1,0:T(1,128)S(1)} %get-tuple-element.34), channel_id=1, source_target_pairs={{0,1},{2,3},{4,5},{6,7},{8,9},{10,11},{12,13},{14,15},{16,17},{18,... | collective-permute-start | bytes 122888 | tf_op jit(solution)/shard_map/ppermute | solution.py:22
  44.3 3.1 %collective-permute-start.6 = (f32[4,10,1,256]{3,2,1,0:T(1,128)S(1)}, f32[4,10,1,256]{3,2,1,0:T(1,128)S(1)}, u32[]{:S(2)}, u32[]{:S(2)}) collective-permute-start(f32[4,10,1,256]{3,2,1,0:T(1,128)S(1)} %get-tuple-element.35), channel_id=1, source_target_pairs={{1,0},{3,2},{5,4},{7,6},{9,8},{11,10},{13,12},{15,14},{17,16},{19,... | collective-permute-start | bytes 122888 | tf_op jit(solution)/shard_map/ppermute | solution.py:23
  51.9 2.4 %copy-start.5 = (f32[1,8,48,256]{3,2,1,0:T(8,128)S(1)}, f32[1,8,48,256]{3,2,1,0:T(8,128)}, u32[]{:S(2)}) copy-start(f32[1,8,48,256]{3,2,1,0:T(8,128)} %copy-done.4) | copy-start | bytes 1179652
  57.3 2.3 %copy-start.7 = (f32[4,8,48,256]{3,2,1,0:T(8,128)}, f32[4,8,48,256]{3,2,1,0:T(8,128)S(1)}, u32[]{:S(2)}) copy-start(f32[4,8,48,256]{3,2,1,0:T(8,128)S(1)} %get-tuple-element.16) | copy-start | bytes 4718596
  57.3 2.3 %copy-start.10 = (f32[4,8,48,256]{3,2,1,0:T(8,128)}, f32[4,8,48,256]{3,2,1,0:T(8,128)S(1)}, u32[]{:S(2)}) copy-start(f32[4,8,48,256]{3,2,1,0:T(8,128)S(1)} %get-tuple-element.31) | copy-start | bytes 4718596
  59.6 0.7 copy-start.13
  59.7 46.7 %copy-start.15 = (f32[64]{0:T(128)S(1)}, f32[64]{0:T(128)}, u32[]{:S(2)}) copy-start(f32[64]{0:T(128)} %param.27) | copy-start | bytes 772
  59.7 46.7 %copy-start.16 = (f32[64]{0:T(128)S(1)}, f32[64]{0:T(128)}, u32[]{:S(2)}) copy-start(f32[64]{0:T(128)} %param.26) | copy-start | bytes 772
  59.7 46.7 %copy-start.17 = (f32[64]{0:T(128)S(1)}, f32[64]{0:T(128)}, u32[]{:S(2)}) copy-start(f32[64]{0:T(128)} %param.31) | copy-start | bytes 772
  59.7 49.3 %copy-start.19 = (f32[128]{0:T(128)S(1)}, f32[128]{0:T(128)}, u32[]{:S(2)}) copy-start(f32[128]{0:T(128)} %param.28) | copy-start | bytes 1540
  59.7 49.3 %copy-start.20 = (f32[128]{0:T(128)S(1)}, f32[128]{0:T(128)}, u32[]{:S(2)}) copy-start(f32[128]{0:T(128)} %param.29) | copy-start | bytes 1540
  60.4 91.5 %copy-start.12 = (f32[8,48,256]{2,1,0:T(8,128)S(1)}, f32[8,48,256]{2,1,0:T(8,128)}, u32[]{:S(2)}) copy-start(f32[8,48,256]{2,1,0:T(8,128)} %param.18) | copy-start | bytes 1179652
  148.7 8.9 %copy-start.18 = (f32[64]{0:T(128)}, f32[64]{0:T(128)S(1)}, u32[]{:S(2)}) copy-start(f32[64]{0:T(128)S(1)} %multiply_add_fusion.1) | copy-start | bytes 772
where the time goes:
time: 158 us
  blocking collectives  84.1 us (53%)
  other arithmetic  27.3 us (17%)
  waiting for transfers between devices  17.6 us (11%)
  starting transfers between devices  16.3 us (10%)
  local copies, waits for them, and re-layouts  9.91 us (6%)
    psum x1, blocking collectives, body(): panel_loads = lax.psum(partial_value, 'gx').astype(jnp.bfloat16)  42.6 us
    psum x1, blocking collectives, body(): lax.psum((jnp.dot(drift_shapes, displacement, precision=lax.Precision.HIG...  36.6 us
    ppermute x4, waiting for transfers between devices, padded_2(): after = lax.ppermute(first, axis, down)  12.9 us
    ppermute x4, starting transfers between devices, padded_2(): before = lax.ppermute(last, axis, up)  11.1 us
    concatenate x4, other arithmetic, padded_2(): value = jnp.concatenate([before, value, after], axis=dim)  8.12 us
    add x2, other arithmetic, advance(): centre_cells[:3]  6.93 us
    ppermute x4, starting transfers between devices, padded_2(): after = lax.ppermute(first, axis, down)  5.17 us
    ppermute x4, waiting for transfers between devices, padded_2(): before = lax.ppermute(last, axis, up)  4.68 us
  transfers between devices with their start and end apart: 8, of which 5 were waited for; matrix products, arithmetic and copies ran while one was open for 2% of the time, Pallas kernels for 0%

commit v1 on v0

v1 whole, which is shorter than its diff:
```python
import functools

import jax
import jax.numpy as jnp
from jax import lax
from jax.experimental import pallas as pl
from jax.experimental.pallas import tpu as pltpu
from jax.sharding import PartitionSpec as P

f32 = jnp.float32
bf16 = jnp.bfloat16
time_step = 0.1
modal_step = 0.5
shape_beta = 0.5
shape_gamma = 0.5
spring_rate = 0.5
LANES = 128
PAD = 8
VMEM_BYTES = 40 * 1024 * 1024


def shifts(size, step, cyclic):
    if cyclic:
        return [((i + step) % size, i) for i in range(size)]
    return [(i, i + step) for i in range(size) if 0 <= i + step < size]


def parts_of(row):
    high = row.astype(bf16).astype(f32)
    rest = row - high
    middle = rest.astype(bf16).astype(f32)
    return [high, middle, rest - middle]


def stacked(rows):
    filler = jnp.zeros((16 - len(rows), rows[0].shape[1]), f32)
    return jnp.concatenate(rows + [filler], axis=0).astype(bf16)


def flow_kernel(
    count_x,
    count_y,
    vel,
    pre,
    vis,
    wind,
    before,
    after,
    left,
    right,
    cell,
    area,
    partial,
    vel_out,
    pre_out,
    payload,
    old,
    mid,
    visc,
    sem,
):
    layers, rows, height = pre.shape
    last = PAD + rows
    ix = lax.axis_index("gx")
    iy = lax.axis_index("gy")
    inner = pl.ds(2, layers)
    own = [
        pltpu.make_async_copy(vel.at[i], old.at[i, inner, pl.ds(PAD, rows)], sem.at[i])
        for i in range(3)
    ]
    own.append(pltpu.make_async_copy(pre, old.at[3, inner, pl.ds(PAD, rows)], sem.at[3]))
    own.append(pltpu.make_async_copy(vis, visc.at[inner, pl.ds(PAD, rows)], sem.at[4]))
    side_left = pltpu.make_async_copy(
        left.at[pl.ds(0, 4)], old.at[:, inner, pl.ds(0, PAD)], sem.at[5]
    )
    side_left_visc = pltpu.make_async_copy(left.at[4], visc.at[inner, pl.ds(0, PAD)], sem.at[6])
    side_right = pltpu.make_async_copy(
        right.at[pl.ds(0, 4)], old.at[:, inner, pl.ds(last, PAD)], sem.at[7]
    )
    side_right_visc = pltpu.make_async_copy(
        right.at[4], visc.at[inner, pl.ds(last, PAD)], sem.at[8]
    )
    for copy in own:
        copy.start()
    has_left = iy > 0
    has_right = iy < count_y - 1
    has_before = ix > 0
    has_after = ix < count_x - 1

    @pl.when(has_left)
    def _():
        side_left.start()
        side_left_visc.start()

    @pl.when(has_right)
    def _():
        side_right.start()
        side_right_visc.start()

    blank = jnp.zeros((4, layers, PAD, height), f32)

    @pl.when(jnp.logical_not(has_left))
    def _():
        old[:, 2 : 2 + layers, 0:PAD, :] = blank
        mid[:, 2 : 2 + layers, 0:PAD, :] = blank

    @pl.when(jnp.logical_not(has_right))
    def _():
        old[:, 2 : 2 + layers, last : last + PAD, :] = blank
        mid[:, 2 : 2 + layers, last : last + PAD, :] = blank

    for message, first, near in ((before, 0, 1), (after, layers + 2, layers + 2)):
        for field in range(4):
            for depth in range(2):
                start = (field * 2 + depth) * rows
                old[field, first + depth, PAD:last, :] = message[start : start + rows, :].astype(f32)
        start = 8 * rows
        visc[near, PAD:last, :] = message[start : start + rows, :].astype(f32)
        corner = message[9 * rows : 9 * rows + 16, :].astype(f32)
        for field in range(4):
            old[field, near, PAD - 1 : PAD, :] = corner[field : field + 1]
            old[field, near, last : last + 1, :] = corner[4 + field : 5 + field]

    for copy in own:
        copy.wait()

    @pl.when(has_left)
    def _():
        side_left.wait()
        side_left_visc.wait()

    @pl.when(has_right)
    def _():
        side_right.wait()
        side_right_visc.wait()

    lane = lax.broadcasted_iota(jnp.int32, (8, height), 1)
    top = lane == height - 1
    bottom = lane == 0
    wind_part = jnp.broadcast_to(wind[...] * (0.5 * time_step), (8, height))
    half = 0.5 * time_step

    def step(source, layer, row, edge):
        here = pl.ds(row, 8)
        centre = [source[f, layer, here, :] for f in range(4)]
        ahead = [source[f, layer + 1, here, :] for f in range(4)]
        behind = [source[f, layer - 1, here, :] for f in range(4)]
        if edge < 0:
            lower = [pltpu.roll(c, 1, 0) for c in centre]
        else:
            lower = [source[f, layer, pl.ds(row - 1, 8), :] for f in range(4)]
        if edge > 0:
            upper = [pltpu.roll(c, 7, 0) for c in centre]
        else:
            upper = [source[f, layer, pl.ds(row + 1, 8), :] for f in range(4)]
        above = [jnp.where(top, 0.0, pltpu.roll(c, height - 1, 1)) for c in centre]
        below = [jnp.where(bottom, 0.0, pltpu.roll(c, 1, 1)) for c in centre]
        factor = visc[layer, here, :] * time_step
        slopes = (ahead[3] - behind[3], upper[3] - lower[3], above[3] - below[3])
        result = []
        for i in range(3):
            around = (ahead[i] + behind[i]) + (upper[i] + lower[i]) + (above[i] + below[i])
            result.append(
                centre[i]
                + factor * (around - 6.0 * centre[i])
                - wind_part * (ahead[i] - behind[i])
                - half * slopes[i]
            )
        result.append(
            centre[3]
            - half * ((ahead[0] - behind[0]) + (upper[1] - lower[1]) + (above[2] - below[2]))
        )
        return result

    def first_step(layer, row, edge=0):
        result = step(old, layer, row, edge)
        for f in range(4):
            mid[f, layer, pl.ds(row, 8), :] = result[f]

    @pl.loop(2, 2 + layers)
    def _(layer):
        for row in range(PAD, last, 8):
            first_step(layer, row)

    @pl.when(has_left)
    def _():
        @pl.loop(2, 2 + layers)
        def _(layer):
            first_step(layer, 0, -1)

    @pl.when(has_right)
    def _():
        @pl.loop(2, 2 + layers)
        def _(layer):
            first_step(layer, last, 1)

    for there, layer in ((has_before, 1), (has_after, layers + 2)):

        @pl.when(there)
        def _(layer=layer):
            for row in range(PAD, last, 8):
                first_step(layer, row)

        @pl.when(jnp.logical_not(there))
        def _(layer=layer):
            mid[:, layer, PAD:last, :] = jnp.zeros((4, rows, height), f32)

    @pl.loop(2, 2 + layers)
    def _(layer):
        for row in range(PAD, last, 8):
            result = step(mid, layer, row, 0)
            for i in range(3):
                vel_out[i, layer - 2, row - PAD : row - PAD + 8, :] = result[i]
            pre_out[layer - 2, row - PAD : row - PAD + 8, :] = result[3]

    slots = cell.shape[0]
    cells = layers * rows
    flat = pre_out[...].reshape(cells, height)
    place = cell[...]
    column = place // height
    level = place - column * height
    pick = (lax.broadcasted_iota(jnp.int32, (slots, cells), 1) == column).astype(f32).astype(bf16)
    found = jnp.zeros((slots, height), f32)
    for part in parts_of(flat):
        found = found + jnp.dot(pick, part.astype(bf16), preferred_element_type=f32)
    at_level = lax.broadcasted_iota(jnp.int32, (slots, height), 1) == level
    sampled = jnp.sum(jnp.where(at_level, found, 0.0), axis=1, keepdims=True)
    loads = (area[...] * sampled).astype(bf16).astype(f32)
    same = lax.broadcasted_iota(jnp.int32, (LANES, LANES), 0) == lax.broadcasted_iota(
        jnp.int32, (LANES, LANES), 1
    )
    lines = []
    for start in range(0, slots, LANES):
        chosen = jnp.where(same, loads[start : start + LANES], 0.0)
        lines.append(jnp.sum(chosen, axis=0, keepdims=True))
    message = jnp.concatenate(lines + [partial[...]], axis=0)
    payload[...] = jnp.broadcast_to(message[None], payload.shape)


def respond(stretch, rate, hysteresis, coefficients):
    hysteresis = hysteresis + modal_step * (
        rate
        - shape_beta * jnp.abs(rate) * hysteresis
        - shape_gamma * rate * jnp.abs(hysteresis)
    )
    force = -(
        coefficients[0:1] * rate + spring_rate * stretch + coefficients[1:2] * hysteresis
    )
    return hysteresis, force


def pulled(forces, shapes):
    sides = []
    for force in forces:
        three = jnp.concatenate(parts_of(force) + [jnp.zeros((13, force.shape[1]), f32)], axis=0)
        sides += [three, -three]
    left = jnp.concatenate(sides, axis=1).astype(bf16)
    right = shapes[...].reshape(-1, shapes.shape[-1])
    return jnp.sum(jnp.dot(left, right, preferred_element_type=f32), axis=0, keepdims=True)


def advance_modes(load, modes, displacement, velocity):
    frequency = modes[2:3]
    acceleration = (
        load
        - 2.0 * modes[3:4] * frequency * velocity
        - frequency * frequency * displacement
    )
    velocity = velocity + modal_step * acceleration
    return displacement + modal_step * velocity, velocity


def first_kernel(count_x, count_y, load_rows, *refs):
    received, panels, dampers, shapes, modes = refs[:5]
    tables = refs[5 : 5 + count_y]
    payload, state, hysteresis_out, held, sem = refs[5 + count_y :]
    iy = lax.axis_index("gy")
    copies = [
        pltpu.make_async_copy(tables[q], held.at[q], sem.at[q]) for q in range(count_y)
    ]
    for copy in copies:
        copy.start()
    panel_count = tables[0].shape[0]
    high_count = panel_count // LANES
    slot_count = panels.shape[-1]
    rank = lax.broadcasted_iota(jnp.int32, (high_count, LANES), 0)
    low_rank = lax.broadcasted_iota(jnp.int32, (LANES, slot_count), 0)
    sides = []
    forces = []
    for q in range(count_y):
        piece = lax.rem(iy + q, count_y)
        ids = panels[q]
        high = ids // LANES
        high = jnp.where(ids < 0, -1, high)
        low = ids - high * LANES
        chunks = []
        for i in range(count_x):
            for r in range(load_rows):
                start = (i * load_rows + r) * LANES
                line = received[i, piece, r : r + 1, :]
                chunks.append(
                    jnp.where(rank == high[:, start : start + LANES], line, 0.0).astype(bf16)
                )
        spread = (low_rank == low).astype(f32).astype(bf16)
        sorted_loads = lax.dot_general(
            jnp.concatenate(chunks, axis=1),
            spread,
            (((1,), (1,)), ((), ())),
            preferred_element_type=f32,
        )
        sides.append(
            jnp.concatenate(
                [jnp.where(rank == c, sorted_loads, 0.0).astype(bf16) for c in range(high_count)],
                axis=1,
            )
        )
        stretch = received[0, piece, load_rows : load_rows + 1, :]
        rate = received[0, piece, load_rows + 1 : load_rows + 2, :]
        for i in range(1, count_x):
            stretch = stretch + received[i, piece, load_rows : load_rows + 1, :]
            rate = rate + received[i, piece, load_rows + 1 : load_rows + 2, :]
        coefficients = dampers[q]
        hysteresis, force = respond(stretch, rate, coefficients[2:3], coefficients)
        hysteresis_out[q] = hysteresis
        forces.append(force)
    for copy in copies:
        copy.wait()
    rows = jnp.zeros((high_count, modes.shape[1]), f32)
    for q in range(count_y):
        rows = rows + jnp.dot(sides[q], held[q], preferred_element_type=f32)
    panel_modal = jnp.sum(rows, axis=0, keepdims=True)
    table = modes[...]
    load = panel_modal + pulled(forces, shapes)
    displacement, velocity = advance_modes(load, table, table[0:1], table[1:2])
    state[0:1, :] = displacement
    state[1:2, :] = velocity
    state[2:3, :] = panel_modal
    state[3:4, :] = panel_modal
    pair = lax.dot_general(
        stacked(parts_of(displacement) + parts_of(velocity)),
        shapes[0].reshape(-1, shapes.shape[-1]),
        (((1,), (1,)), ((), ())),
        preferred_element_type=f32,
    )
    width = pair.shape[1] // 2
    drift = pair[:, :width] - pair[:, width:]
    message = jnp.concatenate(
        [
            jnp.sum(drift[0:3], axis=0, keepdims=True),
            jnp.sum(drift[3:6], axis=0, keepdims=True),
        ],
        axis=0,
    )
    payload[...] = jnp.broadcast_to(message[None], payload.shape)


def second_kernel(count_x, count_y, received, dampers, shapes, modes, state, held, modal, damper):
    iy = lax.axis_index("gy")
    forces = []
    for q in range(count_y):
        piece = lax.rem(iy + q, count_y)
        stretch = received[0, piece, 0:1, :]
        rate = received[0, piece, 1:2, :]
        for i in range(1, count_x):
            stretch = stretch + received[i, piece, 0:1, :]
            rate = rate + received[i, piece, 1:2, :]
        hysteresis, force = respond(stretch, rate, held[q], dampers[q])
        if q == 0:
            damper[...] = hysteresis
        forces.append(force)
    load = state[2:3, :] + pulled(forces, shapes)
    displacement, velocity = advance_modes(load, modes[...], state[0:1, :], state[1:2, :])
    modal[0:1, :] = displacement
    modal[1:2, :] = velocity


def whole(space=pltpu.VMEM):
    return pl.BlockSpec(memory_space=space)


def body(
    velocity,
    pressure,
    viscosity,
    wind_profile,
    panel_area,
    slot_cell,
    slot_panel,
    panel_shapes,
    node_shapes,
    damper_node,
    damper_viscous,
    damper_hysteretic,
    frequency,
    damping_ratio,
    modal_state,
    damper_state,
):
    count_x = lax.axis_size("gx")
    count_y = lax.axis_size("gy")
    total = count_x * count_y
    both = ("gx", "gy")
    ix = lax.axis_index("gx")
    iy = lax.axis_index("gy")
    layers, rows, height = pressure.shape
    slots = slot_cell.shape[1]
    slots_padded = -(-slots // LANES) * LANES
    load_rows = slots_padded // LANES
    damper_count = damper_node.shape[0]
    damper_padded = -(-damper_count // LANES) * LANES
    mode_count = frequency.shape[0]

    def side(start):
        parts = [velocity, pressure[None], viscosity[None]]
        cut = [lax.dynamic_slice_in_dim(part, start, PAD, axis=2) for part in parts]
        return jnp.concatenate(cut, axis=0)

    if count_y == 2:
        facing = side(jnp.where(iy == 0, rows - PAD, 0))
        left = right = lax.ppermute(facing, "gy", [(0, 1), (1, 0)])
    else:
        left = lax.ppermute(side(rows - PAD), "gy", shifts(count_y, 1, False))
        right = lax.ppermute(side(0), "gy", shifts(count_y, -1, False))

    def message(first, near):
        fields = jnp.concatenate(
            [velocity[:, first : first + 2], pressure[None, first : first + 2]], axis=0
        )
        corner_left = jnp.where(iy > 0, left[:4, near, PAD - 1], 0.0)
        corner_right = jnp.where(iy < count_y - 1, right[:4, near, 0], 0.0)
        return jnp.concatenate(
            [
                fields.reshape(8 * rows, height).astype(bf16),
                viscosity[near].astype(bf16),
                corner_left.astype(bf16),
                corner_right.astype(bf16),
                jnp.zeros((8, height), bf16),
            ],
            axis=0,
        )

    before = lax.ppermute(message(layers - 2, layers - 1), "gx", shifts(count_x, 1, False))
    after = lax.ppermute(message(0, 0), "gx", shifts(count_x, -1, False))

    def around(value):
        return [value] + [
            lax.ppermute(value, "gy", shifts(count_y, q, True)) for q in range(1, count_y)
        ]

    tables = around(panel_shapes)
    small = jnp.concatenate(
        [
            damper_viscous,
            damper_hysteretic,
            damper_state,
            damper_node.astype(f32),
            slot_panel[0].astype(f32),
        ]
    )
    smalls = jnp.stack(around(small))
    cut = 4 * damper_count
    dampers = smalls[:, :cut].reshape(count_y, 4, damper_count)
    dampers = jnp.pad(dampers, ((0, 0), (0, 0), (0, damper_padded - damper_count)))
    nodes = smalls[:, cut - damper_count : cut].astype(jnp.int32)
    nodes = jnp.pad(
        nodes, ((0, 0), (0, damper_padded - damper_count)), constant_values=-2
    )
    panels = smalls[:, cut:].astype(jnp.int32).reshape(count_y, count_x, slots)
    panels = jnp.pad(panels, ((0, 0), (0, 0), (0, slots_padded - slots)), constant_values=-1)
    panels = panels.reshape(count_y, 1, count_x * slots_padded)

    node_numbers = jnp.arange(node_shapes.shape[0], dtype=jnp.int32)
    ends = jnp.stack([nodes + 1, nodes], axis=1)
    ends = jnp.where(ends < 0, -1, ends).reshape(-1, 1)
    chosen = (ends == node_numbers[None, :]).astype(bf16)
    shapes = jnp.dot(chosen, node_shapes, preferred_element_type=f32).astype(bf16)
    shapes = shapes.reshape(count_y, 2, damper_padded, mode_count)
    drift = shapes[0, 0].astype(f32) - shapes[0, 1].astype(f32)
    partial = lax.dot_general(
        modal_state, drift, (((1,), (1,)), ((), ())), precision=lax.Precision.HIGHEST
    )

    own_ids = lax.dynamic_slice_in_dim(slot_panel[0], ix * slots, slots)
    area = jnp.where(own_ids < 0, 0.0, panel_area[jnp.maximum(own_ids, 0)])
    area = jnp.pad(area, (0, slots_padded - slots))[:, None]
    cell = jnp.pad(slot_cell[0], (0, slots_padded - slots))[:, None]

    padded = (4, layers + 4, rows + 2 * PAD, height)
    message_rows = load_rows + 2
    velocity_next, pressure_next, payload = pl.pallas_call(
        functools.partial(flow_kernel, count_x, count_y),
        out_shape=(
            jax.ShapeDtypeStruct(velocity.shape, f32),
            jax.ShapeDtypeStruct(pressure.shape, f32),
            jax.ShapeDtypeStruct((total, message_rows, LANES), f32),
        ),
        in_specs=[whole(pl.ANY)] * 3
        + [whole()] * 3
        + [whole(pl.ANY)] * 2
        + [whole()] * 3,
        out_specs=(whole(), whole(), whole()),
        scratch_shapes=[
            pltpu.VMEM(padded, f32),
            pltpu.VMEM(padded, f32),
            pltpu.VMEM(padded[1:], f32),
            pltpu.SemaphoreType.DMA((9,)),
        ],
        compiler_params=pltpu.CompilerParams(vmem_limit_bytes=VMEM_BYTES),
        name="flow",
    )(
        velocity,
        pressure,
        viscosity,
        wind_profile[None, :],
        before,
        after,
        left,
        right,
        cell,
        area,
        partial,
    )
    received = lax.all_to_all(payload, both, 0, 0, tiled=True)
    received = received.reshape(count_x, count_y, message_rows, LANES)

    modes = jnp.concatenate([modal_state, frequency[None], damping_ratio[None]], axis=0)
    payload, state, hysteresis = pl.pallas_call(
        functools.partial(first_kernel, count_x, count_y, load_rows),
        out_shape=(
            jax.ShapeDtypeStruct((total, 2, damper_padded), f32),
            jax.ShapeDtypeStruct((4, mode_count), f32),
            jax.ShapeDtypeStruct((count_y, 1, damper_padded), f32),
        ),
        in_specs=[whole()] * 5 + [whole(pl.ANY)] * count_y,
        out_specs=(whole(), whole(), whole()),
        scratch_shapes=[
            pltpu.VMEM((count_y,) + panel_shapes.shape, bf16),
            pltpu.SemaphoreType.DMA((count_y,)),
        ],
        compiler_params=pltpu.CompilerParams(vmem_limit_bytes=VMEM_BYTES),
        name="first",
    )(received, panels, dampers, shapes, modes, *tables)
    received = lax.all_to_all(payload, both, 0, 0, tiled=True)
    received = received.reshape(count_x, count_y, 2, damper_padded)

    modal_next, damper_next = pl.pallas_call(
        functools.partial(second_kernel, count_x, count_y),
        out_shape=(
            jax.ShapeDtypeStruct((2, mode_count), f32),
            jax.ShapeDtypeStruct((1, damper_padded), f32),
        ),
        in_specs=[whole()] * 6,
        out_specs=(whole(), whole()),
        compiler_params=pltpu.CompilerParams(vmem_limit_bytes=VMEM_BYTES),
        name="second",
    )(received, dampers, shapes, modes, state, hysteresis)
    return (velocity_next, pressure_next, modal_next, damper_next[0, :damper_count])


def solution(mesh):
    placed = (
        P(None, "gx", "gy", None),
        P("gx", "gy", None),
        P("gx", "gy", None),
        P(),
        P("gy"),
        P("gy", "gx"),
        P("gy", None),
        P("gy", "gx"),
        P(None, "gx"),
        P("gy"),
        P("gy"),
        P("gy"),
        P("gx"),
        P("gx"),
        P(None, "gx"),
        P("gy"),
    )
    return jax.shard_map(
        body,
        mesh=mesh,
        in_specs=placed,
        out_specs=(P(None, "gx", "gy", None), P("gx", "gy", None), P(None, "gx"), P("gy")),
        check_vma=False,
    )
```

time: 158 us -> 64.5 us (0.41)
  blocking collectives: 84.1 us -> 8.95 us
  other arithmetic: 27.3 us -> 2.47 us
  Pallas kernels: 0 us -> 8.22 us
  local copies, waits for them, and re-layouts: 9.91 us -> 14.7 us
  waiting for transfers between devices: 17.6 us -> 13.7 us
  starting transfers between devices: 16.3 us -> 14 us
    psum x4 -> x0, blocking collectives: 84.1 us -> none  [the longest x1 42.6 us: body(): panel_loads = lax.psum(partial_value, 'gx').astype(jnp.bfloat16)]
    ppermute x8 -> x5, waiting for transfers between devices: 17.6 us -> 6.52 us  [the longest x1 5.44 us: body(): lax.ppermute(message(layers - 2, layers - 1), 'gx', shifts(count_x, 1, Fa...]
    ppermute x8 -> x5, starting transfers between devices: 16.3 us -> 7.27 us  [the longest x1 5.02 us: body(): lax.ppermute(message(layers - 2, layers - 1), 'gx', shifts(count_x, 1, Fa...]
    all_to_all x0 -> x1, blocking collectives: none -> 8.95 us  [body(): received = lax.all_to_all(payload, both, 0, 0, tiled=True)]
    concatenate x6 -> x3, other arithmetic: 9.32 us -> 0.8 us  [the longest x1 0.75 us: side(): return jnp.concatenate(cut, axis=0)]
    pallas_call x0 -> x3, Pallas kernels: none -> 8.22 us  [the longest x1 5.91 us: body(): pl.pallas_call(functools.partial(flow_kernel, count_x, count_y), out_shap...]
    mul x4 -> x0, other arithmetic: 7.2 us -> none  [the longest x2 4.21 us: advance(): slope_stream = 0.5 * (ahead_cells - behind_cells)]
    all_to_all x0 -> x1, waiting for transfers between devices: none -> 7.2 us  [body(): received = lax.all_to_all(payload, both, 0, 0, tiled=True)]
  transfers between devices with their start and end apart: 8 -> 6, of which waited for: 5 -> 3; matrix products, arithmetic and copies ran while one was open for 2% -> 20% of each run, Pallas kernels for 0% -> 9%
where the time goes in v1:
time: 64.5 us; the launch traced here: 63.9 us
  local copies, waits for them, and re-layouts  14.7 us (23%)
  starting transfers between devices  14 us (22%)
  waiting for transfers between devices  13.7 us (21%)
  blocking collectives  8.95 us (14%)
  Pallas kernels  8.22 us (13%)
  other arithmetic  2.47 us (4%)
  between operations  1.11 us (2%)
  matrix products  0.69 us (1%)
    all_to_all x1, blocking collectives, body(): received = lax.all_to_all(payload, both, 0, 0, tiled=True)  8.95 us
    all_to_all x1, waiting for transfers between devices, body(): received = lax.all_to_all(payload, both, 0, 0, tiled=True)  7.2 us
    all_to_all x1, starting transfers between devices, body(): received = lax.all_to_all(payload, both, 0, 0, tiled=True)  6.77 us
    pallas_call x1, Pallas kernels, body(): pl.pallas_call(functools.partial(flow_kernel, count_x, count_y), out_shap...  5.91 us
    ppermute x1, waiting for transfers between devices, body(): lax.ppermute(message(layers - 2, layers - 1), 'gx', shifts(count_x, 1, Fa...  5.44 us
    ppermute x1, starting transfers between devices, body(): lax.ppermute(message(layers - 2, layers - 1), 'gx', shifts(count_x, 1, Fa...  5.02 us
    concatenate x2, local copies, waits for them, and re-layouts, message(): jnp.concatenate([fields.reshape(8 * rows, height).astype(bf16), viscosity...  3.39 us
    unnamed x48, local copies, waits for them, and re-layouts  2.2 us
  transfers between devices with their start and end apart: 6, of which 3 were waited for; matrix products, arithmetic and copies ran while one was open for 20% of the time, Pallas kernels for 9%

profile of v1, /device:TPU:0, one launch (start us, length us, event | category | flops | bytes accessed | tf_op | source)
XLA Modules:
  0.0 63.9 jit_solution(6171189911813189582)
XLA Ops:
  0.6 0.0 copy-start
  0.7 1.0 %constant_dynamic-slice_fusion.1 = f32[3,8,8,256]{3,2,1,0:T(8,128)S(1)} fusion(f32[3,8,48,256]{3,2,1,0:T(8,128)} %vel.1, s32[]{:T(128)S(6)} %select_n.57), kind=kLoop, calls=%fused_computation.47 | loop fusion | bytes 393220 | tf_op jit(solution)/shard_map/dynamic_slice | solution.py:415
  1.8 0.9 %dynamic-slice_bitcast_fusion = (f32[1,8,8,256]{3,2,1,0:T(8,128)S(1)}, f32[1,8,8,256]{3,2,1,0:T(8,128)S(1)}) fusion(f32[8,48,256]{2,1,0:T(8,128)} %vis.1, s32[]{:T(128)S(6)} %select_n.57, f32[8,48,256]{2,1,0:T(8,128)} %pre.1), kind=kLoop, calls=%fused_computation.14 | loop fusion | bytes 262148 | tf_op jit(solution)/shard_map/dynamic_slice | solution.py:415
  2.7 0.0 copy-start.2
  2.7 0.8 %pad_maximum_fusion = f32[5,8,8,256]{3,2,1,0:T(8,128)} fusion(f32[1,8,8,256]{3,2,1,0:T(8,128)S(1)} %get-tuple-element.34, f32[1,8,8,256]{3,2,1,0:T(8,128)S(1)} %get-tuple-element.35, f32[3,8,8,256]{3,2,1,0:T(8,128)S(1)} %constant_dynamic-slice_fusion.1), kind=kLoop, calls=%fused_computation.6 | loop fusion | flops 163840 | bytes 655360 | tf_op jit(solution)/shard_map/concatenate | solution.py:416
  3.4 0.5 collective-permute-start
  3.9 0.7 %concatenate.28 = f32[4352]{0:T(1024)} concatenate(f32[64]{0:T(128)S(1)} %copy-done.16, f32[64]{0:T(128)S(1)} %copy-done.17, f32[64]{0:T(128)S(1)} %copy-done.18, f32[64]{0:T(128)S(1)} %convert_element_type.81, f32[4096]{0:T(1024)S(1)} %bitcast.60), dimensions={0} | concatenate | bytes 34816 | tf_op jit(solution)/shard_map/concatenate | solution.py:451
  4.6 0.1 collective-permute-start.3
  4.7 0.5 collective-permute-start.4
  5.1 0.1 convert.18
  5.2 0.0 copy-start.8
  5.2 0.7 %convert.19 = bf16[8,48,256]{2,1,0:T(8,128)(2,1)} convert(f32[8,48,256]{2,1,0:T(8,128)S(1)} %copy-done.2) | non-fusion elementwise | flops 98304 | bytes 589824 | tf_op jit(solution)/shard_map/convert.10
  5.9 0.7 %convert.20 = bf16[8,48,256]{2,1,0:T(8,128)(2,1)} convert(f32[8,48,256]{2,1,0:T(8,128)S(1)} %copy-done.3) | non-fusion elementwise | flops 98304 | bytes 589824 | tf_op jit(solution)/shard_map/convert.6
  6.7 0.8 %slice_bitcast_fusion = (bf16[1,2,48,256]{3,2,1,0:T(8,128)(2,1)S(1)}, bf16[1,2,48,256]{3,2,1,0:T(8,128)(2,1)S(1)}) fusion(bf16[8,48,256]{2,1,0:T(8,128)(2,1)} %convert.19), kind=kLoop, calls=%fused_computation.16 | loop fusion | bytes 196608 | tf_op jit(solution)/shard_map/broadcast_in_dim | solution.py:427
  7.5 1.4 %slice_bitcast_fusion.2 = (bf16[48,256]{1,0:T(8,128)(2,1)}, bf16[48,256]{1,0:T(8,128)(2,1)S(1)}) fusion(bf16[8,48,256]{2,1,0:T(8,128)(2,1)} %convert.20), kind=kLoop, calls=%fused_computation.24 | loop fusion | bytes 98304 | tf_op jit(solution)/shard_map/convert_element_type | solution.py:434
  8.9 0.0 copy-start.14
  8.9 1.7 %gather_fusion = f32[256]{0:T(256)S(1)} fusion(f32[2048]{0:T(1024)S(1)} %copy-done.8, s32[1024]{0:T(1024)S(1)} %pad_clamp_fusion), kind=kCustom, calls=%fused_computation | custom fusion | bytes 3072 | tf_op jit(solution)/shard_map/gather | solution.py:484
  10.6 0.1 copy.21
  10.8 0.2 copy.20
  11.1 0.7 %stack.20 = f32[1,4352]{1,0:T(1,128)S(1)} reshape(f32[4352]{0:T(1024)} %concatenate.28) | data formatting | bytes 34816 | tf_op jit(solution)/shard_map/stack | solution.py:460
  11.8 0.0 copy-start.9
  11.8 0.0 copy-start.7
  11.8 0.1 copy.23.cell
  12.0 0.0 collective-permute-done.3
  12.0 0.7 %stack.21 = f32[1,4352]{1,0:T(1,128)S(1)} reshape(f32[4352]{0:T(1024)} %collective-permute-done.3) | data formatting | bytes 34816 | tf_op jit(solution)/shard_map/stack | solution.py:460
  12.7 0.0 copy-start.11
  12.8 0.1 maximum_convert_fusion
  12.9 0.0 collective-permute-done.left.right
  12.9 0.5 copy-done.11
  13.4 0.9 %concatenate.27 = bf16[448,256]{1,0:T(8,128)(2,1)S(1)} concatenate(bf16[384,256]{1,0:T(8,128)(2,1)S(1)} %bitcast.59, bf16[48,256]{1,0:T(8,128)(2,1)} %get-tuple-element.26, bf16[4,256]{1,0:T(4,128)(2,1)S(1)} %bitcast.64, bf16[4,256]{1,0:T(4,128)(2,1)S(1)} %bitcast.62, bf16[8,256]{1,0:T(8,128)(2,1)S(1)} %broadcast.54), dimensions={0} | concatenate | bytes 458752 | tf_op jit(solution)/shard_map/concatenate | solution.py:431
  14.3 1.3 %collective-permute-start.2 = (bf16[448,256]{1,0:T(8,128)(2,1)S(1)}, bf16[448,256]{1,0:T(8,128)(2,1)S(1)}, u32[]{:S(2)}, u32[]{:S(2)}) collective-permute-start(bf16[448,256]{1,0:T(8,128)(2,1)S(1)} %concatenate.27), channel_id=1, source_target_pairs={{2,0},{4,2},{6,4},{8,6},{10,8},{12,10},{14,12},{16,14},{18,16},{20... | collective-permute-start | bytes 688136 | tf_op jit(solution)/shard_map/ppermute | solution.py:443
  15.6 2.5 %concatenate.25 = bf16[448,256]{1,0:T(8,128)(2,1)} concatenate(bf16[384,256]{1,0:T(8,128)(2,1)S(1)} %bitcast.58, bf16[48,256]{1,0:T(8,128)(2,1)S(1)} %get-tuple-element.27, bf16[4,256]{1,0:T(4,128)(2,1)S(1)} %bitcast.63, bf16[4,256]{1,0:T(4,128)(2,1)S(1)} %bitcast.61, bf16[8,256]{1,0:T(8,128)(2,1)S(1)} %broadcast.54), dimensions={0} | concatenate | bytes 458752 | tf_op jit(solution)/shard_map/concatenate | solution.py:431
  18.1 5.0 %collective-permute-start.1 = (bf16[448,256]{1,0:T(8,128)(2,1)}, bf16[448,256]{1,0:T(8,128)(2,1)S(1)}, u32[]{:S(2)}, u32[]{:S(2)}) collective-permute-start(bf16[448,256]{1,0:T(8,128)(2,1)} %concatenate.25), channel_id=1, source_target_pairs={{0,2},{2,4},{4,6},{6,8},{8,10},{10,12},{12,14},{14,16},{16,18},{18... | collective-permute-start | bytes 688136 | tf_op jit(solution)/shard_map/ppermute | solution.py:442
  23.1 0.5 fusion.1
  23.7 0.2 convolution_bitcast_fusion.partial
  23.8 1.1 %collective-permute-done.2.after = bf16[448,256]{1,0:T(8,128)(2,1)S(1)} collective-permute-done((bf16[448,256]{1,0:T(8,128)(2,1)S(1)}, bf16[448,256]{1,0:T(8,128)(2,1)S(1)}, u32[]{:S(2)}, u32[]{:S(2)}) %collective-permute-start.2) | collective-permute-done | bytes 229408 | tf_op jit(solution)/shard_map/ppermute | solution.py:443
  24.9 0.7 %copy-done.5 = bf16[448,256]{1,0:T(8,128)(2,1)} copy-done((bf16[448,256]{1,0:T(8,128)(2,1)}, bf16[448,256]{1,0:T(8,128)(2,1)S(1)}, u32[]{:S(2)}) %copy-start.5) | copy-done | bytes 229400
  25.6 5.4 %collective-permute-done.1.before = bf16[448,256]{1,0:T(8,128)(2,1)S(1)} collective-permute-done((bf16[448,256]{1,0:T(8,128)(2,1)}, bf16[448,256]{1,0:T(8,128)(2,1)S(1)}, u32[]{:S(2)}, u32[]{:S(2)}) %collective-permute-start.1) | collective-permute-done | bytes 229408 | tf_op jit(solution)/shard_map/ppermute | solution.py:442
  31.0 0.9 %copy-done.6 = bf16[448,256]{1,0:T(8,128)(2,1)S(1)} copy-done((bf16[448,256]{1,0:T(8,128)(2,1)S(1)}, bf16[448,256]{1,0:T(8,128)(2,1)}, u32[]{:S(2)}) %copy-start.6) | copy-done | bytes 229400
  32.0 5.9 %flow.1 = (f32[3,8,48,256]{3,2,1,0:T(8,128)}, f32[8,48,256]{2,1,0:T(8,128)}, f32[32,4,128]{2,1,0:T(4,128)}) custom-call(f32[3,8,48,256]{3,2,1,0:T(8,128)S(1)} %copy-done.1, f32[8,48,256]{2,1,0:T(8,128)S(1)} %copy-done.2, f32[8,48,256]{2,1,0:T(8,128)S(1)} %copy-done.3, f32[1,256]{1,0:T(1,128)S(1)} %bitcast.57, ...), custom_call_target="tpu_custom_call" | custom-call | tf_op jit(solution)/shard_map/flow/pallas_call | solution.py:490
  37.9 6.8 %all-to-all-start = ((f32[32,4,128]{2,1,0:T(4,128)}), f32[32,4,128]{2,1,0:T(4,128)S(1)}, u32[]{:S(2)}, u32[]{:S(2)}) async-start(f32[32,4,128]{2,1,0:T(4,128)} %get-tuple-element.14), calls=%async_computation | async-start | bytes 131072 | tf_op jit(solution)/shard_map/all_to_all | solution.py:523
  44.8 0.1 reshape.99
  44.9 0.0 collective-permute-done.4.refs_6_
  44.9 7.2 %all-to-all-done = f32[32,4,128]{2,1,0:T(4,128)S(1)} async-done(((f32[32,4,128]{2,1,0:T(4,128)}), f32[32,4,128]{2,1,0:T(4,128)S(1)}, u32[]{:S(2)}, u32[]{:S(2)}) %all-to-all-start) | async-done | bytes 65568 | tf_op jit(solution)/shard_map/all_to_all | solution.py:523
  52.1 1.6 %first.1 = (f32[32,2,128]{2,1,0:T(2,128)S(1)}, f32[4,128]{1,0:T(4,128)S(1)}, f32[2,1,128]{2,1,0:T(1,128)S(1)}) custom-call(f32[16,2,4,128]{3,2,1,0:T(4,128)S(1)} %bitcast.55, s32[2,1,4096]{2,1,0:T(1,128)S(1)} %reshape.98.refs_1_, f32[2,4,128]{2,1,0:T(4,128)S(1)} %pad.9.refs_2_.dampers, bf16[2,2,128,128]{3,2,1,0:T(8,128)(2,1)S(1)} %bitcast.53, ...), custom_call_target="tpu_custom_call" | custom-call | tf_op jit(solution)/shard_map/first/pallas_call | solution.py:527
  53.7 8.9 %all_to_all.10 = f32[32,2,128]{2,1,0:T(2,128)S(1)} all-to-all(f32[32,2,128]{2,1,0:T(2,128)S(1)} %get-tuple-element.15), channel_id=1, replica_groups=mesh['gx'=16,'gy'=2] {'gx','gy'}, dimensions={0} | all-to-all | bytes 65536 | tf_op jit(solution)/shard_map/all_to_all | solution.py:543
  62.6 0.8 %second.1 = (f32[2,128]{1,0:T(2,128)}, f32[1,128]{1,0:T(1,128)S(1)}) custom-call(f32[16,2,2,128]{3,2,1,0:T(2,128)S(1)} %bitcast.56, f32[2,4,128]{2,1,0:T(4,128)S(1)} %pad.9.refs_2_.dampers, bf16[2,2,128,128]{3,2,1,0:T(8,128)(2,1)S(1)} %bitcast.54, f32[4,128]{1,0:T(4,128)S(1)} %pad_maximum_fusion.4.refs_4_.modes, f32[4,128]{1,0:T(4,128)S(1)} %get-tuple-element.16.state, ...), custom_call_target="tpu_custom_call" | custom-call | tf_op jit(solution)/shard_map/second/pallas_call | solution.py:546
  63.4 0.5 slice_bitcast_fusion.4
  (57 shorter events, 0.3 us)
Async XLA Ops:
  0.6 22.5 %copy-start = (bf16[1024,128]{1,0:T(8,128)(2,1)S(1)}, bf16[1024,128]{1,0:T(8,128)(2,1)}, u32[]{:S(2)}) copy-start(bf16[1024,128]{1,0:T(8,128)(2,1)} %param.24) | copy-start | bytes 786436
  0.6 4.5 %copy-start.1 = (f32[3,8,48,256]{3,2,1,0:T(8,128)S(1)}, f32[3,8,48,256]{3,2,1,0:T(8,128)}, u32[]{:S(2)}) copy-start(f32[3,8,48,256]{3,2,1,0:T(8,128)} %vel.1) | copy-start | bytes 3538948
  0.7 3.2 %copy-start.13 = (s32[1,4096]{1,0:T(1,128)S(1)}, s32[1,4096]{1,0:T(1,128)}, u32[]{:S(2)}) copy-start(s32[1,4096]{1,0:T(1,128)} %param.22) | copy-start | bytes 49156
  0.7 3.2 %copy-start.21 = (s32[64]{0:T(128)S(1)}, s32[64]{0:T(128)}, u32[]{:S(2)}) copy-start(s32[64]{0:T(128)} %param.25) | copy-start | bytes 772
  0.7 3.2 %copy-start.16 = (f32[64]{0:T(128)S(1)}, f32[64]{0:T(128)}, u32[]{:S(2)}) copy-start(f32[64]{0:T(128)} %param.26) | copy-start | bytes 772
  0.7 3.2 %copy-start.17 = (f32[64]{0:T(128)S(1)}, f32[64]{0:T(128)}, u32[]{:S(2)}) copy-start(f32[64]{0:T(128)} %param.27) | copy-start | bytes 772
  0.7 3.2 %copy-start.18 = (f32[64]{0:T(128)S(1)}, f32[64]{0:T(128)}, u32[]{:S(2)}) copy-start(f32[64]{0:T(128)} %param.31) | copy-start | bytes 772
  2.7 2.5 %copy-start.2 = (f32[8,48,256]{2,1,0:T(8,128)S(1)}, f32[8,48,256]{2,1,0:T(8,128)}, u32[]{:S(2)}) copy-start(f32[8,48,256]{2,1,0:T(8,128)} %pre.1) | copy-start | bytes 1179652
  3.4 9.4 %collective-permute-start = (f32[5,8,8,256]{3,2,1,0:T(8,128)}, f32[5,8,8,256]{3,2,1,0:T(8,128)S(1)}, u32[]{:S(2)}, u32[]{:S(2)}) collective-permute-start(f32[5,8,8,256]{3,2,1,0:T(8,128)} %pad_maximum_fusion), channel_id=1, source_target_pairs={{0,1},{1,0},{2,3},{3,2},{4,5},{5,4},{6,7},{7,6},{8,9},{9,8},{10,11... | collective-permute-start | bytes 983048 | tf_op jit(solution)/shard_map/ppermute | solution.py:420
  4.6 1.3 %copy-start.3 = (f32[8,48,256]{2,1,0:T(8,128)S(1)}, f32[8,48,256]{2,1,0:T(8,128)}, u32[]{:S(2)}) copy-start(f32[8,48,256]{2,1,0:T(8,128)} %vis.1) | copy-start | bytes 1179652
  4.6 7.4 %collective-permute-start.3 = (f32[4352]{0:T(1024)}, f32[4352]{0:T(1024)}, u32[]{:S(2)}, u32[]{:S(2)}) collective-permute-start(f32[4352]{0:T(1024)} %concatenate.28), channel_id=1, source_target_pairs={{1,0},{0,1},{3,2},{2,3},{5,4},{4,5},{7,6},{6,7},{9,8},{8,9},{11,10... | collective-permute-start | bytes 52232 | tf_op jit(solution)/shard_map/ppermute | solution.py:447
  4.7 40.2 %collective-permute-start.4 = (bf16[2048,128]{1,0:T(8,128)(2,1)}, bf16[2048,128]{1,0:T(8,128)(2,1)}, u32[]{:S(2)}, u32[]{:S(2)}) collective-permute-start(bf16[2048,128]{1,0:T(8,128)(2,1)} %refs_5_.1), channel_id=1, source_target_pairs={{1,0},{0,1},{3,2},{2,3},{5,4},{4,5},{7,6},{6,7},{9,8},{8,9},{11,10... | collective-permute-start | bytes 1572872 | tf_op jit(solution)/shard_map/ppermute | solution.py:447
  5.2 3.7 %copy-start.8 = (f32[2048]{0:T(1024)S(1)}, f32[2048]{0:T(1024)}, u32[]{:S(2)}) copy-start(f32[2048]{0:T(1024)} %param.20) | copy-start | bytes 24580
  8.9 2.2 %copy-start.15 = (f32[2,128]{1,0:T(2,128)S(1)}, f32[2,128]{1,0:T(2,128)}, u32[]{:S(2)}) copy-start(f32[2,128]{1,0:T(2,128)} %param.30) | copy-start | bytes 3076
  8.9 2.2 %copy-start.19 = (f32[128]{0:T(128)S(1)}, f32[128]{0:T(128)}, u32[]{:S(2)}) copy-start(f32[128]{0:T(128)} %param.29) | copy-start | bytes 1540
  8.9 2.2 %copy-start.20 = (f32[128]{0:T(128)S(1)}, f32[128]{0:T(128)}, u32[]{:S(2)}) copy-start(f32[128]{0:T(128)} %param.28) | copy-start | bytes 1540
  8.9 3.0 %copy-start.14 = (s32[1,256]{1,0:T(1,128)S(1)}, s32[1,256]{1,0:T(1,128)}, u32[]{:S(2)}) copy-start(s32[1,256]{1,0:T(1,128)} %param.21) | copy-start | bytes 3076
  11.8 1.6 %copy-start.9 = (f32[1,4352]{1,0:T(1,128)}, f32[1,4352]{1,0:T(1,128)S(1)}, u32[]{:S(2)}) copy-start(f32[1,4352]{1,0:T(1,128)S(1)} %stack.20) | copy-start | bytes 52228
  11.8 19.2 %copy-start.7 = (f32[256]{0:T(256)S(1)}, f32[256]{0:T(256)}, u32[]{:S(2)}) copy-start(f32[256]{0:T(256)} %param.19) | copy-start | bytes 3076
  12.7 0.6 copy-start.11
  14.3 10.7 %collective-permute-start.2 = (bf16[448,256]{1,0:T(8,128)(2,1)S(1)}, bf16[448,256]{1,0:T(8,128)(2,1)S(1)}, u32[]{:S(2)}, u32[]{:S(2)}) collective-permute-start(bf16[448,256]{1,0:T(8,128)(2,1)S(1)} %concatenate.27), channel_id=1, source_target_pairs={{2,0},{4,2},{6,4},{8,6},{10,8},{12,10},{14,12},{16,14},{18,16},{20... | collective-permute-start | bytes 688136 | tf_op jit(solution)/shard_map/ppermute | solution.py:443
  18.1 12.9 %collective-permute-start.1 = (bf16[448,256]{1,0:T(8,128)(2,1)}, bf16[448,256]{1,0:T(8,128)(2,1)S(1)}, u32[]{:S(2)}, u32[]{:S(2)}) collective-permute-start(bf16[448,256]{1,0:T(8,128)(2,1)} %concatenate.25), channel_id=1, source_target_pairs={{0,2},{2,4},{4,6},{6,8},{8,10},{10,12},{12,14},{14,16},{16,18},{18... | collective-permute-start | bytes 688136 | tf_op jit(solution)/shard_map/ppermute | solution.py:442
  24.9 0.7 %copy-start.5 = (bf16[448,256]{1,0:T(8,128)(2,1)}, bf16[448,256]{1,0:T(8,128)(2,1)S(1)}, u32[]{:S(2)}) copy-start(bf16[448,256]{1,0:T(8,128)(2,1)S(1)} %collective-permute-done.2.after) | copy-start | bytes 688132
  31.0 0.9 %copy-start.6 = (bf16[448,256]{1,0:T(8,128)(2,1)S(1)}, bf16[448,256]{1,0:T(8,128)(2,1)}, u32[]{:S(2)}) copy-start(bf16[448,256]{1,0:T(8,128)(2,1)} %copy-done.5) | copy-start | bytes 688132
  32.0 12.7 %copy-start.10 = (f32[1,4352]{1,0:T(1,128)S(1)}, f32[1,4352]{1,0:T(1,128)}, u32[]{:S(2)}) copy-start(f32[1,4352]{1,0:T(1,128)} %copy-done.9) | copy-start | bytes 52228
  32.0 12.7 %copy-start.12 = (f32[1,4352]{1,0:T(1,128)S(1)}, f32[1,4352]{1,0:T(1,128)}, u32[]{:S(2)}) copy-start(f32[1,4352]{1,0:T(1,128)} %copy-done.11) | copy-start | bytes 52228
  32.0 20.1 %copy-start.4 = (bf16[2048,128]{1,0:T(8,128)(2,1)S(1)}, bf16[2048,128]{1,0:T(8,128)(2,1)}, u32[]{:S(2)}) copy-start(bf16[2048,128]{1,0:T(8,128)(2,1)} %refs_5_.1) | copy-start | bytes 1572868
  37.9 14.2 %all-to-all-start = ((f32[32,4,128]{2,1,0:T(4,128)}), f32[32,4,128]{2,1,0:T(4,128)S(1)}, u32[]{:S(2)}, u32[]{:S(2)}) async-start(f32[32,4,128]{2,1,0:T(4,128)} %get-tuple-element.14), calls=%async_computation | async-start | bytes 131072 | tf_op jit(solution)/shard_map/all_to_all | solution.py:523

commit v2 on v1

v2 whole, which is shorter than its diff:
```python
import functools

import jax
import jax.numpy as jnp
from jax import lax
from jax.experimental import pallas as pl
from jax.experimental.pallas import tpu as pltpu
from jax.sharding import PartitionSpec as P

f32 = jnp.float32
bf16 = jnp.bfloat16
time_step = 0.1
modal_step = 0.5
shape_beta = 0.5
shape_gamma = 0.5
spring_rate = 0.5
LANES = 128
PAD = 8
VMEM_BYTES = 40 * 1024 * 1024


def shifts(size, step, cyclic):
    if cyclic:
        return [((i + step) % size, i) for i in range(size)]
    return [(i, i + step) for i in range(size) if 0 <= i + step < size]


def parts_of(row):
    high = row.astype(bf16).astype(f32)
    rest = row - high
    middle = rest.astype(bf16).astype(f32)
    return [high, middle, rest - middle]


def stacked(rows):
    filler = jnp.zeros((16 - len(rows), rows[0].shape[1]), f32)
    return jnp.concatenate(rows + [filler], axis=0).astype(bf16)


def side_kernel(starts, vel, pre, vis, *refs):
    outs, sem = refs[:-1], refs[-1]
    copies = []
    for place, (start, out) in enumerate(zip(starts, outs)):
        if start is None:
            start = jnp.where(lax.axis_index("gy") == 0, pre.shape[1] - PAD, 0)
        here = pl.ds(pl.multiple_of(start, PAD), PAD)
        copies += [
            pltpu.make_async_copy(vel.at[:, :, here], out.at[pl.ds(0, 3)], sem.at[place, 0]),
            pltpu.make_async_copy(pre.at[:, here], out.at[3], sem.at[place, 1]),
            pltpu.make_async_copy(vis.at[:, here], out.at[4], sem.at[place, 2]),
        ]
    for copy in copies:
        copy.start()
    for copy in copies:
        copy.wait()


def pack_kernel(count_y, vel, pre, vis, left, right, up, down, stage, corner, sem):
    layers, rows, height = pre.shape
    iy = lax.axis_index("gy")
    has = (iy > 0, iy < count_y - 1)
    messages = ((up, layers - 2, layers - 1), (down, 0, 0))
    copies = []
    for side, (out, first, near) in enumerate(messages):
        copies += [
            pltpu.make_async_copy(
                vel.at[:, pl.ds(first, 2)], stage.at[side, pl.ds(0, 3)], sem.at[side, 0]
            ),
            pltpu.make_async_copy(pre.at[pl.ds(first, 2)], stage.at[side, 3], sem.at[side, 1]),
            pltpu.make_async_copy(vis.at[near], stage.at[side, 4, 0], sem.at[side, 2]),
            pltpu.make_async_copy(
                left.at[pl.ds(0, 4), near], corner.at[side, 0], sem.at[side, 3]
            ),
            pltpu.make_async_copy(
                right.at[pl.ds(0, 4), near], corner.at[side, 1], sem.at[side, 4]
            ),
        ]
    for copy in copies:
        copy.start()
    for copy in copies:
        copy.wait()
    for side, (out, first, near) in enumerate(messages):
        for field in range(4):
            for depth in range(2):
                start = (field * 2 + depth) * rows
                out[start : start + rows, :] = stage[side, field, depth].astype(bf16)
        out[8 * rows : 9 * rows, :] = stage[side, 4, 0].astype(bf16)
        lines = [corner[side, 0, f, PAD - 1 : PAD, :] for f in range(4)]
        lines = [jnp.where(has[0], line, 0.0) for line in lines]
        others = [corner[side, 1, f, 0:1, :] for f in range(4)]
        lines += [jnp.where(has[1], line, 0.0) for line in others]
        lines.append(jnp.zeros((8, height), f32))
        out[9 * rows : 9 * rows + 16, :] = jnp.concatenate(lines, axis=0).astype(bf16)


def stepper(wind, height):
    lane = lax.broadcasted_iota(jnp.int32, (8, height), 1)
    top = lane == height - 1
    bottom = lane == 0
    half = 0.5 * time_step
    wind_part = jnp.broadcast_to(wind[...] * half, (8, height))

    def step(get, factor, row, edge):
        def at(offset, low):
            return [get(f, offset, low) for f in range(4)]

        centre, ahead, behind = at(0, row), at(1, row), at(-1, row)
        lower = [pltpu.roll(c, 1, 0) for c in centre] if edge < 0 else at(0, row - 1)
        upper = [pltpu.roll(c, 7, 0) for c in centre] if edge > 0 else at(0, row + 1)
        above = [jnp.where(top, 0.0, pltpu.roll(c, height - 1, 1)) for c in centre]
        below = [jnp.where(bottom, 0.0, pltpu.roll(c, 1, 1)) for c in centre]
        factor = factor * time_step
        slopes = (ahead[3] - behind[3], upper[3] - lower[3], above[3] - below[3])
        result = []
        for i in range(3):
            around = (ahead[i] + behind[i]) + (upper[i] + lower[i]) + (above[i] + below[i])
            result.append(
                centre[i]
                + factor * (around - 6.0 * centre[i])
                - wind_part * (ahead[i] - behind[i])
                - half * slopes[i]
            )
        result.append(
            centre[3]
            - half * ((ahead[0] - behind[0]) + (upper[1] - lower[1]) + (above[2] - below[2]))
        )
        return result

    return step


def inner_kernel(
    count_y, vel, pre, vis, wind, left, right,
    vel_out, old_edge, mid_edge, visc_edge, pre_core,
    old, mid, visc, vel_core, sem, out_sem,
):
    layers, rows, height = pre.shape
    last = PAD + rows
    iy = lax.axis_index("gy")
    has_left = iy > 0
    has_right = iy < count_y - 1
    core = pl.ds(PAD, rows)
    copies = [
        pltpu.make_async_copy(vel.at[i], old.at[i, :, core], sem.at[i]) for i in range(3)
    ]
    copies.append(pltpu.make_async_copy(pre, old.at[3, :, core], sem.at[3]))
    copies.append(pltpu.make_async_copy(vis, visc.at[:, core], sem.at[4]))
    for place, (source, row) in enumerate(((left, 0), (right, last))):
        copies.append(
            pltpu.make_async_copy(
                source.at[pl.ds(0, 4)], old.at[:, :, pl.ds(row, PAD)], sem.at[5 + 2 * place]
            )
        )
        copies.append(
            pltpu.make_async_copy(
                source.at[4], visc.at[:, pl.ds(row, PAD)], sem.at[6 + 2 * place]
            )
        )
    for copy in copies:
        copy.start()
    for copy in copies:
        copy.wait()
    blank = jnp.zeros((4, layers, PAD, height), f32)

    @pl.when(jnp.logical_not(has_left))
    def _():
        old[:, :, 0:PAD, :] = blank
        mid[:, :, 0:PAD, :] = blank

    @pl.when(jnp.logical_not(has_right))
    def _():
        old[:, :, last : last + PAD, :] = blank
        mid[:, :, last : last + PAD, :] = blank

    step = stepper(wind, height)

    def advance(source, layer, row, edge=0):
        def get(f, offset, low):
            return source[f, layer + offset, pl.ds(low, 8), :]

        return step(get, visc[layer, pl.ds(row, 8), :], row, edge)

    def first(layer, row, edge=0):
        result = advance(old, layer, row, edge)
        for f in range(4):
            mid[f, layer, pl.ds(row, 8), :] = result[f]

    @pl.loop(1, layers - 1)
    def _(layer):
        for row in range(PAD, last, 8):
            first(layer, row)

    @pl.when(has_left)
    def _():
        @pl.loop(1, layers - 1)
        def _(layer):
            first(layer, 0, -1)

    @pl.when(has_right)
    def _():
        @pl.loop(1, layers - 1)
        def _(layer):
            first(layer, last, 1)

    @pl.loop(2, layers - 2)
    def _(layer):
        for row in range(PAD, last, 8):
            result = advance(mid, layer, row)
            for i in range(3):
                vel_core[i, layer - 2, row - PAD : row - PAD + 8, :] = result[i]
            pre_core[layer - 2, row - PAD : row - PAD + 8, :] = result[3]

    result = pltpu.make_async_copy(
        vel_core, vel_out.at[:, pl.ds(2, layers - 4)], out_sem
    )
    result.start()
    for side, first_old, place_old, first_mid, place_mid in (
        (0, 0, 2, 1, 3),
        (1, layers - 2, 1, layers - 3, 0),
    ):
        for depth in range(2):
            visc_edge[side, place_old + depth] = visc[first_old + depth]
            for f in range(4):
                old_edge[side, f, place_old + depth] = old[f, first_old + depth]
                mid_edge[side, f, place_mid + depth] = mid[f, first_mid + depth]
    result.wait()


def edge_kernel(
    count_x, count_y, before, after, wind, cell, area, partial, pre_core,
    vel_in, old_in, mid_in, visc_in,
    vel_out, pre_out, payload, old, mid, visc,
    stage, pre_full, vel_edge, sem, out_sem,
):
    layers, rows, height = pre_full.shape
    last = PAD + rows
    ix = lax.axis_index("gx")
    iy = lax.axis_index("gy")
    has_left = iy > 0
    has_right = iy < count_y - 1
    has_before = ix > 0
    has_after = ix < count_x - 1
    copies = [
        pltpu.make_async_copy(message, stage.at[side], sem.at[side])
        for side, message in enumerate((before, after))
    ]
    for copy in copies:
        copy.start()
    pre_full[2 : layers - 2] = pre_core[...]
    slots = cell.shape[1]
    cells = layers * rows
    same = lax.broadcasted_iota(jnp.int32, (LANES, LANES), 0) == lax.broadcasted_iota(
        jnp.int32, (LANES, LANES), 1
    )
    place = cell[...]
    line = place // height
    level = place - line * height

    def stand(row):
        lines = [
            jnp.sum(jnp.where(same, row[:, k : k + LANES], 0.0), axis=1, keepdims=True)
            for k in range(0, slots, LANES)
        ]
        return jnp.concatenate(lines, axis=0)

    line, level = stand(line.astype(f32)), stand(level.astype(f32))
    own_area = stand(area[...])
    pick = lax.broadcasted_iota(jnp.int32, (slots, cells), 1).astype(f32) == line
    pick = pick.astype(f32).astype(bf16)
    at_level = lax.broadcasted_iota(jnp.int32, (slots, height), 1).astype(f32) == level
    for copy in copies:
        copy.wait()
    for side in range(2):
        near = 1 + 2 * side
        for field in range(4):
            for depth in range(2):
                start = (field * 2 + depth) * rows
                old[side, field, 3 * side + depth, PAD:last, :] = stage[
                    side, start : start + rows, :
                ].astype(f32)
        visc[side, near, PAD:last, :] = stage[side, 8 * rows : 9 * rows, :].astype(f32)
        corner = stage[side, 9 * rows : 9 * rows + 16, :].astype(f32)
        for field in range(4):
            old[side, field, near, PAD - 1 : PAD, :] = corner[field : field + 1]
            old[side, field, near, last : last + 1, :] = corner[4 + field : 5 + field]

    step = stepper(wind, height)

    def advance(source, side, layer, row, edge=0):
        def get(f, offset, low):
            return source[side, f, layer + offset, pl.ds(low, 8), :]

        return step(get, visc[side, layer, pl.ds(row, 8), :], row, edge)

    def first(side, layer, row, edge=0):
        result = advance(old, side, layer, row, edge)
        for f in range(4):
            mid[side, f, layer, pl.ds(row, 8), :] = result[f]

    blank = jnp.zeros((4, PAD, height), f32)

    @pl.loop(0, 2)
    def _(side):
        there = jnp.where(side == 0, has_before, has_after)
        outside = 1 + 2 * side
        for row in range(PAD, last, 8):
            first(side, 2, row)

        @pl.when(has_left)
        def _():
            first(side, 2, 0, -1)

        @pl.when(jnp.logical_not(has_left))
        def _():
            mid[side, :, 2, 0:PAD, :] = blank

        @pl.when(has_right)
        def _():
            first(side, 2, last, 1)

        @pl.when(jnp.logical_not(has_right))
        def _():
            mid[side, :, 2, last : last + PAD, :] = blank

        @pl.when(there)
        def _():
            for row in range(PAD, last, 8):
                first(side, outside, row)

        @pl.when(jnp.logical_not(there))
        def _():
            mid[side, :, outside, PAD:last, :] = jnp.zeros((4, rows, height), f32)

        for row in range(PAD, last, 8):
            for layer, place in ((2, side), (3 - 2 * side, 1 - side)):
                result = advance(mid, side, layer, row)
                here = pl.ds(row - PAD, 8)
                for i in range(3):
                    vel_edge[side, i, place, here, :] = result[i]
                pre_full[side * (layers - 2) + place, here, :] = result[3]

    results = [
        pltpu.make_async_copy(
            vel_edge.at[side], vel_out.at[:, pl.ds(side * (layers - 2), 2)], out_sem.at[side]
        )
        for side in range(2)
    ]
    results.append(pltpu.make_async_copy(pre_full, pre_out, out_sem.at[2]))
    for result in results:
        result.start()
    flat = pre_full[...].reshape(cells, height)
    found = jnp.zeros((slots, height), f32)
    for part in parts_of(flat):
        found = found + jnp.dot(pick, part.astype(bf16), preferred_element_type=f32)
    sampled = jnp.sum(jnp.where(at_level, found, 0.0), axis=1, keepdims=True)
    loads = (own_area * sampled).astype(bf16).astype(f32)
    lines = []
    for start in range(0, slots, LANES):
        chosen = jnp.where(same, loads[start : start + LANES], 0.0)
        lines.append(jnp.sum(chosen, axis=0, keepdims=True))
    message = jnp.concatenate(lines + [partial[...]], axis=0)
    payload[...] = jnp.broadcast_to(message[None], payload.shape)
    for result in results:
        result.wait()


def prepare_kernel(slot_count, damper_width, own_ids, areas, nodes, modal, *refs):
    smalls = refs[:-3]
    shapes, partial, area = refs[-3:]
    high_count = areas.shape[0]
    slots = own_ids.shape[1]
    ids = own_ids[...]
    high = jnp.where(ids < 0, -1, ids // LANES)
    low = ids - high * LANES
    high_pick = lax.broadcasted_iota(jnp.int32, (high_count, slots), 0) == high
    low_pick = lax.broadcasted_iota(jnp.int32, (LANES, slots), 0) == low
    high_pick = high_pick.astype(f32).astype(bf16)
    spread = jnp.zeros((LANES, slots), f32)
    for part in parts_of(areas[...]):
        spread = spread + lax.dot_general(
            part.astype(bf16),
            high_pick,
            (((0,), (0,)), ((), ())),
            preferred_element_type=f32,
        )
    area[...] = jnp.sum(jnp.where(low_pick, spread, 0.0), axis=0, keepdims=True)
    node_rank = lax.broadcasted_iota(jnp.int32, (nodes.shape[0], damper_width), 0).astype(f32)
    table = nodes[...]
    for q, small in enumerate(smalls):
        lower = small[:, slot_count + 3 * damper_width : slot_count + 4 * damper_width]
        for end in range(2):
            pick = (node_rank == lower + (1.0 - end)).astype(f32).astype(bf16)
            rows = lax.dot_general(
                pick, table, (((0,), (0,)), ((), ())), preferred_element_type=f32
            )
            shapes[q, end] = rows.astype(bf16)
    state = modal[...]
    partial[...] = drift_times(state[0:1], state[1:2], shapes)


def respond(stretch, rate, hysteresis, viscous, hysteretic):
    hysteresis = hysteresis + modal_step * (
        rate
        - shape_beta * jnp.abs(rate) * hysteresis
        - shape_gamma * rate * jnp.abs(hysteresis)
    )
    force = -(viscous * rate + spring_rate * stretch + hysteretic * hysteresis)
    return hysteresis, force


def pulled(forces, shapes):
    sides = []
    for force in forces:
        three = jnp.concatenate(parts_of(force) + [jnp.zeros((13, force.shape[1]), f32)], axis=0)
        sides += [three, -three]
    left = jnp.concatenate(sides, axis=1).astype(bf16)
    right = shapes[...].reshape(-1, shapes.shape[-1])
    return jnp.sum(jnp.dot(left, right, preferred_element_type=f32), axis=0, keepdims=True)


def drift_times(displacement, velocity, shapes):
    pair = lax.dot_general(
        stacked(parts_of(displacement) + parts_of(velocity)),
        shapes[0].reshape(-1, shapes.shape[-1]),
        (((1,), (1,)), ((), ())),
        preferred_element_type=f32,
    )
    width = pair.shape[1] // 2
    drift = pair[:, :width] - pair[:, width:]
    return jnp.concatenate(
        [
            jnp.sum(drift[0:3], axis=0, keepdims=True),
            jnp.sum(drift[3:6], axis=0, keepdims=True),
        ],
        axis=0,
    )


def advance_modes(load, frequency, ratio, displacement, velocity):
    acceleration = (
        load
        - 2.0 * ratio * frequency * velocity
        - frequency * frequency * displacement
    )
    velocity = velocity + modal_step * acceleration
    return displacement + modal_step * velocity, velocity


def damper_rows(small, slot_count, width):
    return [small[:, slot_count + k * width : slot_count + (k + 1) * width] for k in range(3)]


def first_kernel(count_x, count_y, load_rows, *refs):
    received, shapes, modal, frequency, ratio = refs[:5]
    smalls = refs[5 : 5 + count_y]
    tables = refs[5 + count_y : 5 + 2 * count_y]
    payload, state, hysteresis_out, held, sem = refs[5 + 2 * count_y :]
    iy = lax.axis_index("gy")
    copies = [
        pltpu.make_async_copy(tables[q], held.at[q], sem.at[q]) for q in range(count_y)
    ]
    for copy in copies:
        copy.start()
    panel_count = tables[0].shape[0]
    high_count = panel_count // LANES
    slot_count = count_x * load_rows * LANES
    width = payload.shape[-1]
    rank = lax.broadcasted_iota(jnp.int32, (high_count, LANES), 0).astype(f32)
    low_rank = lax.broadcasted_iota(jnp.int32, (LANES, slot_count), 0).astype(f32)
    sides = []
    forces = []
    for q in range(count_y):
        piece = lax.rem(iy + q, count_y)
        ids = smalls[q][:, :slot_count]
        high = jnp.floor(ids * (1.0 / LANES))
        low = ids - high * LANES
        chunks = []
        for i in range(count_x):
            for r in range(load_rows):
                start = (i * load_rows + r) * LANES
                line = received[i, piece, r : r + 1, :]
                chunks.append(
                    jnp.where(rank == high[:, start : start + LANES], line, 0.0).astype(bf16)
                )
        spread = (low_rank == low).astype(f32).astype(bf16)
        sorted_loads = lax.dot_general(
            jnp.concatenate(chunks, axis=1),
            spread,
            (((1,), (1,)), ((), ())),
            preferred_element_type=f32,
        )
        sides.append(
            jnp.concatenate(
                [jnp.where(rank == c, sorted_loads, 0.0).astype(bf16) for c in range(high_count)],
                axis=1,
            )
        )
        stretch = received[0, piece, load_rows : load_rows + 1, :]
        rate = received[0, piece, load_rows + 1 : load_rows + 2, :]
        for i in range(1, count_x):
            stretch = stretch + received[i, piece, load_rows : load_rows + 1, :]
            rate = rate + received[i, piece, load_rows + 1 : load_rows + 2, :]
        viscous, hysteretic, held_state = damper_rows(smalls[q], slot_count, width)
        hysteresis, force = respond(stretch, rate, held_state, viscous, hysteretic)
        hysteresis_out[q] = hysteresis
        forces.append(force)
    load = pulled(forces, shapes)
    for copy in copies:
        copy.wait()
    rows = jnp.zeros((high_count, modal.shape[1]), f32)
    for q in range(count_y):
        rows = rows + jnp.dot(sides[q], held[q], preferred_element_type=f32)
    panel_modal = jnp.sum(rows, axis=0, keepdims=True)
    displacement, velocity = advance_modes(
        panel_modal + load, frequency[...], ratio[...], modal[0:1, :], modal[1:2, :]
    )
    state[0:1, :] = displacement
    state[1:2, :] = velocity
    state[2:3, :] = panel_modal
    state[3:4, :] = panel_modal
    message = drift_times(displacement, velocity, shapes)
    payload[...] = jnp.broadcast_to(message[None], payload.shape)


def second_kernel(count_x, count_y, slot_count, *refs):
    received, shapes, frequency, ratio, state, held = refs[:6]
    smalls = refs[6 : 6 + count_y]
    modal, damper = refs[6 + count_y :]
    iy = lax.axis_index("gy")
    forces = []
    for q in range(count_y):
        piece = lax.rem(iy + q, count_y)
        stretch = received[0, piece, 0:1, :]
        rate = received[0, piece, 1:2, :]
        for i in range(1, count_x):
            stretch = stretch + received[i, piece, 0:1, :]
            rate = rate + received[i, piece, 1:2, :]
        viscous, hysteretic, _ = damper_rows(smalls[q], slot_count, stretch.shape[1])
        hysteresis, force = respond(stretch, rate, held[q], viscous, hysteretic)
        if q == 0:
            damper[...] = hysteresis[:, : damper.shape[1]]
        forces.append(force)
    load = state[2:3, :] + pulled(forces, shapes)
    displacement, velocity = advance_modes(
        load, frequency[...], ratio[...], state[0:1, :], state[1:2, :]
    )
    modal[0:1, :] = displacement
    modal[1:2, :] = velocity


def whole(space=pltpu.VMEM):
    return pl.BlockSpec(memory_space=space)


def body(
    velocity,
    pressure,
    viscosity,
    wind_profile,
    panel_area,
    slot_cell,
    slot_panel,
    panel_shapes,
    node_shapes,
    damper_node,
    damper_viscous,
    damper_hysteretic,
    frequency,
    damping_ratio,
    modal_state,
    damper_state,
):
    count_x = lax.axis_size("gx")
    count_y = lax.axis_size("gy")
    total = count_x * count_y
    both = ("gx", "gy")
    ix = lax.axis_index("gx")
    layers, rows, height = pressure.shape
    slots = slot_cell.shape[1]
    slots_padded = -(-slots // LANES) * LANES
    load_rows = slots_padded // LANES
    slot_count = count_x * slots_padded
    damper_count = damper_node.shape[0]
    damper_padded = -(-damper_count // LANES) * LANES
    mode_count = frequency.shape[0]
    params = pltpu.CompilerParams(vmem_limit_bytes=VMEM_BYTES)
    shape = jax.ShapeDtypeStruct

    starts = (None,) if count_y == 2 else (rows - PAD, 0)
    sides = pl.pallas_call(
        functools.partial(side_kernel, starts),
        out_shape=tuple(shape((5, layers, PAD, height), f32) for _ in starts),
        in_specs=[whole(pl.ANY)] * 3,
        out_specs=tuple(whole(pl.ANY) for _ in starts),
        scratch_shapes=[pltpu.SemaphoreType.DMA((len(starts), 3))],
        compiler_params=params,
        name="side",
    )(velocity, pressure, viscosity)
    if count_y == 2:
        left = right = lax.ppermute(sides[0], "gy", [(0, 1), (1, 0)])
    else:
        left = lax.ppermute(sides[0], "gy", shifts(count_y, 1, False))
        right = lax.ppermute(sides[1], "gy", shifts(count_y, -1, False))

    message_shape = (9 * rows + 16, height)
    up, down = pl.pallas_call(
        functools.partial(pack_kernel, count_y),
        out_shape=(shape(message_shape, bf16), shape(message_shape, bf16)),
        in_specs=[whole(pl.ANY)] * 5,
        out_specs=(whole(), whole()),
        scratch_shapes=[
            pltpu.VMEM((2, 5, 2, rows, height), f32),
            pltpu.VMEM((2, 2, 4, PAD, height), f32),
            pltpu.SemaphoreType.DMA((2, 5)),
        ],
        compiler_params=params,
        name="pack",
    )(velocity, pressure, viscosity, left, right)
    tied = lax.optimization_barrier(
        (
            up, down, left, right, panel_shapes, node_shapes, panel_area, slot_panel,
            damper_node, damper_viscous, damper_hysteretic, damper_state, modal_state,
        )
    )
    (
        up, down, left, right, panel_shapes, node_shapes, panel_area, slot_panel,
        damper_node, damper_viscous, damper_hysteretic, damper_state, modal_state,
    ) = tied
    before = lax.ppermute(up, "gx", shifts(count_x, 1, False))
    after = lax.ppermute(down, "gx", shifts(count_x, -1, False))

    def around(value):
        return [value] + [
            lax.ppermute(value, "gy", shifts(count_y, q, True)) for q in range(1, count_y)
        ]

    def damper_row(value, filler=0.0):
        extra = damper_padded - damper_count
        return jnp.pad(value, (0, extra), constant_values=filler)[None]

    tables = around(panel_shapes)
    ids = slot_panel
    if slots != slots_padded:
        ids = jnp.pad(
            ids.reshape(count_x, slots),
            ((0, 0), (0, slots_padded - slots)),
            constant_values=-1,
        ).reshape(1, slot_count)
    own_ids = lax.dynamic_slice_in_dim(ids, ix * slots_padded, slots_padded, axis=1)
    small = jnp.concatenate(
        [
            ids.astype(f32),
            damper_row(damper_viscous),
            damper_row(damper_hysteretic),
            damper_row(damper_state),
            damper_row(damper_node.astype(f32), -4.0),
        ],
        axis=1,
    )
    smalls = around(small)
    cell = jnp.pad(slot_cell, ((0, 0), (0, slots_padded - slots)))

    shapes, partial, area = pl.pallas_call(
        functools.partial(prepare_kernel, slot_count, damper_padded),
        out_shape=(
            shape((count_y, 2, damper_padded, mode_count), bf16),
            shape((2, damper_padded), f32),
            shape((1, slots_padded), f32),
        ),
        in_specs=[whole()] * (4 + count_y),
        out_specs=(whole(), whole(), whole()),
        compiler_params=params,
        name="prepare",
    )(own_ids, panel_area.reshape(-1, LANES), node_shapes, modal_state, *smalls)

    tall = rows + 2 * PAD
    wind = wind_profile[None, :]
    velocity_next, old, mid, visc, pre_core = pl.pallas_call(
        functools.partial(inner_kernel, count_y),
        out_shape=(
            shape(velocity.shape, f32),
            shape((2, 4, 5, tall, height), f32),
            shape((2, 4, 5, tall, height), f32),
            shape((2, 5, tall, height), f32),
            shape((layers - 4, rows, height), f32),
        ),
        in_specs=[whole(pl.ANY)] * 3 + [whole()] + [whole(pl.ANY)] * 2,
        out_specs=(whole(pl.ANY), whole(), whole(), whole(), whole()),
        scratch_shapes=[
            pltpu.VMEM((4, layers, tall, height), f32),
            pltpu.VMEM((4, layers, tall, height), f32),
            pltpu.VMEM((layers, tall, height), f32),
            pltpu.VMEM((3, layers - 4, rows, height), f32),
            pltpu.SemaphoreType.DMA((9,)),
            pltpu.SemaphoreType.DMA,
        ],
        compiler_params=params,
        name="inner",
    )(velocity, pressure, viscosity, wind, left, right)

    velocity_next, pressure_next, payload, *_ = pl.pallas_call(
        functools.partial(edge_kernel, count_x, count_y),
        out_shape=(
            shape(velocity.shape, f32),
            shape(pressure.shape, f32),
            shape((total, load_rows + 2, LANES), f32),
            shape(old.shape, f32),
            shape(mid.shape, f32),
            shape(visc.shape, f32),
        ),
        in_specs=[whole(pl.ANY)] * 2
        + [whole()] * 5
        + [whole(pl.ANY)]
        + [whole()] * 3,
        out_specs=(whole(pl.ANY), whole(pl.ANY), whole(), whole(), whole(), whole()),
        input_output_aliases={7: 0, 8: 3, 9: 4, 10: 5},
        scratch_shapes=[
            pltpu.VMEM((2,) + message_shape, bf16),
            pltpu.VMEM((layers, rows, height), f32),
            pltpu.VMEM((2, 3, 2, rows, height), f32),
            pltpu.SemaphoreType.DMA((2,)),
            pltpu.SemaphoreType.DMA((3,)),
        ],
        compiler_params=params,
        name="edge",
    )(before, after, wind, cell, area, partial, pre_core, velocity_next, old, mid, visc)
    received = lax.all_to_all(payload, both, 0, 0, tiled=True)
    received = received.reshape(count_x, count_y, load_rows + 2, LANES)

    frequency = frequency[None]
    damping_ratio = damping_ratio[None]
    payload, state, hysteresis = pl.pallas_call(
        functools.partial(first_kernel, count_x, count_y, load_rows),
        out_shape=(
            shape((total, 2, damper_padded), f32),
            shape((4, mode_count), f32),
            shape((count_y, 1, damper_padded), f32),
        ),
        in_specs=[whole()] * (5 + count_y) + [whole(pl.ANY)] * count_y,
        out_specs=(whole(), whole(), whole()),
        scratch_shapes=[
            pltpu.VMEM((count_y,) + panel_shapes.shape, bf16),
            pltpu.SemaphoreType.DMA((count_y,)),
        ],
        compiler_params=params,
        name="first",
    )(received, shapes, modal_state, frequency, damping_ratio, *smalls, *tables)
    received = lax.all_to_all(payload, both, 0, 0, tiled=True)
    received = received.reshape(count_x, count_y, 2, damper_padded)

    modal_next, damper_next = pl.pallas_call(
        functools.partial(second_kernel, count_x, count_y, slot_count),
        out_shape=(
            shape((2, mode_count), f32),
            shape((1, damper_count), f32),
        ),
        in_specs=[whole()] * (6 + count_y),
        out_specs=(whole(), whole()),
        compiler_params=params,
        name="second",
    )(received, shapes, frequency, damping_ratio, state, hysteresis, *smalls)
    return (velocity_next, pressure_next, modal_next, damper_next.reshape(damper_count))


def solution(mesh):
    placed = (
        P(None, "gx", "gy", None),
        P("gx", "gy", None),
        P("gx", "gy", None),
        P(),
        P("gy"),
        P("gy", "gx"),
        P("gy", None),
        P("gy", "gx"),
        P(None, "gx"),
        P("gy"),
        P("gy"),
        P("gy"),
        P("gx"),
        P("gx"),
        P(None, "gx"),
        P("gy"),
    )
    return jax.shard_map(
        body,
        mesh=mesh,
        in_specs=placed,
        out_specs=(P(None, "gx", "gy", None), P("gx", "gy", None), P(None, "gx"), P("gy")),
        check_vma=False,
    )
```

time: 64.5 us -> 52.4 us (0.81)
  blocking collectives: 8.95 us -> 21.2 us
  local copies, waits for them, and re-layouts: 14.7 us -> 5.34 us
  starting transfers between devices: 14 us -> 7.2 us
  waiting for transfers between devices: 13.7 us -> 7.03 us
  other arithmetic: 2.47 us -> 0.02 us
  Pallas kernels: 8.22 us -> 10.3 us
  matrix products: 0.69 us -> 0 us
    all_to_all x1 -> x2, blocking collectives: 8.95 us -> 21.2 us  [body(): received = lax.all_to_all(payload, both, 0, 0, tiled=True)]
    all_to_all x1 -> x0, waiting for transfers between devices: 7.2 us -> none  [body(): received = lax.all_to_all(payload, both, 0, 0, tiled=True)]
    all_to_all x1 -> x0, starting transfers between devices: 6.77 us -> none  [body(): received = lax.all_to_all(payload, both, 0, 0, tiled=True)]
    concatenate x3 -> x1, local copies, waits for them, and re-layouts: 4.06 us -> 0.01 us  [body(): jnp.concatenate([ids.astype(f32), damper_row(damper_viscous), damper_row(...]
    unnamed x48 -> x41, local copies, waits for them, and re-layouts: 2.2 us -> 5.33 us
    pallas_call x2 -> x6, Pallas kernels: 6.67 us -> 9.1 us  [the longest x1 3.53 us: body(): pl.pallas_call(functools.partial(inner_kernel, count_y), out_shape=(shape...]
    dynamic_slice x2 -> x1, local copies, waits for them, and re-layouts: 1.93 us -> 0.01 us  [body(): lax.dynamic_slice_in_dim(ids, ix * slots_padded, slots_padded, axis=1)]
    gather x2 -> x0, local copies, waits for them, and re-layouts: 1.86 us -> none  [body(): area = jnp.where(own_ids < 0, 0.0, panel_area[jnp.maximum(own_ids, 0)])]
  transfers between devices with their start and end apart: 6 -> 5, of which waited for: 3 -> 2; matrix products, arithmetic and copies ran while one was open for 20% -> 0% of each run, Pallas kernels for 9% -> 15%
where the time goes in v2:
time: 52.4 us; the launch traced here: 52 us
  blocking collectives  21.2 us (40%)
  Pallas kernels  10.3 us (20%)
  starting transfers between devices  7.2 us (14%)
  waiting for transfers between devices  7.03 us (13%)
  local copies, waits for them, and re-layouts  5.34 us (10%)
  between operations  0.88 us (2%)
    all_to_all x2, blocking collectives, body(): received = lax.all_to_all(payload, both, 0, 0, tiled=True)  21.2 us
    ppermute x1, waiting for transfers between devices, body(): after = lax.ppermute(down, 'gx', shifts(count_x, -1, False))  5.77 us
    unnamed x41, local copies, waits for them, and re-layouts  5.33 us
    ppermute x1, starting transfers between devices, body(): before = lax.ppermute(up, 'gx', shifts(count_x, 1, False))  4.78 us
    pallas_call x1, Pallas kernels, body(): pl.pallas_call(functools.partial(inner_kernel, count_y), out_shape=(shape...  3.53 us
    pallas_call x1, Pallas kernels, body(): pl.pallas_call(functools.partial(edge_kernel, count_x, count_y), out_shap...  3.49 us
    ppermute x1, starting transfers between devices, body(): after = lax.ppermute(down, 'gx', shifts(count_x, -1, False))  1.29 us
    ppermute x1, waiting for transfers between devices, body(): left = right = lax.ppermute(sides[0], 'gy', [(0, 1), (1, 0)])  1.26 us
  transfers between devices with their start and end apart: 5, of which 2 were waited for; matrix products, arithmetic and copies ran while one was open for 0% of the time, Pallas kernels for 15%

profile of v2, /device:TPU:0, one launch (start us, length us, event | category | flops | bytes accessed | tf_op | source)
XLA Modules:
  0.0 52.0 jit_solution(3569344784512579450)
XLA Ops:
  0.6 0.0 copy-start
  0.6 1.3 %copy-done = f32[3,8,48,256]{3,2,1,0:T(8,128)S(1)} copy-done((f32[3,8,48,256]{3,2,1,0:T(8,128)S(1)}, f32[3,8,48,256]{3,2,1,0:T(8,128)}, u32[]{:S(2)}) %copy-start) | copy-done | bytes 1179672
  1.9 0.0 copy-start.2
  1.9 1.0 %copy-done.2 = f32[8,48,256]{2,1,0:T(8,128)S(1)} copy-done((f32[8,48,256]{2,1,0:T(8,128)S(1)}, f32[8,48,256]{2,1,0:T(8,128)}, u32[]{:S(2)}) %copy-start.2) | copy-done | bytes 393240
  2.9 0.0 copy-start.4
  2.9 1.0 %copy-done.4 = f32[8,48,256]{2,1,0:T(8,128)S(1)} copy-done((f32[8,48,256]{2,1,0:T(8,128)S(1)}, f32[8,48,256]{2,1,0:T(8,128)}, u32[]{:S(2)}) %copy-start.4) | copy-done | bytes 393240
  3.9 0.0 copy-start.1
  3.9 0.0 copy-start.6
  3.9 0.0 copy-start.15
  3.9 0.0 copy-start.16
  3.9 0.0 copy-start.17
  3.9 0.0 copy-start.18
  3.9 0.0 copy-start.9
  3.9 0.1 side.1
  4.1 0.5 collective-permute-start
  4.6 1.3 %collective-permute-done.left.right = f32[5,8,8,256]{3,2,1,0:T(8,128)S(1)} collective-permute-done((f32[5,8,8,256]{3,2,1,0:T(8,128)S(1)}, f32[5,8,8,256]{3,2,1,0:T(8,128)S(1)}, u32[]{:S(2)}, u32[]{:S(2)}) %collective-permute-start) | collective-permute-done | bytes 327712 | tf_op jit(solution)/shard_map/ppermute | solution.py:600
  5.8 0.0 copy-done.1
  5.8 1.0 %copy-done.3 = f32[8,48,256]{2,1,0:T(8,128)S(1)} copy-done((f32[8,48,256]{2,1,0:T(8,128)S(1)}, f32[8,48,256]{2,1,0:T(8,128)}, u32[]{:S(2)}) %copy-start.3) | copy-done | bytes 393240
  6.8 1.0 %copy-done.5 = f32[8,48,256]{2,1,0:T(8,128)S(1)} copy-done((f32[8,48,256]{2,1,0:T(8,128)S(1)}, f32[8,48,256]{2,1,0:T(8,128)}, u32[]{:S(2)}) %copy-start.5) | copy-done | bytes 393240
  7.8 0.6 %pack.1 = (bf16[448,256]{1,0:T(8,128)(2,1)S(1)}, bf16[448,256]{1,0:T(8,128)(2,1)S(1)}) custom-call(f32[3,8,48,256]{3,2,1,0:T(8,128)S(1)} %copy-done.1, f32[8,48,256]{2,1,0:T(8,128)S(1)} %copy-done.3, f32[8,48,256]{2,1,0:T(8,128)S(1)} %copy-done.5, f32[5,8,8,256]{3,2,1,0:T(8,128)S(1)} %collective-permute-done.left.right, ...), custom_call_target="tpu_custom_call" | custom-call | tf_op jit(solution)/shard_map/pack/pallas_call | solution.py:606
  8.5 0.0 copy-done.14
  8.5 4.8 %collective-permute-start.1 = (bf16[448,256]{1,0:T(8,128)(2,1)S(1)}, bf16[448,256]{1,0:T(8,128)(2,1)S(1)}, u32[]{:S(2)}, u32[]{:S(2)}) collective-permute-start(bf16[448,256]{1,0:T(8,128)(2,1)S(1)} %get-tuple-element.37), channel_id=1, source_target_pairs={{0,2},{2,4},{4,6},{6,8},{8,10},{10,12},{12,14},{14,16},{16,18},{18... | collective-permute-start | bytes 688136 | tf_op jit(solution)/shard_map/ppermute | solution.py:629
  13.3 1.3 %collective-permute-start.2 = (bf16[448,256]{1,0:T(8,128)(2,1)S(1)}, bf16[448,256]{1,0:T(8,128)(2,1)S(1)}, u32[]{:S(2)}, u32[]{:S(2)}) collective-permute-start(bf16[448,256]{1,0:T(8,128)(2,1)S(1)} %get-tuple-element.38), channel_id=1, source_target_pairs={{2,0},{4,2},{6,4},{8,6},{10,8},{12,10},{14,12},{16,14},{18,16},{20... | collective-permute-start | bytes 688136 | tf_op jit(solution)/shard_map/ppermute | solution.py:630
  14.6 0.0 copy-done.6
  14.6 0.1 collective-permute-start.4
  14.7 0.0 copy-done.15
  14.7 0.0 copy-done.16
  14.7 0.0 copy-done.17
  14.8 0.0 copy-done.18
  14.8 0.5 %collective-permute-start.3 = (f32[1,4608]{1,0:T(1,128)S(1)}, f32[1,4608]{1,0:T(1,128)S(1)}, u32[]{:S(2)}, u32[]{:S(2)}) collective-permute-start(f32[1,4608]{1,0:T(1,128)S(1)} %constant_dynamic-update-slice_fusion.refs_0_.refs_5_.refs_6_), channel_id=1, source_target_pairs={{1,0},{0,1},{3,2},{2,3},{5,4},{4,5},{7,6},{6,7},{9,8},{8,9},{11,10... | collective-permute-start | bytes 55304 | tf_op jit(solution)/shard_map/ppermute | solution.py:634
  15.3 0.0 copy-done.9
  15.3 3.5 %inner.1 = (f32[3,8,48,256]{3,2,1,0:T(8,128)}, f32[2,4,5,64,256]{4,3,2,1,0:T(8,128)S(1)}, f32[2,4,5,64,256]{4,3,2,1,0:T(8,128)S(1)}, f32[2,5,64,256]{3,2,1,0:T(8,128)S(1)}, f32[4,48,256]{2,1,0:T(8,128)S(1)}) custom-call(f32[3,8,48,256]{3,2,1,0:T(8,128)S(1)} %copy-done.1, f32[8,48,256]{2,1,0:T(8,128)S(1)} %copy-done.3, f32[8,48,256]{2,1,0:T(8,128)S(1)} %copy-done.5, ...), custom_call_target="tpu_custom_call" | custom-call | tf_op jit(solution)/shard_map/inner/pallas_call | solution.py:678
  18.9 0.0 collective-permute-done.3.refs_1_.refs_6_.refs_7_
  18.9 0.0 copy-done.7
  18.9 0.0 copy-done.8
  18.9 0.0 copy-done.10
  18.9 0.6 %prepare.1 = (bf16[2,2,128,128]{3,2,1,0:T(8,128)(2,1)S(1)}, f32[2,128]{1,0:T(2,128)S(1)}, f32[1,256]{1,0:T(1,128)S(1)}) custom-call(s32[1,256]{1,0:T(1,128)S(1)} %constant_dynamic-slice_fusion.own_ids, f32[16,128]{1,0:T(8,128)S(1)} %bitcast.17, bf16[1024,128]{1,0:T(8,128)(2,1)S(1)} %copy-done.7, f32[2,128]{1,0:T(2,128)S(1)} %copy-done.10, ...), custom_call_target="tpu_custom_call" | custom-call | tf_op jit(solution)/shard_map/prepare/pallas_call | solution.py:663
  19.5 0.0 collective-permute-done.1.before
  19.5 5.8 %collective-permute-done.2.after = bf16[448,256]{1,0:T(8,128)(2,1)S(1)} collective-permute-done((bf16[448,256]{1,0:T(8,128)(2,1)S(1)}, bf16[448,256]{1,0:T(8,128)(2,1)S(1)}, u32[]{:S(2)}, u32[]{:S(2)}) %collective-permute-start.2) | collective-permute-done | bytes 229408 | tf_op jit(solution)/shard_map/ppermute | solution.py:630
  25.3 0.0 copy-done.13
  25.3 3.5 %edge.1 = (f32[3,8,48,256]{3,2,1,0:T(8,128)}, f32[8,48,256]{2,1,0:T(8,128)}, f32[32,4,128]{2,1,0:T(4,128)S(1)}, f32[2,4,5,64,256]{4,3,2,1,0:T(8,128)S(1)}, f32[2...) custom-call(bf16[448,256]{1,0:T(8,128)(2,1)S(1)} %collective-permute, ...), custom_call_target="tpu_custom_call", output_to_operand_aliasing={{0}: (7, {}), {3}: (8, {}), {4}: (9, {}), {5}: (10, {})} | custom-call | tf_op jit(solution)/shard_map/edge/pallas_call | solution.py:701
  28.8 12.3 %all_to_all.10 = f32[32,4,128]{2,1,0:T(4,128)S(1)} all-to-all(f32[32,4,128]{2,1,0:T(4,128)S(1)} %get-tuple-element.58), channel_id=1, replica_groups=mesh['gx'=16,'gy'=2] {'gx','gy'}, dimensions={0} | all-to-all | bytes 131072 | tf_op jit(solution)/shard_map/all_to_all | solution.py:727
  41.1 0.0 collective-permute-done.4.refs_8_
  41.1 0.0 copy-done.11
  41.1 0.0 copy-done.12
  41.1 1.2 %first.1 = (f32[32,2,128]{2,1,0:T(2,128)S(1)}, f32[4,128]{1,0:T(4,128)S(1)}, f32[2,1,128]{2,1,0:T(1,128)S(1)}) custom-call(f32[16,2,4,128]{3,2,1,0:T(4,128)S(1)} %bitcast.15, bf16[2,2,128,128]{3,2,1,0:T(8,128)(2,1)S(1)} %get-tuple-element.59.refs_1_, f32[2,128]{1,0:T(2,128)S(1)} %copy-done.10, f32[1,128]{1,0:T(1,128)S(1)} %bitcast.20, ...), custom_call_target="tpu_custom_call" | custom-call | tf_op jit(solution)/shard_map/first/pallas_call | solution.py:732
  42.3 8.9 %all_to_all.11 = f32[32,2,128]{2,1,0:T(2,128)S(1)} all-to-all(f32[32,2,128]{2,1,0:T(2,128)S(1)} %get-tuple-element.61), channel_id=1, replica_groups=mesh['gx'=16,'gy'=2] {'gx','gy'}, dimensions={0} | all-to-all | bytes 65536 | tf_op jit(solution)/shard_map/all_to_all | solution.py:748
  51.3 0.8 %second.1 = (f32[2,128]{1,0:T(2,128)}, f32[1,64]{1,0:T(1,128)}) custom-call(f32[16,2,2,128]{3,2,1,0:T(2,128)S(1)} %bitcast.16, bf16[2,2,128,128]{3,2,1,0:T(8,128)(2,1)S(1)} %get-tuple-element.59.refs_1_, f32[1,128]{1,0:T(1,128)S(1)} %bitcast.21, f32[1,128]{1,0:T(1,128)S(1)} %bitcast.23, f32[4,128]{1,0:T(4,128)S(1)} %get-tuple-element.62.refs_4_, ...), custom_call_target="tpu_custom_call" | custom-call | tf_op jit(solution)/shard_map/second/pallas_call | solution.py:751
  (16 shorter events, 0.1 us)
Async XLA Ops:
  0.6 1.3 %copy-start = (f32[3,8,48,256]{3,2,1,0:T(8,128)S(1)}, f32[3,8,48,256]{3,2,1,0:T(8,128)}, u32[]{:S(2)}) copy-start(f32[3,8,48,256]{3,2,1,0:T(8,128)} %vel.5) | copy-start | bytes 3538948
  1.9 1.0 %copy-start.2 = (f32[8,48,256]{2,1,0:T(8,128)S(1)}, f32[8,48,256]{2,1,0:T(8,128)}, u32[]{:S(2)}) copy-start(f32[8,48,256]{2,1,0:T(8,128)} %pre.5) | copy-start | bytes 1179652
  2.9 1.0 %copy-start.4 = (f32[8,48,256]{2,1,0:T(8,128)S(1)}, f32[8,48,256]{2,1,0:T(8,128)}, u32[]{:S(2)}) copy-start(f32[8,48,256]{2,1,0:T(8,128)} %vis.5) | copy-start | bytes 1179652
  3.9 1.9 %copy-start.1 = (f32[3,8,48,256]{3,2,1,0:T(8,128)S(1)}, f32[3,8,48,256]{3,2,1,0:T(8,128)}, u32[]{:S(2)}) copy-start(f32[3,8,48,256]{3,2,1,0:T(8,128)} %vel.5) | copy-start | bytes 3538948
  3.9 4.6 %copy-start.14 = (s32[1,4096]{1,0:T(1,128)S(1)}, s32[1,4096]{1,0:T(1,128)}, u32[]{:S(2)}) copy-start(s32[1,4096]{1,0:T(1,128)} %param.22) | copy-start | bytes 49156
  3.9 10.7 %copy-start.6 = (bf16[2048,128]{1,0:T(8,128)(2,1)S(1)}, bf16[2048,128]{1,0:T(8,128)(2,1)}, u32[]{:S(2)}) copy-start(bf16[2048,128]{1,0:T(8,128)(2,1)} %refs_7_) | copy-start | bytes 1572868
  3.9 10.8 %copy-start.15 = (f32[64]{0:T(128)S(1)}, f32[64]{0:T(128)}, u32[]{:S(2)}) copy-start(f32[64]{0:T(128)} %param.26) | copy-start | bytes 772
  3.9 10.8 %copy-start.16 = (f32[64]{0:T(128)S(1)}, f32[64]{0:T(128)}, u32[]{:S(2)}) copy-start(f32[64]{0:T(128)} %param.27) | copy-start | bytes 772
  3.9 10.8 %copy-start.17 = (f32[64]{0:T(128)S(1)}, f32[64]{0:T(128)}, u32[]{:S(2)}) copy-start(f32[64]{0:T(128)} %param.31) | copy-start | bytes 772
  3.9 10.8 %copy-start.18 = (s32[64]{0:T(128)S(1)}, s32[64]{0:T(128)}, u32[]{:S(2)}) copy-start(s32[64]{0:T(128)} %param.25) | copy-start | bytes 772
  3.9 11.4 %copy-start.9 = (f32[256]{0:T(256)S(1)}, f32[256]{0:T(256)}, u32[]{:S(2)}) copy-start(f32[256]{0:T(256)} %param.19) | copy-start | bytes 3076
  4.1 1.8 %collective-permute-start = (f32[5,8,8,256]{3,2,1,0:T(8,128)S(1)}, f32[5,8,8,256]{3,2,1,0:T(8,128)S(1)}, u32[]{:S(2)}, u32[]{:S(2)}) collective-permute-start(f32[5,8,8,256]{3,2,1,0:T(8,128)S(1)} %side.1), channel_id=1, source_target_pairs={{0,1},{1,0},{2,3},{3,2},{4,5},{5,4},{6,7},{7,6},{8,9},{9,8},{10,11... | collective-permute-start | bytes 983048 | tf_op jit(solution)/shard_map/ppermute | solution.py:600
  5.8 1.0 %copy-start.3 = (f32[8,48,256]{2,1,0:T(8,128)S(1)}, f32[8,48,256]{2,1,0:T(8,128)}, u32[]{:S(2)}) copy-start(f32[8,48,256]{2,1,0:T(8,128)} %pre.5) | copy-start | bytes 1179652
  6.8 1.0 %copy-start.5 = (f32[8,48,256]{2,1,0:T(8,128)S(1)}, f32[8,48,256]{2,1,0:T(8,128)}, u32[]{:S(2)}) copy-start(f32[8,48,256]{2,1,0:T(8,128)} %vis.5) | copy-start | bytes 1179652
  7.8 11.1 %copy-start.7 = (bf16[1024,128]{1,0:T(8,128)(2,1)S(1)}, bf16[1024,128]{1,0:T(8,128)(2,1)}, u32[]{:S(2)}) copy-start(bf16[1024,128]{1,0:T(8,128)(2,1)} %nodes) | copy-start | bytes 786436
  7.8 11.1 %copy-start.8 = (f32[2048]{0:T(1024)S(1)}, f32[2048]{0:T(1024)}, u32[]{:S(2)}) copy-start(f32[2048]{0:T(1024)} %param.20) | copy-start | bytes 24580
  7.8 11.1 %copy-start.10 = (f32[2,128]{1,0:T(2,128)S(1)}, f32[2,128]{1,0:T(2,128)}, u32[]{:S(2)}) copy-start(f32[2,128]{1,0:T(2,128)} %refs_2_) | copy-start | bytes 3076
  7.8 17.5 %copy-start.13 = (s32[1,256]{1,0:T(1,128)S(1)}, s32[1,256]{1,0:T(1,128)}, u32[]{:S(2)}) copy-start(s32[1,256]{1,0:T(1,128)} %cell.1) | copy-start | bytes 3076
  8.5 11.0 %collective-permute-start.1 = (bf16[448,256]{1,0:T(8,128)(2,1)S(1)}, bf16[448,256]{1,0:T(8,128)(2,1)S(1)}, u32[]{:S(2)}, u32[]{:S(2)}) collective-permute-start(bf16[448,256]{1,0:T(8,128)(2,1)S(1)} %get-tuple-element.37), channel_id=1, source_target_pairs={{0,2},{2,4},{4,6},{6,8},{8,10},{10,12},{12,14},{14,16},{16,18},{18... | collective-permute-start | bytes 688136 | tf_op jit(solution)/shard_map/ppermute | solution.py:629
  13.3 12.0 %collective-permute-start.2 = (bf16[448,256]{1,0:T(8,128)(2,1)S(1)}, bf16[448,256]{1,0:T(8,128)(2,1)S(1)}, u32[]{:S(2)}, u32[]{:S(2)}) collective-permute-start(bf16[448,256]{1,0:T(8,128)(2,1)S(1)} %get-tuple-element.38), channel_id=1, source_target_pairs={{2,0},{4,2},{6,4},{8,6},{10,8},{12,10},{14,12},{16,14},{18,16},{20... | collective-permute-start | bytes 688136 | tf_op jit(solution)/shard_map/ppermute | solution.py:630
  14.6 26.5 %collective-permute-start.4 = (bf16[2048,128]{1,0:T(8,128)(2,1)S(1)}, bf16[2048,128]{1,0:T(8,128)(2,1)S(1)}, u32[]{:S(2)}, u32[]{:S(2)}) collective-permute-start(bf16[2048,128]{1,0:T(8,128)(2,1)S(1)} %copy-done.6), channel_id=1, source_target_pairs={{1,0},{0,1},{3,2},{2,3},{5,4},{4,5},{7,6},{6,7},{9,8},{8,9},{11,10... | collective-permute-start | bytes 1572872 | tf_op jit(solution)/shard_map/ppermute | solution.py:634
  14.8 4.1 %collective-permute-start.3 = (f32[1,4608]{1,0:T(1,128)S(1)}, f32[1,4608]{1,0:T(1,128)S(1)}, u32[]{:S(2)}, u32[]{:S(2)}) collective-permute-start(f32[1,4608]{1,0:T(1,128)S(1)} %constant_dynamic-update-slice_fusion.refs_0_.refs_5_.refs_6_), channel_id=1, source_target_pairs={{1,0},{0,1},{3,2},{2,3},{5,4},{4,5},{7,6},{6,7},{9,8},{8,9},{11,10... | collective-permute-start | bytes 55304 | tf_op jit(solution)/shard_map/ppermute | solution.py:634
  25.3 15.8 %copy-start.11 = (f32[128]{0:T(128)S(1)}, f32[128]{0:T(128)}, u32[]{:S(2)}) copy-start(f32[128]{0:T(128)} %param.28) | copy-start | bytes 1540
  25.3 15.8 %copy-start.12 = (f32[128]{0:T(128)S(1)}, f32[128]{0:T(128)}, u32[]{:S(2)}) copy-start(f32[128]{0:T(128)} %param.29) | copy-start | bytes 1540

commit v3 on v2

--- a/solution.py
+++ b/solution.py
@@ -23,6 +23,11 @@
     if cyclic:
         return [((i + step) % size, i) for i in range(size)]
     return [(i, i + step) for i in range(size) if 0 <= i + step < size]
+
+
+def pairs(size, first):
+    lower = range(first, size - 1, 2)
+    return [(i, i + 1) for i in lower] + [(i + 1, i) for i in lower]
 
 
 def parts_of(row):
@@ -55,42 +60,46 @@
         copy.wait()
 
 
-def pack_kernel(count_y, vel, pre, vis, left, right, up, down, stage, corner, sem):
+def pack_kernel(vel, pre, vis, near_out, far_out, stage, sem):
     layers, rows, height = pre.shape
-    iy = lax.axis_index("gy")
-    has = (iy > 0, iy < count_y - 1)
-    messages = ((up, layers - 2, layers - 1), (down, 0, 0))
+    odd = lax.rem(lax.axis_index("gx"), 2)
+    messages = ((near_out, 1 - odd), (far_out, odd))
     copies = []
-    for side, (out, first, near) in enumerate(messages):
+    for place, (out, upward) in enumerate(messages):
+        first = upward * (layers - 2)
+        near = upward * (layers - 1)
         copies += [
             pltpu.make_async_copy(
-                vel.at[:, pl.ds(first, 2)], stage.at[side, pl.ds(0, 3)], sem.at[side, 0]
+                vel.at[:, pl.ds(first, 2)], stage.at[place, pl.ds(0, 3)], sem.at[place, 0]
             ),
-            pltpu.make_async_copy(pre.at[pl.ds(first, 2)], stage.at[side, 3], sem.at[side, 1]),
-            pltpu.make_async_copy(vis.at[near], stage.at[side, 4, 0], sem.at[side, 2]),
-            pltpu.make_async_copy(
-                left.at[pl.ds(0, 4), near], corner.at[side, 0], sem.at[side, 3]
-            ),
-            pltpu.make_async_copy(
-                right.at[pl.ds(0, 4), near], corner.at[side, 1], sem.at[side, 4]
-            ),
+            pltpu.make_async_copy(pre.at[pl.ds(first, 2)], stage.at[place, 3], sem.at[place, 1]),
+            pltpu.make_async_copy(vis.at[near], stage.at[place, 4, 0], sem.at[place, 2]),
         ]
     for copy in copies:
         copy.start()
     for copy in copies:
         copy.wait()
-    for side, (out, first, near) in enumerate(messages):
+    for place, (out, _) in enumerate(messages):
         for field in range(4):
             for depth in range(2):
                 start = (field * 2 + depth) * rows
-                out[start : start + rows, :] = stage[side, field, depth].astype(bf16)
-        out[8 * rows : 9 * rows, :] = stage[side, 4, 0].astype(bf16)
-        lines = [corner[side, 0, f, PAD - 1 : PAD, :] for f in range(4)]
-        lines = [jnp.where(has[0], line, 0.0) for line in lines]
-        others = [corner[side, 1, f, 0:1, :] for f in range(4)]
-        lines += [jnp.where(has[1], line, 0.0) for line in others]
+                out[start : start + rows, :] = stage[place, field, depth].astype(bf16)
+        out[8 * rows : 9 * rows, :] = stage[place, 4, 0].astype(bf16)
+
+
+def corner_kernel(count_y, left, right, near_in, far_in, near_out, far_out):
+    layers, height = left.shape[1], left.shape[3]
+    start = near_out.shape[0] - 16
+    odd = lax.rem(lax.axis_index("gx"), 2)
+    iy = lax.axis_index("gy")
+    for out, upward in ((near_out, 1 - odd), (far_out, odd)):
+        near = upward * (layers - 1)
+        lines = [left[f, near, PAD - 1 : PAD, :] for f in range(4)]
+        lines = [jnp.where(iy > 0, line, 0.0) for line in lines]
+        others = [right[f, near, 0:1, :] for f in range(4)]
+        lines += [jnp.where(iy < count_y - 1, line, 0.0) for line in others]
         lines.append(jnp.zeros((8, height), f32))
-        out[9 * rows : 9 * rows + 16, :] = jnp.concatenate(lines, axis=0).astype(bf16)
+        out[start : start + 16, :] = jnp.concatenate(lines, axis=0).astype(bf16)
 
 
 def stepper(wind, height):
@@ -227,7 +236,7 @@
 
 
 def edge_kernel(
-    count_x, count_y, before, after, wind, cell, area, partial, pre_core,
+    count_x, count_y, near_message, far_message, wind, cell, area, partial, pre_core,
     vel_in, old_in, mid_in, visc_in,
     vel_out, pre_out, payload, old, mid, visc,
     stage, pre_full, vel_edge, sem, out_sem,
@@ -240,9 +249,10 @@
     has_right = iy < count_y - 1
     has_before = ix > 0
     has_after = ix < count_x - 1
+    odd = lax.rem(ix, 2)
     copies = [
-        pltpu.make_async_copy(message, stage.at[side], sem.at[side])
-        for side, message in enumerate((before, after))
+        pltpu.make_async_copy(near_message, stage.at[1 - odd], sem.at[0]),
+        pltpu.make_async_copy(far_message, stage.at[odd], sem.at[1]),
     ]
     for copy in copies:
         copy.start()
@@ -586,6 +596,10 @@
     params = pltpu.CompilerParams(vmem_limit_bytes=VMEM_BYTES)
     shape = jax.ShapeDtypeStruct
 
+    raw = [
+        pltpu.with_memory_space_constraint(value, pltpu.HBM)
+        for value in (velocity, pressure, viscosity)
+    ]
     starts = (None,) if count_y == 2 else (rows - PAD, 0)
     sides = pl.pallas_call(
         functools.partial(side_kernel, starts),
@@ -595,7 +609,7 @@
         scratch_shapes=[pltpu.SemaphoreType.DMA((len(starts), 3))],
         compiler_params=params,
         name="side",
-    )(velocity, pressure, viscosity)
+    )(*raw)
     if count_y == 2:
         left = right = lax.ppermute(sides[0], "gy", [(0, 1), (1, 0)])
     else:
@@ -603,31 +617,39 @@
         right = lax.ppermute(sides[1], "gy", shifts(count_y, -1, False))
 
     message_shape = (9 * rows + 16, height)
-    up, down = pl.pallas_call(
-        functools.partial(pack_kernel, count_y),
+    near_message, far_message = pl.pallas_call(
+        pack_kernel,
         out_shape=(shape(message_shape, bf16), shape(message_shape, bf16)),
-        in_specs=[whole(pl.ANY)] * 5,
+        in_specs=[whole(pl.ANY)] * 3,
         out_specs=(whole(), whole()),
         scratch_shapes=[
             pltpu.VMEM((2, 5, 2, rows, height), f32),
-            pltpu.VMEM((2, 2, 4, PAD, height), f32),
-            pltpu.SemaphoreType.DMA((2, 5)),
+            pltpu.SemaphoreType.DMA((2, 3)),
         ],
         compiler_params=params,
         name="pack",
-    )(velocity, pressure, viscosity, left, right)
+    )(*raw)
+    near_message, far_message = pl.pallas_call(
+        functools.partial(corner_kernel, count_y),
+        out_shape=(shape(message_shape, bf16), shape(message_shape, bf16)),
+        in_specs=[whole()] * 4,
+        out_specs=(whole(), whole()),
+        input_output_aliases={2: 0, 3: 1},
+        compiler_params=params,
+        name="corner",
+    )(left, right, near_message, far_message)
     tied = lax.optimization_barrier(
         (
-            up, down, left, right, panel_shapes, node_shapes, panel_area, slot_panel,
+            near_message, far_message, left, right, panel_shapes, node_shapes, panel_area, slot_panel,
             damper_node, damper_viscous, damper_hysteretic, damper_state, modal_state,
         )
     )
     (
-        up, down, left, right, panel_shapes, node_shapes, panel_area, slot_panel,
+        near_message, far_message, left, right, panel_shapes, node_shapes, panel_area, slot_panel,
         damper_node, damper_viscous, damper_hysteretic, damper_state, modal_state,
     ) = tied
-    before = lax.ppermute(up, "gx", shifts(count_x, 1, False))
-    after = lax.ppermute(down, "gx", shifts(count_x, -1, False))
+    near_message = lax.ppermute(near_message, "gx", pairs(count_x, 0))
+    far_message = lax.ppermute(far_message, "gx", pairs(count_x, 1))
 
     def around(value):
         return [value] + [
@@ -696,7 +718,7 @@
         ],
         compiler_params=params,
         name="inner",
-    )(velocity, pressure, viscosity, wind, left, right)
+    )(*raw, wind, left, right)
 
     velocity_next, pressure_next, payload, *_ = pl.pallas_call(
         functools.partial(edge_kernel, count_x, count_y),
@@ -723,7 +745,7 @@
         ],
         compiler_params=params,
         name="edge",
-    )(before, after, wind, cell, area, partial, pre_core, velocity_next, old, mid, visc)
+    )(near_message, far_message, wind, cell, area, partial, pre_core, velocity_next, old, mid, visc)
     received = lax.all_to_all(payload, both, 0, 0, tiled=True)
     received = received.reshape(count_x, count_y, load_rows + 2, LANES)
 

time: 52.4 us -> 45.6 us (0.87)
  local copies, waits for them, and re-layouts: 5.34 us -> 0.1 us
  waiting for transfers between devices: 7.03 us -> 3.34 us
  Pallas kernels: 10.3 us -> 13.1 us
  starting transfers between devices: 7.2 us -> 4.7 us
  blocking collectives: 21.2 us -> 23.1 us
    unnamed x41 -> x29, local copies, waits for them, and re-layouts: 5.33 us -> 0.09 us
    ppermute x2, starting transfers between devices: 6.07 us -> 3.57 us  [the longest x1 2.9 us: body(): near_message = lax.ppermute(near_message, 'gx', pairs(count_x, 0))]
    ppermute x2, waiting for transfers between devices: 5.77 us -> 3.33 us  [the longest x1 3.33 us: body(): near_message = lax.ppermute(near_message, 'gx', pairs(count_x, 0))]
    all_to_all x2, blocking collectives: 21.2 us -> 23.1 us  [body(): received = lax.all_to_all(payload, both, 0, 0, tiled=True)]
    ppermute x1, waiting for transfers between devices: 1.26 us -> 0.01 us  [body(): left = right = lax.ppermute(sides[0], 'gy', [(0, 1), (1, 0)])]
    pallas_call x1, Pallas kernels: 3.53 us -> 4.74 us  [body(): pl.pallas_call(functools.partial(inner_kernel, count_y), out_shape=(shape...]
    pallas_call x1, Pallas kernels: 0.09 us -> 1.09 us  [body(): pl.pallas_call(functools.partial(side_kernel, starts), out_shape=tuple((s...]
    pallas_call x1 -> x2, Pallas kernels: 0.64 us -> 1.27 us  [the longest x1 1.24 us: body(): pl.pallas_call(pack_kernel, out_shape=(shape(message_shape, bf16), shape(...]
  transfers between devices with their start and end apart: 5 -> 5, of which waited for: 2 -> 1; matrix products, arithmetic and copies ran while one was open for 0% -> 0% of each run, Pallas kernels for 15% -> 22%
where the time goes in v3:
time: 45.6 us; the launch traced here: 45.3 us
  blocking collectives  23.1 us (51%)
  Pallas kernels  13.1 us (29%)
  starting transfers between devices  4.7 us (10%)
  waiting for transfers between devices  3.34 us (7%)
  between operations  0.92 us (2%)
    all_to_all x2, blocking collectives, body(): received = lax.all_to_all(payload, both, 0, 0, tiled=True)  23.1 us
    pallas_call x1, Pallas kernels, body(): pl.pallas_call(functools.partial(inner_kernel, count_y), out_shape=(shape...  4.74 us
    pallas_call x1, Pallas kernels, body(): pl.pallas_call(functools.partial(edge_kernel, count_x, count_y), out_shap...  3.47 us
    ppermute x1, waiting for transfers between devices, body(): near_message = lax.ppermute(near_message, 'gx', pairs(count_x, 0))  3.33 us
    ppermute x1, starting transfers between devices, body(): near_message = lax.ppermute(near_message, 'gx', pairs(count_x, 0))  2.9 us
    pallas_call x1, Pallas kernels, body(): pl.pallas_call(pack_kernel, out_shape=(shape(message_shape, bf16), shape(...  1.24 us
    pallas_call x1, Pallas kernels, body(): pl.pallas_call(functools.partial(first_kernel, count_x, count_y, load_row...  1.22 us
    pallas_call x1, Pallas kernels, body(): pl.pallas_call(functools.partial(side_kernel, starts), out_shape=tuple((s...  1.09 us
  transfers between devices with their start and end apart: 5, of which 1 were waited for; matrix products, arithmetic and copies ran while one was open for 0% of the time, Pallas kernels for 22%

profile of v3, /device:TPU:0, one launch (start us, length us, event | category | flops | bytes accessed | tf_op | source)
XLA Modules:
  0.0 45.3 jit_solution(3665149219777095344)
XLA Ops:
  0.6 0.0 copy-start.8
  0.6 0.0 copy-start
  0.7 0.0 copy-start.12
  0.7 0.0 copy-start.9
  0.7 0.0 copy-start.10
  0.7 0.0 copy-start.11
  0.7 0.0 copy-start.3
  0.7 1.1 %side.1 = f32[5,8,8,256]{3,2,1,0:T(8,128)S(1)} custom-call(f32[3,8,48,256]{3,2,1,0:T(8,128)} %vel.5, f32[8,48,256]{2,1,0:T(8,128)} %pre.5, f32[8,48,256]{2,1,0:T(8,128)} %vis.5), custom_call_target="tpu_custom_call" | custom-call | tf_op jit(solution)/shard_map/side/pallas_call | solution.py:604
  1.8 0.0 copy-start.1
  1.8 0.0 copy-start.2
  1.8 0.0 copy-start.4
  1.8 0.0 copy-start.7
  1.9 0.5 %collective-permute-start = (f32[5,8,8,256]{3,2,1,0:T(8,128)S(1)}, f32[5,8,8,256]{3,2,1,0:T(8,128)S(1)}, u32[]{:S(2)}, u32[]{:S(2)}) collective-permute-start(f32[5,8,8,256]{3,2,1,0:T(8,128)S(1)} %side.1), channel_id=1, source_target_pairs={{0,1},{1,0},{2,3},{3,2},{4,5},{5,4},{6,7},{7,6},{8,9},{9,8},{10,11... | collective-permute-start | bytes 983048 | tf_op jit(solution)/shard_map/ppermute | solution.py:614
  2.4 1.2 %pack.1 = (bf16[448,256]{1,0:T(8,128)(2,1)S(1)}, bf16[448,256]{1,0:T(8,128)(2,1)S(1)}) custom-call(f32[3,8,48,256]{3,2,1,0:T(8,128)} %vel.5, f32[8,48,256]{2,1,0:T(8,128)} %pre.5, f32[8,48,256]{2,1,0:T(8,128)} %vis.5), custom_call_target="tpu_custom_call" | custom-call | tf_op jit(solution)/shard_map/pack/pallas_call | solution.py:620
  3.6 0.0 collective-permute-done.left.right
  3.7 0.0 copy-done.8
  3.7 2.9 %collective-permute-start.1 = (bf16[448,256]{1,0:T(8,128)(2,1)S(1)}, bf16[448,256]{1,0:T(8,128)(2,1)S(1)}, u32[]{:S(2)}, u32[]{:S(2)}) collective-permute-start(bf16[448,256]{1,0:T(8,128)(2,1)S(1)} %get-tuple-element.41), channel_id=1, source_target_pairs={{0,2},{4,6},{8,10},{12,14},{16,18},{20,22},{24,26},{28,30},{2,0},{... | collective-permute-start | bytes 688136 | tf_op jit(solution)/shard_map/ppermute | solution.py:651
  6.6 0.7 %collective-permute-start.2 = (bf16[448,256]{1,0:T(8,128)(2,1)S(1)}, bf16[448,256]{1,0:T(8,128)(2,1)S(1)}, u32[]{:S(2)}, u32[]{:S(2)}) collective-permute-start(bf16[448,256]{1,0:T(8,128)(2,1)S(1)} %get-tuple-element.42), channel_id=1, source_target_pairs={{2,4},{6,8},{10,12},{14,16},{18,20},{22,24},{26,28},{4,2},{8,6},{1... | collective-permute-start | bytes 688136 | tf_op jit(solution)/shard_map/ppermute | solution.py:652
  7.3 0.0 copy-done
  7.3 0.1 collective-permute-start.4
  7.4 0.0 copy-done.9
  7.4 0.0 copy-done.10
  7.4 0.0 copy-done.11
  7.4 0.0 copy-done.12
  7.5 0.5 %collective-permute-start.3 = (f32[1,4608]{1,0:T(1,128)S(1)}, f32[1,4608]{1,0:T(1,128)S(1)}, u32[]{:S(2)}, u32[]{:S(2)}) collective-permute-start(f32[1,4608]{1,0:T(1,128)S(1)} %constant_dynamic-update-slice_fusion.refs_0_.refs_5_.refs_6_), channel_id=1, source_target_pairs={{1,0},{0,1},{3,2},{2,3},{5,4},{4,5},{7,6},{6,7},{9,8},{8,9},{11,10... | collective-permute-start | bytes 55304 | tf_op jit(solution)/shard_map/ppermute | solution.py:656
  8.0 0.0 copy-done.3
  8.0 4.7 %inner.1 = (f32[3,8,48,256]{3,2,1,0:T(8,128)}, f32[2,4,5,64,256]{4,3,2,1,0:T(8,128)S(1)}, f32[2,4,5,64,256]{4,3,2,1,0:T(8,128)S(1)}, f32[2,5,64,256]{3,2,1,0:T(8,128)S(1)}, f32[4,48,256]{2,1,0:T(8,128)S(1)}) custom-call(f32[3,8,48,256]{3,2,1,0:T(8,128)} %vel.5, f32[8,48,256]{2,1,0:T(8,128)} %pre.5, f32[8,48,256]{2,1,0:T(8,128)} %vis.5, ...), custom_call_target="tpu_custom_call" | custom-call | tf_op jit(solution)/shard_map/inner/pallas_call | solution.py:700
  12.8 0.0 collective-permute-done.3.refs_1_.refs_6_.refs_7_
  12.8 0.0 copy-done.1
  12.8 0.0 copy-done.2
  12.8 0.0 copy-done.4
  12.8 0.6 %prepare.1 = (bf16[2,2,128,128]{3,2,1,0:T(8,128)(2,1)S(1)}, f32[2,128]{1,0:T(2,128)S(1)}, f32[1,256]{1,0:T(1,128)S(1)}) custom-call(s32[1,256]{1,0:T(1,128)S(1)} %constant_dynamic-slice_fusion.own_ids, f32[16,128]{1,0:T(8,128)S(1)} %bitcast.17, bf16[1024,128]{1,0:T(8,128)(2,1)S(1)} %copy-done.1, f32[2,128]{1,0:T(2,128)S(1)} %copy-done.4, ...), custom_call_target="tpu_custom_call" | custom-call | tf_op jit(solution)/shard_map/prepare/pallas_call | solution.py:685
  13.4 3.3 %collective-permute-done.1.near_message = bf16[448,256]{1,0:T(8,128)(2,1)S(1)} collective-permute-done((bf16[448,256]{1,0:T(8,128)(2,1)S(1)}, bf16[448,256]{1,0:T(8,128)(2,1)S(1)}, u32[]{:S(2)}, u32[]{:S(2)}) %collective-permute-start.1) | collective-permute-done | bytes 229408 | tf_op jit(solution)/shard_map/ppermute | solution.py:651
  16.7 0.0 collective-permute-done.2.far_message
  16.7 0.0 copy-done.7
  16.7 0.0 copy-start.5
  16.7 0.0 copy-start.6
  16.7 3.5 %edge.1 = (f32[3,8,48,256]{3,2,1,0:T(8,128)}, f32[8,48,256]{2,1,0:T(8,128)}, f32[32,4,128]{2,1,0:T(4,128)S(1)}, f32[2,4,5,64,256]{4,3,2,1,0:T(8,128)S(1)}, f32[2...) custom-call(bf16[448,256]{1,0:T(8,128)(2,1)S(1)} %collective-permute, ...), custom_call_target="tpu_custom_call", output_to_operand_aliasing={{0}: (7, {}), {3}: (8, {}), {4}: (9, {}), {5}: (10, {})} | custom-call | tf_op jit(solution)/shard_map/edge/pallas_call | solution.py:723
  20.2 14.2 %all_to_all.10 = f32[32,4,128]{2,1,0:T(4,128)S(1)} all-to-all(f32[32,4,128]{2,1,0:T(4,128)S(1)} %get-tuple-element.62), channel_id=1, replica_groups=mesh['gx'=16,'gy'=2] {'gx','gy'}, dimensions={0} | all-to-all | bytes 131072 | tf_op jit(solution)/shard_map/all_to_all | solution.py:749
  34.4 0.0 collective-permute-done.4.refs_8_
  34.4 0.0 copy-done.5
  34.4 0.0 copy-done.6
  34.4 1.2 %first.1 = (f32[32,2,128]{2,1,0:T(2,128)S(1)}, f32[4,128]{1,0:T(4,128)S(1)}, f32[2,1,128]{2,1,0:T(1,128)S(1)}) custom-call(f32[16,2,4,128]{3,2,1,0:T(4,128)S(1)} %bitcast.15, bf16[2,2,128,128]{3,2,1,0:T(8,128)(2,1)S(1)} %get-tuple-element.63.refs_1_, f32[2,128]{1,0:T(2,128)S(1)} %copy-done.4, f32[1,128]{1,0:T(1,128)S(1)} %bitcast.20, f32[1,128]{1,0:T(1,128)S(1)} %bitcast.22, ...), custom_call_target="tpu_custom_call" | custom-call | tf_op jit(solution)/shard_map/first/pallas_call | solution.py:754
  35.6 8.9 %all_to_all.11 = f32[32,2,128]{2,1,0:T(2,128)S(1)} all-to-all(f32[32,2,128]{2,1,0:T(2,128)S(1)} %get-tuple-element.65), channel_id=1, replica_groups=mesh['gx'=16,'gy'=2] {'gx','gy'}, dimensions={0} | all-to-all | bytes 65536 | tf_op jit(solution)/shard_map/all_to_all | solution.py:770
  44.6 0.8 %second.1 = (f32[2,128]{1,0:T(2,128)}, f32[1,64]{1,0:T(1,128)}) custom-call(f32[16,2,2,128]{3,2,1,0:T(2,128)S(1)} %bitcast.16, bf16[2,2,128,128]{3,2,1,0:T(8,128)(2,1)S(1)} %get-tuple-element.63.refs_1_, f32[1,128]{1,0:T(1,128)S(1)} %bitcast.21, f32[1,128]{1,0:T(1,128)S(1)} %bitcast.23, f32[4,128]{1,0:T(4,128)S(1)} %get-tuple-element.66.refs_4_, ...), custom_call_target="tpu_custom_call" | custom-call | tf_op jit(solution)/shard_map/second/pallas_call | solution.py:773
  (8 shorter events, 0.1 us)
Async XLA Ops:
  0.6 3.0 %copy-start.8 = (s32[1,4096]{1,0:T(1,128)S(1)}, s32[1,4096]{1,0:T(1,128)}, u32[]{:S(2)}) copy-start(s32[1,4096]{1,0:T(1,128)} %param.22) | copy-start | bytes 49156
  0.6 6.6 %copy-start = (bf16[2048,128]{1,0:T(8,128)(2,1)S(1)}, bf16[2048,128]{1,0:T(8,128)(2,1)}, u32[]{:S(2)}) copy-start(bf16[2048,128]{1,0:T(8,128)(2,1)} %refs_7_) | copy-start | bytes 1572868
  0.7 6.8 %copy-start.12 = (s32[64]{0:T(128)S(1)}, s32[64]{0:T(128)}, u32[]{:S(2)}) copy-start(s32[64]{0:T(128)} %param.25) | copy-start | bytes 772
  0.7 6.7 %copy-start.9 = (f32[64]{0:T(128)S(1)}, f32[64]{0:T(128)}, u32[]{:S(2)}) copy-start(f32[64]{0:T(128)} %param.26) | copy-start | bytes 772
  0.7 6.7 %copy-start.10 = (f32[64]{0:T(128)S(1)}, f32[64]{0:T(128)}, u32[]{:S(2)}) copy-start(f32[64]{0:T(128)} %param.27) | copy-start | bytes 772
  0.7 6.7 %copy-start.11 = (f32[64]{0:T(128)S(1)}, f32[64]{0:T(128)}, u32[]{:S(2)}) copy-start(f32[64]{0:T(128)} %param.31) | copy-start | bytes 772
  0.7 7.3 %copy-start.3 = (f32[256]{0:T(256)S(1)}, f32[256]{0:T(256)}, u32[]{:S(2)}) copy-start(f32[256]{0:T(256)} %param.19) | copy-start | bytes 3076
  1.8 11.0 %copy-start.1 = (bf16[1024,128]{1,0:T(8,128)(2,1)S(1)}, bf16[1024,128]{1,0:T(8,128)(2,1)}, u32[]{:S(2)}) copy-start(bf16[1024,128]{1,0:T(8,128)(2,1)} %nodes) | copy-start | bytes 786436
  1.8 11.0 %copy-start.2 = (f32[2048]{0:T(1024)S(1)}, f32[2048]{0:T(1024)}, u32[]{:S(2)}) copy-start(f32[2048]{0:T(1024)} %param.20) | copy-start | bytes 24580
  1.8 11.0 %copy-start.4 = (f32[2,128]{1,0:T(2,128)S(1)}, f32[2,128]{1,0:T(2,128)}, u32[]{:S(2)}) copy-start(f32[2,128]{1,0:T(2,128)} %refs_2_) | copy-start | bytes 3076
  1.8 14.9 %copy-start.7 = (s32[1,256]{1,0:T(1,128)S(1)}, s32[1,256]{1,0:T(1,128)}, u32[]{:S(2)}) copy-start(s32[1,256]{1,0:T(1,128)} %cell.1) | copy-start | bytes 3076
  1.9 1.8 %collective-permute-start = (f32[5,8,8,256]{3,2,1,0:T(8,128)S(1)}, f32[5,8,8,256]{3,2,1,0:T(8,128)S(1)}, u32[]{:S(2)}, u32[]{:S(2)}) collective-permute-start(f32[5,8,8,256]{3,2,1,0:T(8,128)S(1)} %side.1), channel_id=1, source_target_pairs={{0,1},{1,0},{2,3},{3,2},{4,5},{5,4},{6,7},{7,6},{8,9},{9,8},{10,11... | collective-permute-start | bytes 983048 | tf_op jit(solution)/shard_map/ppermute | solution.py:614
  3.7 13.0 %collective-permute-start.1 = (bf16[448,256]{1,0:T(8,128)(2,1)S(1)}, bf16[448,256]{1,0:T(8,128)(2,1)S(1)}, u32[]{:S(2)}, u32[]{:S(2)}) collective-permute-start(bf16[448,256]{1,0:T(8,128)(2,1)S(1)} %get-tuple-element.41), channel_id=1, source_target_pairs={{0,2},{4,6},{8,10},{12,14},{16,18},{20,22},{24,26},{28,30},{2,0},{... | collective-permute-start | bytes 688136 | tf_op jit(solution)/shard_map/ppermute | solution.py:651
  6.6 10.1 %collective-permute-start.2 = (bf16[448,256]{1,0:T(8,128)(2,1)S(1)}, bf16[448,256]{1,0:T(8,128)(2,1)S(1)}, u32[]{:S(2)}, u32[]{:S(2)}) collective-permute-start(bf16[448,256]{1,0:T(8,128)(2,1)S(1)} %get-tuple-element.42), channel_id=1, source_target_pairs={{2,4},{6,8},{10,12},{14,16},{18,20},{22,24},{26,28},{4,2},{8,6},{1... | collective-permute-start | bytes 688136 | tf_op jit(solution)/shard_map/ppermute | solution.py:652
  7.3 27.1 %collective-permute-start.4 = (bf16[2048,128]{1,0:T(8,128)(2,1)S(1)}, bf16[2048,128]{1,0:T(8,128)(2,1)S(1)}, u32[]{:S(2)}, u32[]{:S(2)}) collective-permute-start(bf16[2048,128]{1,0:T(8,128)(2,1)S(1)} %copy-done), channel_id=1, source_target_pairs={{1,0},{0,1},{3,2},{2,3},{5,4},{4,5},{7,6},{6,7},{9,8},{8,9},{11,10... | collective-permute-start | bytes 1572872 | tf_op jit(solution)/shard_map/ppermute | solution.py:656
  7.5 5.3 %collective-permute-start.3 = (f32[1,4608]{1,0:T(1,128)S(1)}, f32[1,4608]{1,0:T(1,128)S(1)}, u32[]{:S(2)}, u32[]{:S(2)}) collective-permute-start(f32[1,4608]{1,0:T(1,128)S(1)} %constant_dynamic-update-slice_fusion.refs_0_.refs_5_.refs_6_), channel_id=1, source_target_pairs={{1,0},{0,1},{3,2},{2,3},{5,4},{4,5},{7,6},{6,7},{9,8},{8,9},{11,10... | collective-permute-start | bytes 55304 | tf_op jit(solution)/shard_map/ppermute | solution.py:656
  16.7 17.7 %copy-start.5 = (f32[128]{0:T(128)S(1)}, f32[128]{0:T(128)}, u32[]{:S(2)}) copy-start(f32[128]{0:T(128)} %param.28) | copy-start | bytes 1540
  16.7 17.7 %copy-start.6 = (f32[128]{0:T(128)S(1)}, f32[128]{0:T(128)}, u32[]{:S(2)}) copy-start(f32[128]{0:T(128)} %param.29) | copy-start | bytes 1540

commit v4 on v3

--- a/solution.py
+++ b/solution.py
@@ -236,10 +236,10 @@
 
 
 def edge_kernel(
-    count_x, count_y, near_message, far_message, wind, cell, area, partial, pre_core,
+    count_x, count_y, near_message, far_message, wind, pick, weight, partial, pre_core,
     vel_in, old_in, mid_in, visc_in,
     vel_out, pre_out, payload, old, mid, visc,
-    stage, pre_full, vel_edge, sem, out_sem,
+    pre_full, vel_edge, out_sem,
 ):
     layers, rows, height = pre_full.shape
     last = PAD + rows
@@ -250,46 +250,17 @@
     has_before = ix > 0
     has_after = ix < count_x - 1
     odd = lax.rem(ix, 2)
-    copies = [
-        pltpu.make_async_copy(near_message, stage.at[1 - odd], sem.at[0]),
-        pltpu.make_async_copy(far_message, stage.at[odd], sem.at[1]),
-    ]
-    for copy in copies:
-        copy.start()
     pre_full[2 : layers - 2] = pre_core[...]
-    slots = cell.shape[1]
-    cells = layers * rows
-    same = lax.broadcasted_iota(jnp.int32, (LANES, LANES), 0) == lax.broadcasted_iota(
-        jnp.int32, (LANES, LANES), 1
-    )
-    place = cell[...]
-    line = place // height
-    level = place - line * height
-
-    def stand(row):
-        lines = [
-            jnp.sum(jnp.where(same, row[:, k : k + LANES], 0.0), axis=1, keepdims=True)
-            for k in range(0, slots, LANES)
-        ]
-        return jnp.concatenate(lines, axis=0)
-
-    line, level = stand(line.astype(f32)), stand(level.astype(f32))
-    own_area = stand(area[...])
-    pick = lax.broadcasted_iota(jnp.int32, (slots, cells), 1).astype(f32) == line
-    pick = pick.astype(f32).astype(bf16)
-    at_level = lax.broadcasted_iota(jnp.int32, (slots, height), 1).astype(f32) == level
-    for copy in copies:
-        copy.wait()
-    for side in range(2):
+    for message, side in ((near_message, 1 - odd), (far_message, odd)):
         near = 1 + 2 * side
         for field in range(4):
             for depth in range(2):
                 start = (field * 2 + depth) * rows
-                old[side, field, 3 * side + depth, PAD:last, :] = stage[
-                    side, start : start + rows, :
+                old[side, field, 3 * side + depth, PAD:last, :] = message[
+                    start : start + rows, :
                 ].astype(f32)
-        visc[side, near, PAD:last, :] = stage[side, 8 * rows : 9 * rows, :].astype(f32)
-        corner = stage[side, 9 * rows : 9 * rows + 16, :].astype(f32)
+        visc[side, near, PAD:last, :] = message[8 * rows : 9 * rows, :].astype(f32)
+        corner = message[9 * rows : 9 * rows + 16, :].astype(f32)
         for field in range(4):
             old[side, field, near, PAD - 1 : PAD, :] = corner[field : field + 1]
             old[side, field, near, last : last + 1, :] = corner[4 + field : 5 + field]
@@ -308,6 +279,11 @@
             mid[side, f, layer, pl.ds(row, 8), :] = result[f]
 
     blank = jnp.zeros((4, PAD, height), f32)
+
+    def vel_copy(side):
+        return pltpu.make_async_copy(
+            vel_edge.at[side], vel_out.at[:, pl.ds(side * (layers - 2), 2)], out_sem.at[side]
+        )
 
     @pl.loop(0, 2)
     def _(side):
@@ -348,37 +324,38 @@
                 for i in range(3):
                     vel_edge[side, i, place, here, :] = result[i]
                 pre_full[side * (layers - 2) + place, here, :] = result[3]
-
-    results = [
-        pltpu.make_async_copy(
-            vel_edge.at[side], vel_out.at[:, pl.ds(side * (layers - 2), 2)], out_sem.at[side]
-        )
-        for side in range(2)
-    ]
-    results.append(pltpu.make_async_copy(pre_full, pre_out, out_sem.at[2]))
-    for result in results:
-        result.start()
-    flat = pre_full[...].reshape(cells, height)
-    found = jnp.zeros((slots, height), f32)
+        vel_copy(side).start()
+
+    pre_copy = pltpu.make_async_copy(pre_full, pre_out, out_sem.at[2])
+    pre_copy.start()
+    flat = pre_full[...].reshape(layers * rows, height)
+    found = jnp.zeros(weight.shape, f32)
     for part in parts_of(flat):
-        found = found + jnp.dot(pick, part.astype(bf16), preferred_element_type=f32)
-    sampled = jnp.sum(jnp.where(at_level, found, 0.0), axis=1, keepdims=True)
-    loads = (own_area * sampled).astype(bf16).astype(f32)
+        found = found + jnp.dot(pick[...], part.astype(bf16), preferred_element_type=f32)
+    loads = jnp.sum(weight[...] * found, axis=1, keepdims=True).astype(bf16).astype(f32)
+    slots = weight.shape[0]
+    same = lax.broadcasted_iota(jnp.int32, (LANES, LANES), 0) == lax.broadcasted_iota(
+        jnp.int32, (LANES, LANES), 1
+    )
     lines = []
     for start in range(0, slots, LANES):
         chosen = jnp.where(same, loads[start : start + LANES], 0.0)
         lines.append(jnp.sum(chosen, axis=0, keepdims=True))
     message = jnp.concatenate(lines + [partial[...]], axis=0)
     payload[...] = jnp.broadcast_to(message[None], payload.shape)
-    for result in results:
-        result.wait()
-
-
-def prepare_kernel(slot_count, damper_width, own_ids, areas, nodes, modal, *refs):
-    smalls = refs[:-3]
-    shapes, partial, area = refs[-3:]
+    pre_copy.wait()
+    for side in range(2):
+        vel_copy(side).wait()
+
+
+def prepare_kernel(slot_count, damper_width, own_ids, cell, areas, nodes, modal, *refs):
+    count_y = (len(refs) - 4) // 2
+    smalls = refs[:count_y]
+    shapes, partial, pick, weight = refs[count_y : count_y + 4]
+    spreads = refs[count_y + 4 :]
     high_count = areas.shape[0]
     slots = own_ids.shape[1]
+    cells, height = pick.shape[1], weight.shape[1]
     ids = own_ids[...]
     high = jnp.where(ids < 0, -1, ids // LANES)
     low = ids - high * LANES
@@ -393,15 +370,38 @@
             (((0,), (0,)), ((), ())),
             preferred_element_type=f32,
         )
-    area[...] = jnp.sum(jnp.where(low_pick, spread, 0.0), axis=0, keepdims=True)
+    area = jnp.sum(jnp.where(low_pick, spread, 0.0), axis=0, keepdims=True)
+    same = lax.broadcasted_iota(jnp.int32, (LANES, LANES), 0) == lax.broadcasted_iota(
+        jnp.int32, (LANES, LANES), 1
+    )
+
+    def stand(row):
+        lines = [
+            jnp.sum(jnp.where(same, row[:, k : k + LANES], 0.0), axis=1, keepdims=True)
+            for k in range(0, slots, LANES)
+        ]
+        return jnp.concatenate(lines, axis=0)
+
+    place = cell[...]
+    line = place // height
+    level = place - line * height
+    line, level = stand(line.astype(f32)), stand(level.astype(f32))
+    rank = lax.broadcasted_iota(jnp.int32, (slots, cells), 1).astype(f32)
+    pick[...] = (rank == line).astype(f32).astype(bf16)
+    rank = lax.broadcasted_iota(jnp.int32, (slots, height), 1).astype(f32)
+    weight[...] = jnp.where(rank == level, stand(area), 0.0)
+    low_rank = lax.broadcasted_iota(jnp.int32, (LANES, slot_count), 0).astype(f32)
     node_rank = lax.broadcasted_iota(jnp.int32, (nodes.shape[0], damper_width), 0).astype(f32)
     table = nodes[...]
     for q, small in enumerate(smalls):
+        numbers = small[:, :slot_count]
+        numbers = numbers - jnp.floor(numbers * (1.0 / LANES)) * LANES
+        spreads[q][...] = (low_rank == numbers).astype(f32).astype(bf16)
         lower = small[:, slot_count + 3 * damper_width : slot_count + 4 * damper_width]
         for end in range(2):
-            pick = (node_rank == lower + (1.0 - end)).astype(f32).astype(bf16)
+            picked = (node_rank == lower + (1.0 - end)).astype(f32).astype(bf16)
             rows = lax.dot_general(
-                pick, table, (((0,), (0,)), ((), ())), preferred_element_type=f32
+                picked, table, (((0,), (0,)), ((), ())), preferred_element_type=f32
             )
             shapes[q, end] = rows.astype(bf16)
     state = modal[...]
@@ -464,26 +464,20 @@
     received, shapes, modal, frequency, ratio = refs[:5]
     smalls = refs[5 : 5 + count_y]
     tables = refs[5 + count_y : 5 + 2 * count_y]
-    payload, state, hysteresis_out, held, sem = refs[5 + 2 * count_y :]
+    spreads = refs[5 + 2 * count_y : 5 + 3 * count_y]
+    payload, state, hysteresis_out = refs[5 + 3 * count_y :]
     iy = lax.axis_index("gy")
-    copies = [
-        pltpu.make_async_copy(tables[q], held.at[q], sem.at[q]) for q in range(count_y)
-    ]
-    for copy in copies:
-        copy.start()
     panel_count = tables[0].shape[0]
     high_count = panel_count // LANES
     slot_count = count_x * load_rows * LANES
     width = payload.shape[-1]
     rank = lax.broadcasted_iota(jnp.int32, (high_count, LANES), 0).astype(f32)
-    low_rank = lax.broadcasted_iota(jnp.int32, (LANES, slot_count), 0).astype(f32)
     sides = []
     forces = []
     for q in range(count_y):
         piece = lax.rem(iy + q, count_y)
         ids = smalls[q][:, :slot_count]
         high = jnp.floor(ids * (1.0 / LANES))
-        low = ids - high * LANES
         chunks = []
         for i in range(count_x):
             for r in range(load_rows):
@@ -492,10 +486,9 @@
                 chunks.append(
                     jnp.where(rank == high[:, start : start + LANES], line, 0.0).astype(bf16)
                 )
-        spread = (low_rank == low).astype(f32).astype(bf16)
         sorted_loads = lax.dot_general(
             jnp.concatenate(chunks, axis=1),
-            spread,
+            spreads[q][...],
             (((1,), (1,)), ((), ())),
             preferred_element_type=f32,
         )
@@ -515,11 +508,9 @@
         hysteresis_out[q] = hysteresis
         forces.append(force)
     load = pulled(forces, shapes)
-    for copy in copies:
-        copy.wait()
     rows = jnp.zeros((high_count, modal.shape[1]), f32)
     for q in range(count_y):
-        rows = rows + jnp.dot(sides[q], held[q], preferred_element_type=f32)
+        rows = rows + jnp.dot(sides[q], tables[q][...], preferred_element_type=f32)
     panel_modal = jnp.sum(rows, axis=0, keepdims=True)
     displacement, velocity = advance_modes(
         panel_modal + load, frequency[...], ratio[...], modal[0:1, :], modal[1:2, :]
@@ -682,18 +673,20 @@
     smalls = around(small)
     cell = jnp.pad(slot_cell, ((0, 0), (0, slots_padded - slots)))
 
-    shapes, partial, area = pl.pallas_call(
+    shapes, partial, pick, weight, *spreads = pl.pallas_call(
         functools.partial(prepare_kernel, slot_count, damper_padded),
         out_shape=(
             shape((count_y, 2, damper_padded, mode_count), bf16),
             shape((2, damper_padded), f32),
-            shape((1, slots_padded), f32),
-        ),
-        in_specs=[whole()] * (4 + count_y),
-        out_specs=(whole(), whole(), whole()),
+            shape((slots_padded, layers * rows), bf16),
+            shape((slots_padded, height), f32),
+        )
+        + (shape((LANES, slot_count), bf16),) * count_y,
+        in_specs=[whole()] * (5 + count_y),
+        out_specs=(whole(),) * (4 + count_y),
         compiler_params=params,
         name="prepare",
-    )(own_ids, panel_area.reshape(-1, LANES), node_shapes, modal_state, *smalls)
+    )(own_ids, cell, panel_area.reshape(-1, LANES), node_shapes, modal_state, *smalls)
 
     tall = rows + 2 * PAD
     wind = wind_profile[None, :]
@@ -730,22 +723,22 @@
             shape(mid.shape, f32),
             shape(visc.shape, f32),
         ),
-        in_specs=[whole(pl.ANY)] * 2
-        + [whole()] * 5
+        in_specs=[whole()] * 7
         + [whole(pl.ANY)]
         + [whole()] * 3,
         out_specs=(whole(pl.ANY), whole(pl.ANY), whole(), whole(), whole(), whole()),
         input_output_aliases={7: 0, 8: 3, 9: 4, 10: 5},
         scratch_shapes=[
-            pltpu.VMEM((2,) + message_shape, bf16),
             pltpu.VMEM((layers, rows, height), f32),
             pltpu.VMEM((2, 3, 2, rows, height), f32),
-            pltpu.SemaphoreType.DMA((2,)),
             pltpu.SemaphoreType.DMA((3,)),
         ],
         compiler_params=params,
         name="edge",
-    )(near_message, far_message, wind, cell, area, partial, pre_core, velocity_next, old, mid, visc)
+    )(
+        near_message, far_message, wind, pick, weight, partial, pre_core,
+        velocity_next, old, mid, visc,
+    )
     received = lax.all_to_all(payload, both, 0, 0, tiled=True)
     received = received.reshape(count_x, count_y, load_rows + 2, LANES)
 
@@ -758,15 +751,11 @@
             shape((4, mode_count), f32),
             shape((count_y, 1, damper_padded), f32),
         ),
-        in_specs=[whole()] * (5 + count_y) + [whole(pl.ANY)] * count_y,
+        in_specs=[whole()] * (5 + 3 * count_y),
         out_specs=(whole(), whole(), whole()),
-        scratch_shapes=[
-            pltpu.VMEM((count_y,) + panel_shapes.shape, bf16),
-            pltpu.SemaphoreType.DMA((count_y,)),
-        ],
         compiler_params=params,
         name="first",
-    )(received, shapes, modal_state, frequency, damping_ratio, *smalls, *tables)
+    )(received, shapes, modal_state, frequency, damping_ratio, *smalls, *tables, *spreads)
     received = lax.all_to_all(payload, both, 0, 0, tiled=True)
     received = received.reshape(count_x, count_y, 2, damper_padded)
 

time: 45.6 us -> 44.7 us (0.980)
  waiting for transfers between devices: 3.34 us -> 2.84 us
    pallas_call x1, Pallas kernels: 3.47 us -> 2.77 us  [body(): pl.pallas_call(functools.partial(edge_kernel, count_x, count_y), out_shap...]
    ppermute x1, waiting for transfers between devices: 3.33 us -> 2.82 us  [body(): near_message = lax.ppermute(near_message, 'gx', pairs(count_x, 0))]
    pallas_call x1, Pallas kernels: 0.58 us -> 1.07 us  [body(): pl.pallas_call(functools.partial(prepare_kernel, slot_count, damper_padde...]
where the time goes in v4:
time: 44.7 us; the launch traced here: 44.5 us
  blocking collectives  23.2 us (52%)
  Pallas kernels  12.7 us (28%)
  starting transfers between devices  4.7 us (11%)
  waiting for transfers between devices  2.84 us (6%)
  between operations  0.92 us (2%)
    all_to_all x2, blocking collectives, body(): received = lax.all_to_all(payload, both, 0, 0, tiled=True)  23.2 us
    pallas_call x1, Pallas kernels, body(): pl.pallas_call(functools.partial(inner_kernel, count_y), out_shape=(shape...  4.74 us
    ppermute x1, starting transfers between devices, body(): near_message = lax.ppermute(near_message, 'gx', pairs(count_x, 0))  2.9 us
    ppermute x1, waiting for transfers between devices, body(): near_message = lax.ppermute(near_message, 'gx', pairs(count_x, 0))  2.82 us
    pallas_call x1, Pallas kernels, body(): pl.pallas_call(functools.partial(edge_kernel, count_x, count_y), out_shap...  2.77 us
    pallas_call x1, Pallas kernels, body(): pl.pallas_call(pack_kernel, out_shape=(shape(message_shape, bf16), shape(...  1.24 us
    pallas_call x1, Pallas kernels, body(): pl.pallas_call(functools.partial(side_kernel, starts), out_shape=tuple((s...  1.09 us
    pallas_call x1, Pallas kernels, body(): pl.pallas_call(functools.partial(prepare_kernel, slot_count, damper_padde...  1.07 us
  transfers between devices with their start and end apart: 5, of which 1 were waited for; matrix products, arithmetic and copies ran while one was open for 0% of the time, Pallas kernels for 22%

profile of v4, /device:TPU:0, one launch (start us, length us, event | category | flops | bytes accessed | tf_op | source)
XLA Modules:
  0.0 44.5 jit_solution(14673122433971299335)
XLA Ops:
  0.6 0.0 copy-start.8
  0.6 0.0 copy-start
  0.7 0.0 copy-start.12
  0.7 0.0 copy-start.9
  0.7 0.0 copy-start.10
  0.7 0.0 copy-start.11
  0.7 0.0 copy-start.3
  0.7 1.1 %side.1 = f32[5,8,8,256]{3,2,1,0:T(8,128)S(1)} custom-call(f32[3,8,48,256]{3,2,1,0:T(8,128)} %vel.5, f32[8,48,256]{2,1,0:T(8,128)} %pre.5, f32[8,48,256]{2,1,0:T(8,128)} %vis.5), custom_call_target="tpu_custom_call" | custom-call | tf_op jit(solution)/shard_map/side/pallas_call | solution.py:595
  1.8 0.0 copy-start.1
  1.8 0.0 copy-start.2
  1.8 0.0 copy-start.4
  1.8 0.0 copy-start.7
  1.9 0.5 %collective-permute-start = (f32[5,8,8,256]{3,2,1,0:T(8,128)S(1)}, f32[5,8,8,256]{3,2,1,0:T(8,128)S(1)}, u32[]{:S(2)}, u32[]{:S(2)}) collective-permute-start(f32[5,8,8,256]{3,2,1,0:T(8,128)S(1)} %side.1), channel_id=1, source_target_pairs={{0,1},{1,0},{2,3},{3,2},{4,5},{5,4},{6,7},{7,6},{8,9},{9,8},{10,11... | collective-permute-start | bytes 983048 | tf_op jit(solution)/shard_map/ppermute | solution.py:605
  2.4 1.2 %pack.1 = (bf16[448,256]{1,0:T(8,128)(2,1)S(1)}, bf16[448,256]{1,0:T(8,128)(2,1)S(1)}) custom-call(f32[3,8,48,256]{3,2,1,0:T(8,128)} %vel.5, f32[8,48,256]{2,1,0:T(8,128)} %pre.5, f32[8,48,256]{2,1,0:T(8,128)} %vis.5), custom_call_target="tpu_custom_call" | custom-call | tf_op jit(solution)/shard_map/pack/pallas_call | solution.py:611
  3.6 0.0 collective-permute-done.left.right
  3.7 0.0 copy-done.8
  3.7 2.9 %collective-permute-start.1 = (bf16[448,256]{1,0:T(8,128)(2,1)S(1)}, bf16[448,256]{1,0:T(8,128)(2,1)S(1)}, u32[]{:S(2)}, u32[]{:S(2)}) collective-permute-start(bf16[448,256]{1,0:T(8,128)(2,1)S(1)} %get-tuple-element.44), channel_id=1, source_target_pairs={{0,2},{4,6},{8,10},{12,14},{16,18},{20,22},{24,26},{28,30},{2,0},{... | collective-permute-start | bytes 688136 | tf_op jit(solution)/shard_map/ppermute | solution.py:642
  6.6 0.7 %collective-permute-start.2 = (bf16[448,256]{1,0:T(8,128)(2,1)S(1)}, bf16[448,256]{1,0:T(8,128)(2,1)S(1)}, u32[]{:S(2)}, u32[]{:S(2)}) collective-permute-start(bf16[448,256]{1,0:T(8,128)(2,1)S(1)} %get-tuple-element.45), channel_id=1, source_target_pairs={{2,4},{6,8},{10,12},{14,16},{18,20},{22,24},{26,28},{4,2},{8,6},{1... | collective-permute-start | bytes 688136 | tf_op jit(solution)/shard_map/ppermute | solution.py:643
  7.3 0.0 copy-done
  7.3 0.1 collective-permute-start.4
  7.4 0.0 copy-done.9
  7.4 0.0 copy-done.10
  7.4 0.0 copy-done.11
  7.4 0.0 copy-done.12
  7.5 0.5 %collective-permute-start.3 = (f32[1,4608]{1,0:T(1,128)S(1)}, f32[1,4608]{1,0:T(1,128)S(1)}, u32[]{:S(2)}, u32[]{:S(2)}) collective-permute-start(f32[1,4608]{1,0:T(1,128)S(1)} %constant_dynamic-update-slice_fusion.refs_0_.refs_5_.refs_6_), channel_id=1, source_target_pairs={{1,0},{0,1},{3,2},{2,3},{5,4},{4,5},{7,6},{6,7},{9,8},{8,9},{11,10... | collective-permute-start | bytes 55304 | tf_op jit(solution)/shard_map/ppermute | solution.py:647
  8.0 0.0 copy-done.3
  8.0 4.7 %inner.1 = (f32[3,8,48,256]{3,2,1,0:T(8,128)}, f32[2,4,5,64,256]{4,3,2,1,0:T(8,128)S(1)}, f32[2,4,5,64,256]{4,3,2,1,0:T(8,128)S(1)}, f32[2,5,64,256]{3,2,1,0:T(8,128)S(1)}, f32[4,48,256]{2,1,0:T(8,128)S(1)}) custom-call(f32[3,8,48,256]{3,2,1,0:T(8,128)} %vel.5, f32[8,48,256]{2,1,0:T(8,128)} %pre.5, f32[8,48,256]{2,1,0:T(8,128)} %vis.5, ...), custom_call_target="tpu_custom_call" | custom-call | tf_op jit(solution)/shard_map/inner/pallas_call | solution.py:693
  12.8 0.0 collective-permute-done.3.refs_1_.refs_6_.refs_7_
  12.8 0.0 copy-done.1
  12.8 0.0 copy-done.2
  12.8 0.0 copy-done.4
  12.8 0.0 copy-done.7
  12.8 1.1 %prepare.1 = (bf16[2,2,128,128]{3,2,1,0:T(8,128)(2,1)S(1)}, f32[2,128]{1,0:T(2,128)S(1)}, bf16[256,384]{1,0:T(8,128)(2,1)S(1)}, f32[256,256]{1,0:T(8,128)S(1)}, ...) custom-call(s32[1,256]{1,0:T(1,128)S(1)} %constant_dynamic-slice_fusion.own_ids, s32[1,256]{1,0:T(1,128)S(1)} %copy-done.7, ...), custom_call_target="tpu_custom_call" | custom-call | tf_op jit(solution)/shard_map/prepare/pallas_call | solution.py:676
  13.9 2.8 %collective-permute-done.1.near_message = bf16[448,256]{1,0:T(8,128)(2,1)S(1)} collective-permute-done((bf16[448,256]{1,0:T(8,128)(2,1)S(1)}, bf16[448,256]{1,0:T(8,128)(2,1)S(1)}, u32[]{:S(2)}, u32[]{:S(2)}) %collective-permute-start.1) | collective-permute-done | bytes 229408 | tf_op jit(solution)/shard_map/ppermute | solution.py:642
  16.7 0.0 collective-permute-done.2.far_message
  16.7 0.0 copy-start.5
  16.7 0.0 copy-start.6
  16.7 2.8 %edge.1 = (f32[3,8,48,256]{3,2,1,0:T(8,128)}, f32[8,48,256]{2,1,0:T(8,128)}, f32[32,4,128]{2,1,0:T(4,128)S(1)}, f32[2,4,5,64,256]{4,3,2,1,0:T(8,128)S(1)}, f32[2...) custom-call(bf16[448,256]{1,0:T(8,128)(2,1)S(1)} %collective-permute, ...), custom_call_target="tpu_custom_call", output_to_operand_aliasing={{0}: (7, {}), {3}: (8, {}), {4}: (9, {}), {5}: (10, {})} | custom-call | tf_op jit(solution)/shard_map/edge/pallas_call | solution.py:716
  19.5 14.2 %all_to_all.10 = f32[32,4,128]{2,1,0:T(4,128)S(1)} all-to-all(f32[32,4,128]{2,1,0:T(4,128)S(1)} %get-tuple-element.66), channel_id=1, replica_groups=mesh['gx'=16,'gy'=2] {'gx','gy'}, dimensions={0} | all-to-all | bytes 131072 | tf_op jit(solution)/shard_map/all_to_all | solution.py:742
  33.7 0.0 collective-permute-done.4.refs_8_
  33.7 0.0 copy-done.5
  33.7 0.0 copy-done.6
  33.7 1.1 %first.1 = (f32[32,2,128]{2,1,0:T(2,128)S(1)}, f32[4,128]{1,0:T(4,128)S(1)}, f32[2,1,128]{2,1,0:T(1,128)S(1)}) custom-call(f32[16,2,4,128]{3,2,1,0:T(4,128)S(1)} %bitcast.15, bf16[2,2,128,128]{3,2,1,0:T(8,128)(2,1)S(1)} %get-tuple-element.67.refs_1_, f32[2,128]{1,0:T(2,128)S(1)} %copy-done.4, f32[1,128]{1,0:T(1,128)S(1)} %bitcast.20, f32[1,128]{1,0:T(1,128)S(1)} %bitcast.22, ...), custom_call_target="tpu_custom_call" | custom-call | tf_op jit(solution)/shard_map/first/pallas_call | solution.py:747
  34.8 8.9 %all_to_all.11 = f32[32,2,128]{2,1,0:T(2,128)S(1)} all-to-all(f32[32,2,128]{2,1,0:T(2,128)S(1)} %get-tuple-element.71), channel_id=1, replica_groups=mesh['gx'=16,'gy'=2] {'gx','gy'}, dimensions={0} | all-to-all | bytes 65536 | tf_op jit(solution)/shard_map/all_to_all | solution.py:759
  43.7 0.8 %second.1 = (f32[2,128]{1,0:T(2,128)}, f32[1,64]{1,0:T(1,128)}) custom-call(f32[16,2,2,128]{3,2,1,0:T(2,128)S(1)} %bitcast.16, bf16[2,2,128,128]{3,2,1,0:T(8,128)(2,1)S(1)} %get-tuple-element.67.refs_1_, f32[1,128]{1,0:T(1,128)S(1)} %bitcast.21, f32[1,128]{1,0:T(1,128)S(1)} %bitcast.23, f32[4,128]{1,0:T(4,128)S(1)} %get-tuple-element.72.refs_4_, ...), custom_call_target="tpu_custom_call" | custom-call | tf_op jit(solution)/shard_map/second/pallas_call | solution.py:762
  (8 shorter events, 0.1 us)
Async XLA Ops:
  0.6 3.0 %copy-start.8 = (s32[1,4096]{1,0:T(1,128)S(1)}, s32[1,4096]{1,0:T(1,128)}, u32[]{:S(2)}) copy-start(s32[1,4096]{1,0:T(1,128)} %param.22) | copy-start | bytes 49156
  0.6 6.6 %copy-start = (bf16[2048,128]{1,0:T(8,128)(2,1)S(1)}, bf16[2048,128]{1,0:T(8,128)(2,1)}, u32[]{:S(2)}) copy-start(bf16[2048,128]{1,0:T(8,128)(2,1)} %refs_7_) | copy-start | bytes 1572868
  0.7 6.8 %copy-start.12 = (s32[64]{0:T(128)S(1)}, s32[64]{0:T(128)}, u32[]{:S(2)}) copy-start(s32[64]{0:T(128)} %param.25) | copy-start | bytes 772
  0.7 6.7 %copy-start.9 = (f32[64]{0:T(128)S(1)}, f32[64]{0:T(128)}, u32[]{:S(2)}) copy-start(f32[64]{0:T(128)} %param.26) | copy-start | bytes 772
  0.7 6.7 %copy-start.10 = (f32[64]{0:T(128)S(1)}, f32[64]{0:T(128)}, u32[]{:S(2)}) copy-start(f32[64]{0:T(128)} %param.27) | copy-start | bytes 772
  0.7 6.7 %copy-start.11 = (f32[64]{0:T(128)S(1)}, f32[64]{0:T(128)}, u32[]{:S(2)}) copy-start(f32[64]{0:T(128)} %param.31) | copy-start | bytes 772
  0.7 7.3 %copy-start.3 = (f32[256]{0:T(256)S(1)}, f32[256]{0:T(256)}, u32[]{:S(2)}) copy-start(f32[256]{0:T(256)} %param.19) | copy-start | bytes 3076
  1.8 11.0 %copy-start.1 = (bf16[1024,128]{1,0:T(8,128)(2,1)S(1)}, bf16[1024,128]{1,0:T(8,128)(2,1)}, u32[]{:S(2)}) copy-start(bf16[1024,128]{1,0:T(8,128)(2,1)} %nodes) | copy-start | bytes 786436
  1.8 11.0 %copy-start.2 = (f32[2048]{0:T(1024)S(1)}, f32[2048]{0:T(1024)}, u32[]{:S(2)}) copy-start(f32[2048]{0:T(1024)} %param.20) | copy-start | bytes 24580
  1.8 11.0 %copy-start.4 = (f32[2,128]{1,0:T(2,128)S(1)}, f32[2,128]{1,0:T(2,128)}, u32[]{:S(2)}) copy-start(f32[2,128]{1,0:T(2,128)} %refs_2_) | copy-start | bytes 3076
  1.8 11.0 %copy-start.7 = (s32[1,256]{1,0:T(1,128)S(1)}, s32[1,256]{1,0:T(1,128)}, u32[]{:S(2)}) copy-start(s32[1,256]{1,0:T(1,128)} %cell.1) | copy-start | bytes 3076
  1.9 1.8 %collective-permute-start = (f32[5,8,8,256]{3,2,1,0:T(8,128)S(1)}, f32[5,8,8,256]{3,2,1,0:T(8,128)S(1)}, u32[]{:S(2)}, u32[]{:S(2)}) collective-permute-start(f32[5,8,8,256]{3,2,1,0:T(8,128)S(1)} %side.1), channel_id=1, source_target_pairs={{0,1},{1,0},{2,3},{3,2},{4,5},{5,4},{6,7},{7,6},{8,9},{9,8},{10,11... | collective-permute-start | bytes 983048 | tf_op jit(solution)/shard_map/ppermute | solution.py:605
  3.7 13.0 %collective-permute-start.1 = (bf16[448,256]{1,0:T(8,128)(2,1)S(1)}, bf16[448,256]{1,0:T(8,128)(2,1)S(1)}, u32[]{:S(2)}, u32[]{:S(2)}) collective-permute-start(bf16[448,256]{1,0:T(8,128)(2,1)S(1)} %get-tuple-element.44), channel_id=1, source_target_pairs={{0,2},{4,6},{8,10},{12,14},{16,18},{20,22},{24,26},{28,30},{2,0},{... | collective-permute-start | bytes 688136 | tf_op jit(solution)/shard_map/ppermute | solution.py:642
  6.6 10.1 %collective-permute-start.2 = (bf16[448,256]{1,0:T(8,128)(2,1)S(1)}, bf16[448,256]{1,0:T(8,128)(2,1)S(1)}, u32[]{:S(2)}, u32[]{:S(2)}) collective-permute-start(bf16[448,256]{1,0:T(8,128)(2,1)S(1)} %get-tuple-element.45), channel_id=1, source_target_pairs={{2,4},{6,8},{10,12},{14,16},{18,20},{22,24},{26,28},{4,2},{8,6},{1... | collective-permute-start | bytes 688136 | tf_op jit(solution)/shard_map/ppermute | solution.py:643
  7.3 26.4 %collective-permute-start.4 = (bf16[2048,128]{1,0:T(8,128)(2,1)S(1)}, bf16[2048,128]{1,0:T(8,128)(2,1)S(1)}, u32[]{:S(2)}, u32[]{:S(2)}) collective-permute-start(bf16[2048,128]{1,0:T(8,128)(2,1)S(1)} %copy-done), channel_id=1, source_target_pairs={{1,0},{0,1},{3,2},{2,3},{5,4},{4,5},{7,6},{6,7},{9,8},{8,9},{11,10... | collective-permute-start | bytes 1572872 | tf_op jit(solution)/shard_map/ppermute | solution.py:647
  7.5 5.3 %collective-permute-start.3 = (f32[1,4608]{1,0:T(1,128)S(1)}, f32[1,4608]{1,0:T(1,128)S(1)}, u32[]{:S(2)}, u32[]{:S(2)}) collective-permute-start(f32[1,4608]{1,0:T(1,128)S(1)} %constant_dynamic-update-slice_fusion.refs_0_.refs_5_.refs_6_), channel_id=1, source_target_pairs={{1,0},{0,1},{3,2},{2,3},{5,4},{4,5},{7,6},{6,7},{9,8},{8,9},{11,10... | collective-permute-start | bytes 55304 | tf_op jit(solution)/shard_map/ppermute | solution.py:647
  16.7 17.0 %copy-start.5 = (f32[128]{0:T(128)S(1)}, f32[128]{0:T(128)}, u32[]{:S(2)}) copy-start(f32[128]{0:T(128)} %param.28) | copy-start | bytes 1540
  16.7 17.0 %copy-start.6 = (f32[128]{0:T(128)S(1)}, f32[128]{0:T(128)}, u32[]{:S(2)}) copy-start(f32[128]{0:T(128)} %param.29) | copy-start | bytes 1540

commit v5 on v4

--- a/solution.py
+++ b/solution.py
@@ -42,25 +42,8 @@
     return jnp.concatenate(rows + [filler], axis=0).astype(bf16)
 
 
-def side_kernel(starts, vel, pre, vis, *refs):
-    outs, sem = refs[:-1], refs[-1]
-    copies = []
-    for place, (start, out) in enumerate(zip(starts, outs)):
-        if start is None:
-            start = jnp.where(lax.axis_index("gy") == 0, pre.shape[1] - PAD, 0)
-        here = pl.ds(pl.multiple_of(start, PAD), PAD)
-        copies += [
-            pltpu.make_async_copy(vel.at[:, :, here], out.at[pl.ds(0, 3)], sem.at[place, 0]),
-            pltpu.make_async_copy(pre.at[:, here], out.at[3], sem.at[place, 1]),
-            pltpu.make_async_copy(vis.at[:, here], out.at[4], sem.at[place, 2]),
-        ]
-    for copy in copies:
-        copy.start()
-    for copy in copies:
-        copy.wait()
-
-
-def pack_kernel(vel, pre, vis, near_out, far_out, stage, sem):
+def pack_kernel(starts, vel, pre, vis, near_out, far_out, *refs):
+    sides, (stage, sem, side_sem) = refs[:-3], refs[-3:]
     layers, rows, height = pre.shape
     odd = lax.rem(lax.axis_index("gx"), 2)
     messages = ((near_out, 1 - odd), (far_out, odd))
@@ -75,7 +58,17 @@
             pltpu.make_async_copy(pre.at[pl.ds(first, 2)], stage.at[place, 3], sem.at[place, 1]),
             pltpu.make_async_copy(vis.at[near], stage.at[place, 4, 0], sem.at[place, 2]),
         ]
-    for copy in copies:
+    more = []
+    for place, (start, out) in enumerate(zip(starts, sides)):
+        if start is None:
+            start = jnp.where(lax.axis_index("gy") == 0, rows - PAD, 0)
+        here = pl.ds(pl.multiple_of(start, PAD), PAD)
+        more += [
+            pltpu.make_async_copy(vel.at[:, :, here], out.at[pl.ds(0, 3)], side_sem.at[place, 0]),
+            pltpu.make_async_copy(pre.at[:, here], out.at[3], side_sem.at[place, 1]),
+            pltpu.make_async_copy(vis.at[:, here], out.at[4], side_sem.at[place, 2]),
+        ]
+    for copy in copies + more:
         copy.start()
     for copy in copies:
         copy.wait()
@@ -85,21 +78,45 @@
                 start = (field * 2 + depth) * rows
                 out[start : start + rows, :] = stage[place, field, depth].astype(bf16)
         out[8 * rows : 9 * rows, :] = stage[place, 4, 0].astype(bf16)
-
-
-def corner_kernel(count_y, left, right, near_in, far_in, near_out, far_out):
+    for copy in more:
+        copy.wait()
+
+
+def corner_kernel(count_y, left, right, far_in, far_out):
     layers, height = left.shape[1], left.shape[3]
-    start = near_out.shape[0] - 16
+    start = far_out.shape[0] - 16
+    iy = lax.axis_index("gy")
+    near = lax.rem(lax.axis_index("gx"), 2) * (layers - 1)
+    lines = [left[f, near, PAD - 1 : PAD, :] for f in range(4)]
+    lines = [jnp.where(iy > 0, line, 0.0) for line in lines]
+    others = [right[f, near, 0:1, :] for f in range(4)]
+    lines += [jnp.where(iy < count_y - 1, line, 0.0) for line in others]
+    lines.append(jnp.zeros((8, height), f32))
+    far_out[start : start + 16, :] = jnp.concatenate(lines, axis=0).astype(bf16)
+
+
+def line_kernel(rows, message, *outs):
     odd = lax.rem(lax.axis_index("gx"), 2)
-    iy = lax.axis_index("gy")
-    for out, upward in ((near_out, 1 - odd), (far_out, odd)):
-        near = upward * (layers - 1)
-        lines = [left[f, near, PAD - 1 : PAD, :] for f in range(4)]
-        lines = [jnp.where(iy > 0, line, 0.0) for line in lines]
-        others = [right[f, near, 0:1, :] for f in range(4)]
-        lines += [jnp.where(iy < count_y - 1, line, 0.0) for line in others]
-        lines.append(jnp.zeros((8, height), f32))
-        out[start : start + 16, :] = jnp.concatenate(lines, axis=0).astype(bf16)
+    height = message.shape[1]
+
+    def lines(row):
+        low = row // 16 * 16
+        found = []
+        for field in range(4):
+            pair = []
+            for depth in range(2):
+                start = (field * 2 + depth) * rows + low
+                block = message[start : start + 16, :].astype(f32)
+                pair.append(block[row - low : row - low + 1])
+            found.append(jnp.where(odd == 1, pair[1], pair[0]))
+        return jnp.concatenate(found + [jnp.zeros((4, height), f32)], axis=0)
+
+    last, first = lines(rows - 1), lines(0)
+    if len(outs) == 1:
+        outs[0][...] = jnp.where(lax.axis_index("gy") == 0, last, first)
+    else:
+        outs[0][...] = last
+        outs[1][...] = first
 
 
 def stepper(wind, height):
@@ -140,8 +157,8 @@
 
 def inner_kernel(
     count_y, vel, pre, vis, wind, left, right,
-    vel_out, old_edge, mid_edge, visc_edge, pre_core,
-    old, mid, visc, vel_core, sem, out_sem,
+    vel_out, old_edge, mid_edge, visc_edge, pre_out,
+    old, mid, visc, sem,
 ):
     layers, rows, height = pre.shape
     last = PAD + rows
@@ -216,13 +233,9 @@
         for row in range(PAD, last, 8):
             result = advance(mid, layer, row)
             for i in range(3):
-                vel_core[i, layer - 2, row - PAD : row - PAD + 8, :] = result[i]
-            pre_core[layer - 2, row - PAD : row - PAD + 8, :] = result[3]
-
-    result = pltpu.make_async_copy(
-        vel_core, vel_out.at[:, pl.ds(2, layers - 4)], out_sem
-    )
-    result.start()
+                vel_out[i, layer, row - PAD : row - PAD + 8, :] = result[i]
+            pre_out[layer, row - PAD : row - PAD + 8, :] = result[3]
+
     for side, first_old, place_old, first_mid, place_mid in (
         (0, 0, 2, 1, 3),
         (1, layers - 2, 1, layers - 3, 0),
@@ -232,14 +245,12 @@
             for f in range(4):
                 old_edge[side, f, place_old + depth] = old[f, first_old + depth]
                 mid_edge[side, f, place_mid + depth] = mid[f, first_mid + depth]
-    result.wait()
 
 
 def edge_kernel(
-    count_x, count_y, near_message, far_message, wind, pick, weight, partial, pre_core,
-    vel_in, old_in, mid_in, visc_in,
-    vel_out, pre_out, payload, old, mid, visc,
-    pre_full, vel_edge, out_sem,
+    count_x, count_y, near_message, far_message, left_lines, right_lines, wind, pick, weight, found, partial,
+    vel_in, pre_in, old_in, mid_in, visc_in,
+    vel_out, pre_full, payload, old, mid, visc,
 ):
     layers, rows, height = pre_full.shape
     last = PAD + rows
@@ -250,7 +261,6 @@
     has_before = ix > 0
     has_after = ix < count_x - 1
     odd = lax.rem(ix, 2)
-    pre_full[2 : layers - 2] = pre_core[...]
     for message, side in ((near_message, 1 - odd), (far_message, odd)):
         near = 1 + 2 * side
         for field in range(4):
@@ -260,10 +270,15 @@
                     start : start + rows, :
                 ].astype(f32)
         visc[side, near, PAD:last, :] = message[8 * rows : 9 * rows, :].astype(f32)
-        corner = message[9 * rows : 9 * rows + 16, :].astype(f32)
+        if message is near_message:
+            low = jnp.where(has_left, left_lines[...], 0.0)
+            high = jnp.where(has_right, right_lines[...], 0.0)
+        else:
+            corner = message[9 * rows : 9 * rows + 16, :].astype(f32)
+            low, high = corner[0:4], corner[4:8]
         for field in range(4):
-            old[side, field, near, PAD - 1 : PAD, :] = corner[field : field + 1]
-            old[side, field, near, last : last + 1, :] = corner[4 + field : 5 + field]
+            old[side, field, near, PAD - 1 : PAD, :] = low[field : field + 1]
+            old[side, field, near, last : last + 1, :] = high[field : field + 1]
 
     step = stepper(wind, height)
 
@@ -279,11 +294,6 @@
             mid[side, f, layer, pl.ds(row, 8), :] = result[f]
 
     blank = jnp.zeros((4, PAD, height), f32)
-
-    def vel_copy(side):
-        return pltpu.make_async_copy(
-            vel_edge.at[side], vel_out.at[:, pl.ds(side * (layers - 2), 2)], out_sem.at[side]
-        )
 
     @pl.loop(0, 2)
     def _(side):
@@ -321,18 +331,16 @@
             for layer, place in ((2, side), (3 - 2 * side, 1 - side)):
                 result = advance(mid, side, layer, row)
                 here = pl.ds(row - PAD, 8)
+                target = side * (layers - 2) + place
                 for i in range(3):
-                    vel_edge[side, i, place, here, :] = result[i]
-                pre_full[side * (layers - 2) + place, here, :] = result[3]
-        vel_copy(side).start()
-
-    pre_copy = pltpu.make_async_copy(pre_full, pre_out, out_sem.at[2])
-    pre_copy.start()
-    flat = pre_full[...].reshape(layers * rows, height)
-    found = jnp.zeros(weight.shape, f32)
-    for part in parts_of(flat):
-        found = found + jnp.dot(pick[...], part.astype(bf16), preferred_element_type=f32)
-    loads = jnp.sum(weight[...] * found, axis=1, keepdims=True).astype(bf16).astype(f32)
+                    vel_out[i, target, here, :] = result[i]
+                pre_full[target, here, :] = result[3]
+
+    flat = [pre_full[start : start + 2].reshape(2 * rows, height) for start in (0, layers - 2)]
+    total = found[...]
+    for part in parts_of(jnp.concatenate(flat, axis=0)):
+        total = total + jnp.dot(pick[...], part.astype(bf16), preferred_element_type=f32)
+    loads = jnp.sum(weight[...] * total, axis=1, keepdims=True).astype(bf16).astype(f32)
     slots = weight.shape[0]
     same = lax.broadcasted_iota(jnp.int32, (LANES, LANES), 0) == lax.broadcasted_iota(
         jnp.int32, (LANES, LANES), 1
@@ -343,19 +351,17 @@
         lines.append(jnp.sum(chosen, axis=0, keepdims=True))
     message = jnp.concatenate(lines + [partial[...]], axis=0)
     payload[...] = jnp.broadcast_to(message[None], payload.shape)
-    pre_copy.wait()
-    for side in range(2):
-        vel_copy(side).wait()
-
-
-def prepare_kernel(slot_count, damper_width, own_ids, cell, areas, nodes, modal, *refs):
-    count_y = (len(refs) - 4) // 2
+
+
+def prepare_kernel(slot_count, damper_width, own_ids, cell, areas, nodes, modal, pre, *refs):
+    count_y = (len(refs) - 5) // 2
     smalls = refs[:count_y]
-    shapes, partial, pick, weight = refs[count_y : count_y + 4]
-    spreads = refs[count_y + 4 :]
+    shapes, partial, pick, weight, found = refs[count_y : count_y + 5]
+    spreads = refs[count_y + 5 :]
+    layers, rows = pre.shape[:2]
     high_count = areas.shape[0]
     slots = own_ids.shape[1]
-    cells, height = pick.shape[1], weight.shape[1]
+    height = weight.shape[1]
     ids = own_ids[...]
     high = jnp.where(ids < 0, -1, ids // LANES)
     low = ids - high * LANES
@@ -386,8 +392,16 @@
     line = place // height
     level = place - line * height
     line, level = stand(line.astype(f32)), stand(level.astype(f32))
-    rank = lax.broadcasted_iota(jnp.int32, (slots, cells), 1).astype(f32)
-    pick[...] = (rank == line).astype(f32).astype(bf16)
+    rank = lax.broadcasted_iota(jnp.int32, (slots, 4 * rows), 1).astype(f32)
+    shift = jnp.where(rank < 2 * rows, 0.0, float((layers - 4) * rows))
+    pick[...] = (rank + shift == line).astype(f32).astype(bf16)
+    inside = lax.broadcasted_iota(jnp.int32, (slots, (layers - 4) * rows), 1).astype(f32)
+    inside = (inside + 2.0 * rows == line).astype(f32).astype(bf16)
+    core = pre[2 : layers - 2].reshape((layers - 4) * rows, height)
+    total = jnp.zeros((slots, height), f32)
+    for part in parts_of(core):
+        total = total + jnp.dot(inside, part.astype(bf16), preferred_element_type=f32)
+    found[...] = total
     rank = lax.broadcasted_iota(jnp.int32, (slots, height), 1).astype(f32)
     weight[...] = jnp.where(rank == level, stand(area), 0.0)
     low_rank = lax.broadcasted_iota(jnp.int32, (LANES, slot_count), 0).astype(f32)
@@ -465,7 +479,13 @@
     smalls = refs[5 : 5 + count_y]
     tables = refs[5 + count_y : 5 + 2 * count_y]
     spreads = refs[5 + 2 * count_y : 5 + 3 * count_y]
-    payload, state, hysteresis_out = refs[5 + 3 * count_y :]
+    vel, pre, payload, state, hysteresis_out, vel_out, pre_out, sem = refs[5 + 3 * count_y :]
+    writes = [
+        pltpu.make_async_copy(vel, vel_out, sem.at[0]),
+        pltpu.make_async_copy(pre, pre_out, sem.at[1]),
+    ]
+    for write in writes:
+        write.start()
     iy = lax.axis_index("gy")
     panel_count = tables[0].shape[0]
     high_count = panel_count // LANES
@@ -521,6 +541,8 @@
     state[3:4, :] = panel_modal
     message = drift_times(displacement, velocity, shapes)
     payload[...] = jnp.broadcast_to(message[None], payload.shape)
+    for write in writes:
+        write.wait()
 
 
 def second_kernel(count_x, count_y, slot_count, *refs):
@@ -592,54 +614,52 @@
         for value in (velocity, pressure, viscosity)
     ]
     starts = (None,) if count_y == 2 else (rows - PAD, 0)
-    sides = pl.pallas_call(
-        functools.partial(side_kernel, starts),
-        out_shape=tuple(shape((5, layers, PAD, height), f32) for _ in starts),
+
+    def swapped(values):
+        if count_y == 2:
+            value = lax.ppermute(values[0], "gy", [(0, 1), (1, 0)])
+            return value, value
+        return (
+            lax.ppermute(values[0], "gy", shifts(count_y, 1, False)),
+            lax.ppermute(values[1], "gy", shifts(count_y, -1, False)),
+        )
+
+    near_shape, far_shape = (9 * rows, height), (9 * rows + 16, height)
+    near_message, far_message, *sides = pl.pallas_call(
+        functools.partial(pack_kernel, starts),
+        out_shape=(pltpu.VMEM(near_shape, bf16), pltpu.VMEM(far_shape, bf16))
+        + tuple(shape((5, layers, PAD, height), f32) for _ in starts),
         in_specs=[whole(pl.ANY)] * 3,
-        out_specs=tuple(whole(pl.ANY) for _ in starts),
-        scratch_shapes=[pltpu.SemaphoreType.DMA((len(starts), 3))],
-        compiler_params=params,
-        name="side",
-    )(*raw)
-    if count_y == 2:
-        left = right = lax.ppermute(sides[0], "gy", [(0, 1), (1, 0)])
-    else:
-        left = lax.ppermute(sides[0], "gy", shifts(count_y, 1, False))
-        right = lax.ppermute(sides[1], "gy", shifts(count_y, -1, False))
-
-    message_shape = (9 * rows + 16, height)
-    near_message, far_message = pl.pallas_call(
-        pack_kernel,
-        out_shape=(shape(message_shape, bf16), shape(message_shape, bf16)),
-        in_specs=[whole(pl.ANY)] * 3,
-        out_specs=(whole(), whole()),
+        out_specs=(whole(),) * 2 + (whole(pl.ANY),) * len(starts),
         scratch_shapes=[
             pltpu.VMEM((2, 5, 2, rows, height), f32),
             pltpu.SemaphoreType.DMA((2, 3)),
+            pltpu.SemaphoreType.DMA((len(starts), 3)),
         ],
         compiler_params=params,
         name="pack",
     )(*raw)
-    near_message, far_message = pl.pallas_call(
+    near_message = lax.ppermute(near_message, "gx", pairs(count_x, 0))
+    left, right = swapped(sides)
+    far_message = pl.pallas_call(
         functools.partial(corner_kernel, count_y),
-        out_shape=(shape(message_shape, bf16), shape(message_shape, bf16)),
-        in_specs=[whole()] * 4,
-        out_specs=(whole(), whole()),
-        input_output_aliases={2: 0, 3: 1},
+        out_shape=pltpu.VMEM(far_shape, bf16),
+        in_specs=[whole()] * 3,
+        out_specs=whole(),
+        input_output_aliases={2: 0},
         compiler_params=params,
         name="corner",
-    )(left, right, near_message, far_message)
+    )(left, right, far_message)
     tied = lax.optimization_barrier(
         (
-            near_message, far_message, left, right, panel_shapes, node_shapes, panel_area, slot_panel,
+            far_message, left, right, panel_shapes, node_shapes, panel_area, slot_panel,
             damper_node, damper_viscous, damper_hysteretic, damper_state, modal_state,
         )
     )
     (
-        near_message, far_message, left, right, panel_shapes, node_shapes, panel_area, slot_panel,
+        far_message, left, right, panel_shapes, node_shapes, panel_area, slot_panel,
         damper_node, damper_viscous, damper_hysteretic, damper_state, modal_state,
     ) = tied
-    near_message = lax.ppermute(near_message, "gx", pairs(count_x, 0))
     far_message = lax.ppermute(far_message, "gx", pairs(count_x, 1))
 
     def around(value):
@@ -673,89 +693,101 @@
     smalls = around(small)
     cell = jnp.pad(slot_cell, ((0, 0), (0, slots_padded - slots)))
 
-    shapes, partial, pick, weight, *spreads = pl.pallas_call(
+    tall = rows + 2 * PAD
+    wind = wind_profile[None, :]
+    velocity_next, old, mid, visc, pressure_next = pl.pallas_call(
+        functools.partial(inner_kernel, count_y),
+        out_shape=(
+            pltpu.VMEM(velocity.shape, f32),
+            shape((2, 4, 5, tall, height), f32),
+            shape((2, 4, 5, tall, height), f32),
+            shape((2, 5, tall, height), f32),
+            pltpu.VMEM(pressure.shape, f32),
+        ),
+        in_specs=[whole(pl.ANY)] * 3 + [whole()] + [whole(pl.ANY)] * 2,
+        out_specs=(whole(), whole(), whole(), whole(), whole()),
+        scratch_shapes=[
+            pltpu.VMEM((4, layers, tall, height), f32),
+            pltpu.VMEM((4, layers, tall, height), f32),
+            pltpu.VMEM((layers, tall, height), f32),
+            pltpu.SemaphoreType.DMA((9,)),
+        ],
+        compiler_params=params,
+        name="inner",
+    )(*raw, wind, left, right)
+
+    shapes, partial, pick, weight, found, *spreads = pl.pallas_call(
         functools.partial(prepare_kernel, slot_count, damper_padded),
         out_shape=(
             shape((count_y, 2, damper_padded, mode_count), bf16),
             shape((2, damper_padded), f32),
-            shape((slots_padded, layers * rows), bf16),
+            shape((slots_padded, 4 * rows), bf16),
+            shape((slots_padded, height), f32),
             shape((slots_padded, height), f32),
         )
         + (shape((LANES, slot_count), bf16),) * count_y,
-        in_specs=[whole()] * (5 + count_y),
-        out_specs=(whole(),) * (4 + count_y),
+        in_specs=[whole()] * (6 + count_y),
+        out_specs=(whole(),) * (5 + count_y),
         compiler_params=params,
         name="prepare",
-    )(own_ids, cell, panel_area.reshape(-1, LANES), node_shapes, modal_state, *smalls)
-
-    tall = rows + 2 * PAD
-    wind = wind_profile[None, :]
-    velocity_next, old, mid, visc, pre_core = pl.pallas_call(
-        functools.partial(inner_kernel, count_y),
-        out_shape=(
-            shape(velocity.shape, f32),
-            shape((2, 4, 5, tall, height), f32),
-            shape((2, 4, 5, tall, height), f32),
-            shape((2, 5, tall, height), f32),
-            shape((layers - 4, rows, height), f32),
-        ),
-        in_specs=[whole(pl.ANY)] * 3 + [whole()] + [whole(pl.ANY)] * 2,
-        out_specs=(whole(pl.ANY), whole(), whole(), whole(), whole()),
-        scratch_shapes=[
-            pltpu.VMEM((4, layers, tall, height), f32),
-            pltpu.VMEM((4, layers, tall, height), f32),
-            pltpu.VMEM((layers, tall, height), f32),
-            pltpu.VMEM((3, layers - 4, rows, height), f32),
-            pltpu.SemaphoreType.DMA((9,)),
-            pltpu.SemaphoreType.DMA,
-        ],
+    )(
+        own_ids, cell, panel_area.reshape(-1, LANES), node_shapes, modal_state,
+        pressure_next, *smalls,
+    )
+
+    near_message, pressure_next = lax.optimization_barrier((near_message, pressure_next))
+    lines = pl.pallas_call(
+        functools.partial(line_kernel, rows),
+        out_shape=tuple(shape((8, height), f32) for _ in starts),
+        in_specs=[whole()],
+        out_specs=tuple(whole() for _ in starts),
         compiler_params=params,
-        name="inner",
-    )(*raw, wind, left, right)
-
+        name="lines",
+    )(near_message)
+    left_lines, right_lines = swapped(lines)
     velocity_next, pressure_next, payload, *_ = pl.pallas_call(
         functools.partial(edge_kernel, count_x, count_y),
         out_shape=(
-            shape(velocity.shape, f32),
-            shape(pressure.shape, f32),
+            pltpu.VMEM(velocity.shape, f32),
+            pltpu.VMEM(pressure.shape, f32),
             shape((total, load_rows + 2, LANES), f32),
             shape(old.shape, f32),
             shape(mid.shape, f32),
             shape(visc.shape, f32),
         ),
-        in_specs=[whole()] * 7
-        + [whole(pl.ANY)]
-        + [whole()] * 3,
-        out_specs=(whole(pl.ANY), whole(pl.ANY), whole(), whole(), whole(), whole()),
-        input_output_aliases={7: 0, 8: 3, 9: 4, 10: 5},
-        scratch_shapes=[
-            pltpu.VMEM((layers, rows, height), f32),
-            pltpu.VMEM((2, 3, 2, rows, height), f32),
-            pltpu.SemaphoreType.DMA((3,)),
-        ],
+        in_specs=[whole()] * 14,
+        out_specs=(whole(),) * 6,
+        input_output_aliases={9: 0, 10: 1, 11: 3, 12: 4, 13: 5},
         compiler_params=params,
         name="edge",
     )(
-        near_message, far_message, wind, pick, weight, partial, pre_core,
-        velocity_next, old, mid, visc,
+        near_message, far_message, left_lines, right_lines,
+        wind, pick, weight, found, partial,
+        velocity_next, pressure_next, old, mid, visc,
     )
     received = lax.all_to_all(payload, both, 0, 0, tiled=True)
     received = received.reshape(count_x, count_y, load_rows + 2, LANES)
 
     frequency = frequency[None]
     damping_ratio = damping_ratio[None]
-    payload, state, hysteresis = pl.pallas_call(
+    payload, state, hysteresis, velocity_next, pressure_next = pl.pallas_call(
         functools.partial(first_kernel, count_x, count_y, load_rows),
         out_shape=(
             shape((total, 2, damper_padded), f32),
             shape((4, mode_count), f32),
             shape((count_y, 1, damper_padded), f32),
+            shape(velocity.shape, f32),
+            shape(pressure.shape, f32),
         ),
-        in_specs=[whole()] * (5 + 3 * count_y),
-        out_specs=(whole(), whole(), whole()),
+        in_specs=[whole()] * (7 + 3 * count_y),
+        out_specs=(whole(),) * 3 + (whole(pl.ANY),) * 2,
+        scratch_shapes=[pltpu.SemaphoreType.DMA((2,))],
         compiler_params=params,
         name="first",
-    )(received, shapes, modal_state, frequency, damping_ratio, *smalls, *tables, *spreads)
+    )(
+        received, shapes, modal_state, frequency, damping_ratio,
+        *smalls, *tables, *spreads, velocity_next, pressure_next,
+    )
     received = lax.all_to_all(payload, both, 0, 0, tiled=True)
     received = received.reshape(count_x, count_y, 2, damper_padded)
 

time: 44.7 us -> 43.4 us (0.971)
  blocking collectives: 23.2 us -> 26.2 us
  waiting for transfers between devices: 2.84 us -> 0.76 us
  Pallas kernels: 12.7 us -> 10.7 us
    all_to_all x2, blocking collectives: 23.2 us -> 26.2 us  [body(): received = lax.all_to_all(payload, both, 0, 0, tiled=True)]
    ppermute x1, waiting for transfers between devices: 2.82 us -> 0.74 us  [body(): near_message = lax.ppermute(near_message, 'gx', pairs(count_x, 0))]
    pallas_call x4, Pallas kernels: 7.1 us -> 5.54 us  [the longest x1 4.06 us: body(): pl.pallas_call(functools.partial(inner_kernel, count_y), out_shape=(pltpu...]
    pallas_call x1, Pallas kernels: 2.77 us -> 1.94 us  [body(): pl.pallas_call(functools.partial(edge_kernel, count_x, count_y), out_shap...]
  transfers between devices with their start and end apart: 5 -> 6, of which waited for: 1 -> 1; matrix products, arithmetic and copies ran while one was open for 0% -> 0% of each run, Pallas kernels for 22% -> 17%
where the time goes in v5:
time: 43.4 us; the launch traced here: 43.2 us
  blocking collectives  26.2 us (60%)
  Pallas kernels  10.7 us (25%)
  starting transfers between devices  4.47 us (10%)
  between operations  0.93 us (2%)
  waiting for transfers between devices  0.76 us (2%)
    all_to_all x2, blocking collectives, body(): received = lax.all_to_all(payload, both, 0, 0, tiled=True)  26.2 us
    pallas_call x1, Pallas kernels, body(): pl.pallas_call(functools.partial(inner_kernel, count_y), out_shape=(pltpu...  4.06 us
    ppermute x1, starting transfers between devices, body(): near_message = lax.ppermute(near_message, 'gx', pairs(count_x, 0))  2.56 us
    pallas_call x1, Pallas kernels, body(): pl.pallas_call(functools.partial(edge_kernel, count_x, count_y), out_shap...  1.94 us
    pallas_call x1, Pallas kernels, body(): pl.pallas_call(functools.partial(pack_kernel, starts), out_shape=(pltpu.V...  1.46 us
    pallas_call x1, Pallas kernels, body(): pl.pallas_call(functools.partial(first_kernel, count_x, count_y, load_row...  1.31 us
    pallas_call x1, Pallas kernels, body(): pl.pallas_call(functools.partial(prepare_kernel, slot_count, damper_padde...  1.16 us
  transfers between devices with their start and end apart: 6, of which 1 were waited for; matrix products, arithmetic and copies ran while one was open for 0% of the time, Pallas kernels for 17%

profile of v5, /device:TPU:0, one launch (start us, length us, event | category | flops | bytes accessed | tf_op | source)
XLA Modules:
  0.0 43.2 jit_solution(13363720859920946643)
XLA Ops:
  0.6 0.0 copy-start.2
  0.6 0.0 copy-start.8
  0.7 0.0 copy-start
  0.7 0.0 copy-start.1
  0.7 0.0 copy-start.12
  0.7 0.0 copy-start.9
  0.7 0.0 copy-start.10
  0.7 0.0 copy-start.4
  0.7 0.0 copy-start.11
  0.7 0.0 copy-start.3
  0.7 0.0 copy-start.7
  0.7 1.5 %pack.1 = (bf16[432,256]{1,0:T(8,128)(2,1)S(1)}, bf16[448,256]{1,0:T(8,128)(2,1)S(1)}, f32[5,8,8,256]{3,2,1,0:T(8,128)S(1)}) custom-call(f32[3,8,48,256]{3,2,1,0:T(8,128)} %vel.3, f32[8,48,256]{2,1,0:T(8,128)} %pre.3, f32[8,48,256]{2,1,0:T(8,128)} %vis.3), custom_call_target="tpu_custom_call" | custom-call | tf_op jit(solution)/shard_map/pack/pallas_call | solution.py:628
  2.2 0.5 %collective-permute-start.1 = (f32[5,8,8,256]{3,2,1,0:T(8,128)S(1)}, f32[5,8,8,256]{3,2,1,0:T(8,128)S(1)}, u32[]{:S(2)}, u32[]{:S(2)}) collective-permute-start(f32[5,8,8,256]{3,2,1,0:T(8,128)S(1)} %get-tuple-element.44), channel_id=1, source_target_pairs={{0,1},{1,0},{2,3},{3,2},{4,5},{5,4},{6,7},{7,6},{8,9},{9,8},{10,11... | collective-permute-start | bytes 983048 | tf_op jit(solution)/shard_map/ppermute | solution.py:620
  2.7 2.6 %collective-permute-start = (bf16[432,256]{1,0:T(8,128)(2,1)S(1)}, bf16[432,256]{1,0:T(8,128)(2,1)S(1)}, u32[]{:S(2)}, u32[]{:S(2)}) collective-permute-start(bf16[432,256]{1,0:T(8,128)(2,1)S(1)} %get-tuple-element.43), channel_id=1, source_target_pairs={{0,2},{4,6},{8,10},{12,14},{16,18},{20,22},{24,26},{28,30},{2,0},{... | collective-permute-start | bytes 663560 | tf_op jit(solution)/shard_map/ppermute | solution.py:642
  5.3 0.0 collective-permute-done.1.left.right
  5.3 0.0 copy-done.8
  5.3 0.7 %collective-permute-start.2 = (bf16[448,256]{1,0:T(8,128)(2,1)S(1)}, bf16[448,256]{1,0:T(8,128)(2,1)S(1)}, u32[]{:S(2)}, u32[]{:S(2)}) collective-permute-start(bf16[448,256]{1,0:T(8,128)(2,1)S(1)} %corner.1), channel_id=1, source_target_pairs={{2,4},{6,8},{10,12},{14,16},{18,20},{22,24},{26,28},{4,2},{8,6},{1... | collective-permute-start | bytes 688136 | tf_op jit(solution)/shard_map/ppermute | solution.py:663
  6.0 0.0 copy-done
  6.0 0.2 collective-permute-start.5
  6.3 0.0 copy-done.9
  6.3 0.0 copy-done.10
  6.3 0.0 copy-done.11
  6.3 0.0 copy-done.12
  6.4 0.4 collective-permute-start.4
  6.8 0.0 copy-done.3
  6.8 4.1 %inner.1 = (f32[3,8,48,256]{3,2,1,0:T(8,128)S(1)}, f32[2,4,5,64,256]{4,3,2,1,0:T(8,128)S(1)}, f32[2,4,5,64,256]{4,3,2,1,0:T(8,128)S(1)}, f32[2,5,64,256]{3,2,1,0:T(8,128)S(1)}, f32[8,48,256]{2,1,0:T(8,128)S(1)}) custom-call(f32[3,8,48,256]{3,2,1,0:T(8,128)} %vel.3, f32[8,48,256]{2,1,0:T(8,128)} %pre.3, f32[8,48,256]{2,1,0:T(8,128)} %vis.3, ...), custom_call_target="tpu_custom_call" | custom-call | tf_op jit(solution)/shard_map/inner/pallas_call | solution.py:698
  10.8 0.7 %collective-permute-done.message.near_message = bf16[432,256]{1,0:T(8,128)(2,1)S(1)} collective-permute-done((bf16[432,256]{1,0:T(8,128)(2,1)S(1)}, bf16[432,256]{1,0:T(8,128)(2,1)S(1)}, u32[]{:S(2)}, u32[]{:S(2)}) %collective-permute-start) | collective-permute-done | bytes 221216 | tf_op jit(solution)/shard_map/ppermute | solution.py:642
  11.6 0.1 collective-permute-start.3
  11.7 0.0 collective-permute-done.4.refs_1_.refs_6_.refs_7_
  11.7 0.0 copy-done.2
  11.7 0.0 copy-done.1
  11.7 0.0 copy-done.4
  11.7 0.0 copy-done.7
  11.7 1.2 %prepare.1 = (bf16[2,2,128,128]{3,2,1,0:T(8,128)(2,1)S(1)}, f32[2,128]{1,0:T(2,128)S(1)}, bf16[256,192]{1,0:T(8,128)(2,1)S(1)}, f32[256,256]{1,0:T(8,128)S(1)}, ...) custom-call(s32[1,256]{1,0:T(1,128)S(1)} %constant_dynamic-slice_fusion.own_ids, ...), custom_call_target="tpu_custom_call" | custom-call | tf_op jit(solution)/shard_map/prepare/pallas_call | solution.py:719
  12.9 0.0 collective-permute-done.3.left_lines.right_lines
  12.9 0.0 collective-permute-done.2.far_message
  12.9 0.0 copy-start.5
  12.9 0.0 copy-start.6
  13.0 1.9 %edge.1 = (f32[3,8,48,256]{3,2,1,0:T(8,128)S(1)}, f32[8,48,256]{2,1,0:T(8,128)S(1)}, f32[32,4,128]{2,1,0:T(4,128)S(1)}, f32[2,4,5,64,256]{4,3,2,1,0:T(8,128)S(1)...) custom-call(bf16[432,256]{1,0:T(8,128)(2,1)S(1)} %collective-permute, ...), custom_call_target="tpu_custom_call", output_to_operand_aliasing={{0}: (9, {}), {1}: (10, {}), {3}: (11, {}), {4}: (12, {}), ... | custom-call | tf_op jit(solution)/shard_map/edge/pallas_call | solution.py:748
  14.9 17.3 %all_to_all.10 = f32[32,4,128]{2,1,0:T(4,128)S(1)} all-to-all(f32[32,4,128]{2,1,0:T(4,128)S(1)} %get-tuple-element.68), channel_id=1, replica_groups=mesh['gx'=16,'gy'=2] {'gx','gy'}, dimensions={0} | all-to-all | bytes 131072 | tf_op jit(solution)/shard_map/all_to_all | solution.py:768
  32.2 0.0 collective-permute-done.5.refs_8_
  32.2 0.0 copy-done.5
  32.2 0.0 copy-done.6
  32.2 1.3 %first.1 = (f32[32,2,128]{2,1,0:T(2,128)S(1)}, f32[4,128]{1,0:T(4,128)S(1)}, f32[2,1,128]{2,1,0:T(1,128)S(1)}, f32[3,8,48,256]{3,2,1,0:T(8,128)}, f32[8,48,256]{2,1,0:T(8,128)}) custom-call(f32[16,2,4,128]{3,2,1,0:T(4,128)S(1)} %bitcast.15, bf16[2,2,128,128]{3,2,1,0:T(8,128)(2,1)S(1)} %get-tuple-element.69.refs_1_, f32[2,128]{1,0:T(2,128)S(1)} %copy-done.4, ...), custom_call_target="tpu_custom_call" | custom-call | tf_op jit(solution)/shard_map/first/pallas_call | solution.py:773
  33.5 8.9 %all_to_all.11 = f32[32,2,128]{2,1,0:T(2,128)S(1)} all-to-all(f32[32,2,128]{2,1,0:T(2,128)S(1)} %get-tuple-element.77), channel_id=1, replica_groups=mesh['gx'=16,'gy'=2] {'gx','gy'}, dimensions={0} | all-to-all | bytes 65536 | tf_op jit(solution)/shard_map/all_to_all | solution.py:791
  42.5 0.8 %second.1 = (f32[2,128]{1,0:T(2,128)}, f32[1,64]{1,0:T(1,128)}) custom-call(f32[16,2,2,128]{3,2,1,0:T(2,128)S(1)} %bitcast.16, bf16[2,2,128,128]{3,2,1,0:T(8,128)(2,1)S(1)} %get-tuple-element.69.refs_1_, f32[1,128]{1,0:T(1,128)S(1)} %bitcast.21, f32[1,128]{1,0:T(1,128)S(1)} %bitcast.23, f32[4,128]{1,0:T(4,128)S(1)} %get-tuple-element.78.refs_4_, ...), custom_call_target="tpu_custom_call" | custom-call | tf_op jit(solution)/shard_map/second/pallas_call | solution.py:794
  (9 shorter events, 0.1 us)
Async XLA Ops:
  0.6 11.1 %copy-start.2 = (f32[2048]{0:T(1024)S(1)}, f32[2048]{0:T(1024)}, u32[]{:S(2)}) copy-start(f32[2048]{0:T(1024)} %param.20) | copy-start | bytes 24580
  0.6 4.7 %copy-start.8 = (s32[1,4096]{1,0:T(1,128)S(1)}, s32[1,4096]{1,0:T(1,128)}, u32[]{:S(2)}) copy-start(s32[1,4096]{1,0:T(1,128)} %param.22) | copy-start | bytes 49156
  0.7 5.4 %copy-start = (bf16[2048,128]{1,0:T(8,128)(2,1)S(1)}, bf16[2048,128]{1,0:T(8,128)(2,1)}, u32[]{:S(2)}) copy-start(bf16[2048,128]{1,0:T(8,128)(2,1)} %refs_7_) | copy-start | bytes 1572868
  0.7 11.0 %copy-start.1 = (bf16[1024,128]{1,0:T(8,128)(2,1)S(1)}, bf16[1024,128]{1,0:T(8,128)(2,1)}, u32[]{:S(2)}) copy-start(bf16[1024,128]{1,0:T(8,128)(2,1)} %nodes) | copy-start | bytes 786436
  0.7 5.6 %copy-start.12 = (s32[64]{0:T(128)S(1)}, s32[64]{0:T(128)}, u32[]{:S(2)}) copy-start(s32[64]{0:T(128)} %param.25) | copy-start | bytes 772
  0.7 5.6 %copy-start.9 = (f32[64]{0:T(128)S(1)}, f32[64]{0:T(128)}, u32[]{:S(2)}) copy-start(f32[64]{0:T(128)} %param.26) | copy-start | bytes 772
  0.7 5.6 %copy-start.10 = (f32[64]{0:T(128)S(1)}, f32[64]{0:T(128)}, u32[]{:S(2)}) copy-start(f32[64]{0:T(128)} %param.27) | copy-start | bytes 772
  0.7 11.0 %copy-start.4 = (f32[2,128]{1,0:T(2,128)S(1)}, f32[2,128]{1,0:T(2,128)}, u32[]{:S(2)}) copy-start(f32[2,128]{1,0:T(2,128)} %refs_2_) | copy-start | bytes 3076
  0.7 5.6 %copy-start.11 = (f32[64]{0:T(128)S(1)}, f32[64]{0:T(128)}, u32[]{:S(2)}) copy-start(f32[64]{0:T(128)} %param.31) | copy-start | bytes 772
  0.7 6.0 %copy-start.3 = (f32[256]{0:T(256)S(1)}, f32[256]{0:T(256)}, u32[]{:S(2)}) copy-start(f32[256]{0:T(256)} %param.19) | copy-start | bytes 3076
  0.7 11.0 %copy-start.7 = (s32[1,256]{1,0:T(1,128)S(1)}, s32[1,256]{1,0:T(1,128)}, u32[]{:S(2)}) copy-start(s32[1,256]{1,0:T(1,128)} %cell.1) | copy-start | bytes 3076
  2.2 3.1 %collective-permute-start.1 = (f32[5,8,8,256]{3,2,1,0:T(8,128)S(1)}, f32[5,8,8,256]{3,2,1,0:T(8,128)S(1)}, u32[]{:S(2)}, u32[]{:S(2)}) collective-permute-start(f32[5,8,8,256]{3,2,1,0:T(8,128)S(1)} %get-tuple-element.44), channel_id=1, source_target_pairs={{0,1},{1,0},{2,3},{3,2},{4,5},{5,4},{6,7},{7,6},{8,9},{9,8},{10,11... | collective-permute-start | bytes 983048 | tf_op jit(solution)/shard_map/ppermute | solution.py:620
  2.7 8.8 %collective-permute-start = (bf16[432,256]{1,0:T(8,128)(2,1)S(1)}, bf16[432,256]{1,0:T(8,128)(2,1)S(1)}, u32[]{:S(2)}, u32[]{:S(2)}) collective-permute-start(bf16[432,256]{1,0:T(8,128)(2,1)S(1)} %get-tuple-element.43), channel_id=1, source_target_pairs={{0,2},{4,6},{8,10},{12,14},{16,18},{20,22},{24,26},{28,30},{2,0},{... | collective-permute-start | bytes 663560 | tf_op jit(solution)/shard_map/ppermute | solution.py:642
  5.3 7.6 %collective-permute-start.2 = (bf16[448,256]{1,0:T(8,128)(2,1)S(1)}, bf16[448,256]{1,0:T(8,128)(2,1)S(1)}, u32[]{:S(2)}, u32[]{:S(2)}) collective-permute-start(bf16[448,256]{1,0:T(8,128)(2,1)S(1)} %corner.1), channel_id=1, source_target_pairs={{2,4},{6,8},{10,12},{14,16},{18,20},{22,24},{26,28},{4,2},{8,6},{1... | collective-permute-start | bytes 688136 | tf_op jit(solution)/shard_map/ppermute | solution.py:663
  6.0 26.2 %collective-permute-start.5 = (bf16[2048,128]{1,0:T(8,128)(2,1)S(1)}, bf16[2048,128]{1,0:T(8,128)(2,1)S(1)}, u32[]{:S(2)}, u32[]{:S(2)}) collective-permute-start(bf16[2048,128]{1,0:T(8,128)(2,1)S(1)} %copy-done), channel_id=1, source_target_pairs={{1,0},{0,1},{3,2},{2,3},{5,4},{4,5},{7,6},{6,7},{9,8},{8,9},{11,10... | collective-permute-start | bytes 1572872 | tf_op jit(solution)/shard_map/ppermute | solution.py:667
  6.4 5.3 %collective-permute-start.4 = (f32[1,4608]{1,0:T(1,128)S(1)}, f32[1,4608]{1,0:T(1,128)S(1)}, u32[]{:S(2)}, u32[]{:S(2)}) collective-permute-start(f32[1,4608]{1,0:T(1,128)S(1)} %constant_dynamic-update-slice_fusion.refs_0_.refs_5_.refs_6_), channel_id=1, source_target_pairs={{1,0},{0,1},{3,2},{2,3},{5,4},{4,5},{7,6},{6,7},{9,8},{8,9},{11,10... | collective-permute-start | bytes 55304 | tf_op jit(solution)/shard_map/ppermute | solution.py:667
  11.6 1.3 %collective-permute-start.3 = (f32[8,256]{1,0:T(8,128)S(1)}, f32[8,256]{1,0:T(8,128)S(1)}, u32[]{:S(2)}, u32[]{:S(2)}) collective-permute-start(f32[8,256]{1,0:T(8,128)S(1)} %lines.1), channel_id=1, source_target_pairs={{0,1},{1,0},{2,3},{3,2},{4,5},{5,4},{6,7},{7,6},{8,9},{9,8},{10,11... | collective-permute-start | bytes 24584 | tf_op jit(solution)/shard_map/ppermute | solution.py:620
  12.9 19.3 %copy-start.5 = (f32[128]{0:T(128)S(1)}, f32[128]{0:T(128)}, u32[]{:S(2)}) copy-start(f32[128]{0:T(128)} %param.28) | copy-start | bytes 1540
  12.9 19.3 %copy-start.6 = (f32[128]{0:T(128)S(1)}, f32[128]{0:T(128)}, u32[]{:S(2)}) copy-start(f32[128]{0:T(128)} %param.29) | copy-start | bytes 1540

commit v6 on v5

--- a/solution.py
+++ b/solution.py
@@ -43,7 +43,8 @@
 
 
 def pack_kernel(starts, vel, pre, vis, near_out, far_out, *refs):
-    sides, (stage, sem, side_sem) = refs[:-3], refs[-3:]
+    sides, lines = refs[: len(starts)], refs[len(starts) : -3]
+    stage, sem, side_sem = refs[-3:]
     layers, rows, height = pre.shape
     odd = lax.rem(lax.axis_index("gx"), 2)
     messages = ((near_out, 1 - odd), (far_out, odd))
@@ -78,6 +79,16 @@
                 start = (field * 2 + depth) * rows
                 out[start : start + rows, :] = stage[place, field, depth].astype(bf16)
         out[8 * rows : 9 * rows, :] = stage[place, 4, 0].astype(bf16)
+    last = [stage[0, f, 1 - odd, rows - 1 : rows, :] for f in range(4)]
+    first = [stage[0, f, 1 - odd, 0:1, :] for f in range(4)]
+    filler = [jnp.zeros((12, height), f32)]
+    last = jnp.concatenate(last + filler, axis=0)
+    first = jnp.concatenate(first + filler, axis=0)
+    if len(lines) == 1:
+        lines[0][...] = jnp.where(lax.axis_index("gy") == 0, last, first).astype(bf16)
+    else:
+        lines[0][...] = last.astype(bf16)
+        lines[1][...] = first.astype(bf16)
     for copy in more:
         copy.wait()
 
@@ -93,30 +104,6 @@
     lines += [jnp.where(iy < count_y - 1, line, 0.0) for line in others]
     lines.append(jnp.zeros((8, height), f32))
     far_out[start : start + 16, :] = jnp.concatenate(lines, axis=0).astype(bf16)
-
-
-def line_kernel(rows, message, *outs):
-    odd = lax.rem(lax.axis_index("gx"), 2)
-    height = message.shape[1]
-
-    def lines(row):
-        low = row // 16 * 16
-        found = []
-        for field in range(4):
-            pair = []
-            for depth in range(2):
-                start = (field * 2 + depth) * rows + low
-                block = message[start : start + 16, :].astype(f32)
-                pair.append(block[row - low : row - low + 1])
-            found.append(jnp.where(odd == 1, pair[1], pair[0]))
-        return jnp.concatenate(found + [jnp.zeros((4, height), f32)], axis=0)
-
-    last, first = lines(rows - 1), lines(0)
-    if len(outs) == 1:
-        outs[0][...] = jnp.where(lax.axis_index("gy") == 0, last, first)
-    else:
-        outs[0][...] = last
-        outs[1][...] = first
 
 
 def stepper(wind, height):
@@ -247,99 +234,99 @@
                 mid_edge[side, f, place_mid + depth] = mid[f, first_mid + depth]
 
 
-def edge_kernel(
-    count_x, count_y, near_message, far_message, left_lines, right_lines, wind, pick, weight, found, partial,
-    vel_in, pre_in, old_in, mid_in, visc_in,
-    vel_out, pre_full, payload, old, mid, visc,
-):
-    layers, rows, height = pre_full.shape
+def edge_kernel(count_x, count_y, is_near, message, *refs):
+    if is_near:
+        left_lines, right_lines = refs[:2]
+        wind, pick, found = refs[2:5]
+        vel_out, pre_out, found_out, old, mid, visc = refs[10:]
+    else:
+        wind, pick, found, weight, partial = refs[:5]
+        vel_out, pre_out, payload, old, mid, visc = refs[10:]
+    layers, rows, height = pre_out.shape
     last = PAD + rows
     ix = lax.axis_index("gx")
     iy = lax.axis_index("gy")
     has_left = iy > 0
     has_right = iy < count_y - 1
-    has_before = ix > 0
-    has_after = ix < count_x - 1
     odd = lax.rem(ix, 2)
-    for message, side in ((near_message, 1 - odd), (far_message, odd)):
-        near = 1 + 2 * side
-        for field in range(4):
-            for depth in range(2):
-                start = (field * 2 + depth) * rows
-                old[side, field, 3 * side + depth, PAD:last, :] = message[
-                    start : start + rows, :
-                ].astype(f32)
-        visc[side, near, PAD:last, :] = message[8 * rows : 9 * rows, :].astype(f32)
-        if message is near_message:
-            low = jnp.where(has_left, left_lines[...], 0.0)
-            high = jnp.where(has_right, right_lines[...], 0.0)
-        else:
-            corner = message[9 * rows : 9 * rows + 16, :].astype(f32)
-            low, high = corner[0:4], corner[4:8]
-        for field in range(4):
-            old[side, field, near, PAD - 1 : PAD, :] = low[field : field + 1]
-            old[side, field, near, last : last + 1, :] = high[field : field + 1]
+    side = 1 - odd if is_near else odd
+    there = jnp.where(side == 0, ix > 0, ix < count_x - 1)
+    outside = 1 + 2 * side
+    for field in range(4):
+        for depth in range(2):
+            start = (field * 2 + depth) * rows
+            old[side, field, 3 * side + depth, PAD:last, :] = message[
+                start : start + rows, :
+            ].astype(f32)
+    visc[side, outside, PAD:last, :] = message[8 * rows : 9 * rows, :].astype(f32)
+    if is_near:
+        low = jnp.where(has_left, left_lines[...].astype(f32), 0.0)
+        high = jnp.where(has_right, right_lines[...].astype(f32), 0.0)
+    else:
+        corner = message[9 * rows : 9 * rows + 16, :].astype(f32)
+        low, high = corner[0:4], corner[4:8]
+    for field in range(4):
+        old[side, field, outside, PAD - 1 : PAD, :] = low[field : field + 1]
+        old[side, field, outside, last : last + 1, :] = high[field : field + 1]
 
     step = stepper(wind, height)
 
-    def advance(source, side, layer, row, edge=0):
+    def advance(source, layer, row, edge=0):
         def get(f, offset, low):
             return source[side, f, layer + offset, pl.ds(low, 8), :]
 
         return step(get, visc[side, layer, pl.ds(row, 8), :], row, edge)
 
-    def first(side, layer, row, edge=0):
-        result = advance(old, side, layer, row, edge)
+    def first(layer, row, edge=0):
+        result = advance(old, layer, row, edge)
         for f in range(4):
             mid[side, f, layer, pl.ds(row, 8), :] = result[f]
 
     blank = jnp.zeros((4, PAD, height), f32)
-
-    @pl.loop(0, 2)
-    def _(side):
-        there = jnp.where(side == 0, has_before, has_after)
-        outside = 1 + 2 * side
+    for row in range(PAD, last, 8):
+        first(2, row)
+
+    @pl.when(has_left)
+    def _():
+        first(2, 0, -1)
+
+    @pl.when(jnp.logical_not(has_left))
+    def _():
+        mid[side, :, 2, 0:PAD, :] = blank
+
+    @pl.when(has_right)
+    def _():
+        first(2, last, 1)
+
+    @pl.when(jnp.logical_not(has_right))
+    def _():
+        mid[side, :, 2, last : last + PAD, :] = blank
+
+    @pl.when(there)
+    def _():
         for row in range(PAD, last, 8):
-            first(side, 2, row)
-
-        @pl.when(has_left)
-        def _():
-            first(side, 2, 0, -1)
-
-        @pl.when(jnp.logical_not(has_left))
-        def _():
-            mid[side, :, 2, 0:PAD, :] = blank
-
-        @pl.when(has_right)
-        def _():
-            first(side, 2, last, 1)
-
-        @pl.when(jnp.logical_not(has_right))
-        def _():
-            mid[side, :, 2, last : last + PAD, :] = blank
-
-        @pl.when(there)
-        def _():
-            for row in range(PAD, last, 8):
-                first(side, outside, row)
-
-        @pl.when(jnp.logical_not(there))
-        def _():
-            mid[side, :, outside, PAD:last, :] = jnp.zeros((4, rows, height), f32)
-
-        for row in range(PAD, last, 8):
-            for layer, place in ((2, side), (3 - 2 * side, 1 - side)):
-                result = advance(mid, side, layer, row)
-                here = pl.ds(row - PAD, 8)
-                target = side * (layers - 2) + place
-                for i in range(3):
-                    vel_out[i, target, here, :] = result[i]
-                pre_full[target, here, :] = result[3]
-
-    flat = [pre_full[start : start + 2].reshape(2 * rows, height) for start in (0, layers - 2)]
+            first(outside, row)
+
+    @pl.when(jnp.logical_not(there))
+    def _():
+        mid[side, :, outside, PAD:last, :] = jnp.zeros((4, rows, height), f32)
+
+    for row in range(PAD, last, 8):
+        for layer, place in ((2, side), (3 - 2 * side, 1 - side)):
+            result = advance(mid, layer, row)
+            here = pl.ds(row - PAD, 8)
+            target = side * (layers - 2) + place
+            for i in range(3):
+                vel_out[i, target, here, :] = result[i]
+            pre_out[target, here, :] = result[3]
+
+    flat = pre_out[pl.ds(side * (layers - 2), 2)].reshape(2 * rows, height)
     total = found[...]
-    for part in parts_of(jnp.concatenate(flat, axis=0)):
-        total = total + jnp.dot(pick[...], part.astype(bf16), preferred_element_type=f32)
+    for part in parts_of(flat):
+        total = total + jnp.dot(pick[side], part.astype(bf16), preferred_element_type=f32)
+    if is_near:
+        found_out[...] = total
+        return
     loads = jnp.sum(weight[...] * total, axis=1, keepdims=True).astype(bf16).astype(f32)
     slots = weight.shape[0]
     same = lax.broadcasted_iota(jnp.int32, (LANES, LANES), 0) == lax.broadcasted_iota(
@@ -392,9 +379,10 @@
     line = place // height
     level = place - line * height
     line, level = stand(line.astype(f32)), stand(level.astype(f32))
-    rank = lax.broadcasted_iota(jnp.int32, (slots, 4 * rows), 1).astype(f32)
-    shift = jnp.where(rank < 2 * rows, 0.0, float((layers - 4) * rows))
-    pick[...] = (rank + shift == line).astype(f32).astype(bf16)
+    rank = lax.broadcasted_iota(jnp.int32, (slots, 2 * rows), 1).astype(f32)
+    for side in range(2):
+        start = float(side * (layers - 2) * rows)
+        pick[side] = (rank + start == line).astype(f32).astype(bf16)
     inside = lax.broadcasted_iota(jnp.int32, (slots, (layers - 4) * rows), 1).astype(f32)
     inside = (inside + 2.0 * rows == line).astype(f32).astype(bf16)
     core = pre[2 : layers - 2].reshape((layers - 4) * rows, height)
@@ -625,12 +613,13 @@
         )
 
     near_shape, far_shape = (9 * rows, height), (9 * rows + 16, height)
-    near_message, far_message, *sides = pl.pallas_call(
+    near_message, far_message, *rest = pl.pallas_call(
         functools.partial(pack_kernel, starts),
         out_shape=(pltpu.VMEM(near_shape, bf16), pltpu.VMEM(far_shape, bf16))
-        + tuple(shape((5, layers, PAD, height), f32) for _ in starts),
+        + tuple(shape((5, layers, PAD, height), f32) for _ in starts)
+        + tuple(pltpu.VMEM((16, height), bf16) for _ in starts),
         in_specs=[whole(pl.ANY)] * 3,
-        out_specs=(whole(),) * 2 + (whole(pl.ANY),) * len(starts),
+        out_specs=(whole(),) * 2 + (whole(pl.ANY),) * len(starts) + (whole(),) * len(starts),
         scratch_shapes=[
             pltpu.VMEM((2, 5, 2, rows, height), f32),
             pltpu.SemaphoreType.DMA((2, 3)),
@@ -640,7 +629,8 @@
         name="pack",
     )(*raw)
     near_message = lax.ppermute(near_message, "gx", pairs(count_x, 0))
-    left, right = swapped(sides)
+    left, right = swapped(rest[: len(starts)])
+    lines = rest[len(starts) :]
     far_message = pl.pallas_call(
         functools.partial(corner_kernel, count_y),
         out_shape=pltpu.VMEM(far_shape, bf16),
@@ -661,6 +651,20 @@
         damper_node, damper_viscous, damper_hysteretic, damper_state, modal_state,
     ) = tied
     far_message = lax.ppermute(far_message, "gx", pairs(count_x, 1))
+    across = [
+        [
+            (i * count_y + k, j * count_y + k + step)
+            for i, j in pairs(count_x, 0)
+            for k in range(count_y)
+            if 0 <= k + step < count_y
+        ]
+        for step in (1, -1)
+    ]
+    if count_y == 2:
+        left_lines = right_lines = lax.ppermute(lines[0], both, across[0] + across[1])
+    else:
+        left_lines = lax.ppermute(lines[0], both, across[0])
+        right_lines = lax.ppermute(lines[1], both, across[1])
 
     def around(value):
         return [value] + [
@@ -721,7 +725,7 @@
         out_shape=(
             shape((count_y, 2, damper_padded, mode_count), bf16),
             shape((2, damper_padded), f32),
-            shape((slots_padded, 4 * rows), bf16),
+            shape((2, slots_padded, 2 * rows), bf16),
             shape((slots_padded, height), f32),
             shape((slots_padded, height), f32),
         )
@@ -735,35 +739,45 @@
         pressure_next, *smalls,
     )
 
-    near_message, pressure_next = lax.optimization_barrier((near_message, pressure_next))
-    lines = pl.pallas_call(
-        functools.partial(line_kernel, rows),
-        out_shape=tuple(shape((8, height), f32) for _ in starts),
-        in_specs=[whole()],
-        out_specs=tuple(whole() for _ in starts),
-        compiler_params=params,
-        name="lines",
-    )(near_message)
-    left_lines, right_lines = swapped(lines)
-    velocity_next, pressure_next, payload, *_ = pl.pallas_call(
-        functools.partial(edge_kernel, count_x, count_y),
-        out_shape=(
-            pltpu.VMEM(velocity.shape, f32),
-            pltpu.VMEM(pressure.shape, f32),
-            shape((total, load_rows + 2, LANES), f32),
-            shape(old.shape, f32),
-            shape(mid.shape, f32),
-            shape(visc.shape, f32),
-        ),
-        in_specs=[whole()] * 14,
-        out_specs=(whole(),) * 6,
-        input_output_aliases={9: 0, 10: 1, 11: 3, 12: 4, 13: 5},
-        compiler_params=params,
-        name="edge",
-    )(
-        near_message, far_message, left_lines, right_lines,
-        wind, pick, weight, found, partial,
-        velocity_next, pressure_next, old, mid, visc,
+    def edge(is_near, result, *operands):
+        kept = (velocity_next, pressure_next, old, mid, visc)
+        base = len(operands)
+        return pl.pallas_call(
+            functools.partial(edge_kernel, count_x, count_y, is_near),
+            out_shape=(
+                pltpu.VMEM(velocity.shape, f32),
+                pltpu.VMEM(pressure.shape, f32),
+                result,
+                pltpu.VMEM(old.shape, f32),
+                pltpu.VMEM(mid.shape, f32),
+                pltpu.VMEM(visc.shape, f32),
+            ),
+            in_specs=[whole()] * (base + 5),
+            out_specs=(whole(),) * 6,
+            input_output_aliases={base: 0, base + 1: 1, base + 2: 3, base + 3: 4, base + 4: 5},
+            compiler_params=params,
+            name="near" if is_near else "far",
+        )(*operands, *kept)
+
+    velocity_next, pressure_next, found, old, mid, visc = edge(
+        True,
+        pltpu.VMEM(found.shape, f32),
+        near_message,
+        left_lines,
+        right_lines,
+        wind,
+        pick,
+        found,
+    )
+    velocity_next, pressure_next, payload, *_ = edge(
+        False,
+        shape((total, load_rows + 2, LANES), f32),
+        far_message,
+        wind,
+        pick,
+        found,
+        weight,
+        partial,
     )
     received = lax.all_to_all(payload, both, 0, 0, tiled=True)
     received = received.reshape(count_x, count_y, load_rows + 2, LANES)

time: 43.4 us -> 42.1 us (0.970)
  waiting for transfers between devices: 0.76 us -> 0.02 us
  blocking collectives: 26.2 us -> 25.7 us
    ppermute x1, waiting for transfers between devices: 0.74 us -> 0.01 us  [body(): near_message = lax.ppermute(near_message, 'gx', pairs(count_x, 0))]
    all_to_all x2, blocking collectives: 26.2 us -> 25.7 us  [body(): received = lax.all_to_all(payload, both, 0, 0, tiled=True)]
  transfers between devices with their start and end apart: 6 -> 6, of which waited for: 1 -> 0; matrix products, arithmetic and copies ran while one was open for 0% -> 0% of each run, Pallas kernels for 17% -> 17%
where the time goes in v6:
time: 42.1 us; the launch traced here: 41.9 us
  blocking collectives  25.7 us (61%)
  Pallas kernels  10.6 us (25%)
  starting transfers between devices  4.47 us (11%)
  between operations  0.92 us (2%)
    all_to_all x2, blocking collectives, body(): received = lax.all_to_all(payload, both, 0, 0, tiled=True)  25.7 us
    pallas_call x1, Pallas kernels, body(): pl.pallas_call(functools.partial(inner_kernel, count_y), out_shape=(pltpu...  4.06 us
    ppermute x1, starting transfers between devices, body(): near_message = lax.ppermute(near_message, 'gx', pairs(count_x, 0))  2.56 us
    pallas_call x2, Pallas kernels, edge(): pl.pallas_call(functools.partial(edge_kernel, count_x, count_y, is_near),...  1.9 us
    pallas_call x1, Pallas kernels, body(): pl.pallas_call(functools.partial(pack_kernel, starts), out_shape=(pltpu.V...  1.46 us
    pallas_call x1, Pallas kernels, body(): pl.pallas_call(functools.partial(first_kernel, count_x, count_y, load_row...  1.29 us
    pallas_call x1, Pallas kernels, body(): pl.pallas_call(functools.partial(prepare_kernel, slot_count, damper_padde...  1.15 us
  transfers between devices with their start and end apart: 6, of which 0 were waited for; matrix products, arithmetic and copies ran while one was open for 0% of the time, Pallas kernels for 17%

profile of v6, /device:TPU:0, one launch (start us, length us, event | category | flops | bytes accessed | tf_op | source)
XLA Modules:
  0.0 41.9 jit_solution(14524274935039183803)
XLA Ops:
  0.6 0.0 copy-start.3
  0.6 0.0 copy-start.8
  0.7 0.0 copy-start
  0.7 0.0 copy-start.1
  0.7 0.0 copy-start.12
  0.7 0.0 copy-start.9
  0.7 0.0 copy-start.10
  0.7 0.0 copy-start.4
  0.7 0.0 copy-start.11
  0.7 0.0 copy-start.2
  0.7 0.0 copy-start.7
  0.7 1.5 %pack.1 = (bf16[432,256]{1,0:T(8,128)(2,1)S(1)}, bf16[448,256]{1,0:T(8,128)(2,1)S(1)}, f32[5,8,8,256]{3,2,1,0:T(8,128)S(1)}, bf16[16,256]{1,0:T(8,128)(2,1)S(1)}) custom-call(f32[3,8,48,256]{3,2,1,0:T(8,128)} %vel.3, f32[8,48,256]{2,1,0:T(8,128)} %pre.3, f32[8,48,256]{2,1,0:T(8,128)} %vis.3), custom_call_target="tpu_custom_call" | custom-call | tf_op jit(solution)/shard_map/pack/pallas_call | solution.py:616
  2.2 0.5 %collective-permute-start = (f32[5,8,8,256]{3,2,1,0:T(8,128)S(1)}, f32[5,8,8,256]{3,2,1,0:T(8,128)S(1)}, u32[]{:S(2)}, u32[]{:S(2)}) collective-permute-start(f32[5,8,8,256]{3,2,1,0:T(8,128)S(1)} %get-tuple-element.48), channel_id=1, source_target_pairs={{0,1},{1,0},{2,3},{3,2},{4,5},{5,4},{6,7},{7,6},{8,9},{9,8},{10,11... | collective-permute-start | bytes 983048 | tf_op jit(solution)/shard_map/ppermute | solution.py:608
  2.7 2.6 %collective-permute-start.3 = (bf16[432,256]{1,0:T(8,128)(2,1)S(1)}, bf16[432,256]{1,0:T(8,128)(2,1)S(1)}, u32[]{:S(2)}, u32[]{:S(2)}) collective-permute-start(bf16[432,256]{1,0:T(8,128)(2,1)S(1)} %get-tuple-element.63), channel_id=1, source_target_pairs={{0,2},{4,6},{8,10},{12,14},{16,18},{20,22},{24,26},{28,30},{2,0},{... | collective-permute-start | bytes 663560 | tf_op jit(solution)/shard_map/ppermute | solution.py:631
  5.3 0.1 collective-permute-start.4
  5.4 0.0 collective-permute-done.left.right
  5.4 0.0 copy-done.8
  5.4 0.7 %collective-permute-start.1 = (bf16[448,256]{1,0:T(8,128)(2,1)S(1)}, bf16[448,256]{1,0:T(8,128)(2,1)S(1)}, u32[]{:S(2)}, u32[]{:S(2)}) collective-permute-start(bf16[448,256]{1,0:T(8,128)(2,1)S(1)} %corner.1), channel_id=1, source_target_pairs={{2,4},{6,8},{10,12},{14,16},{18,20},{22,24},{26,28},{4,2},{8,6},{1... | collective-permute-start | bytes 688136 | tf_op jit(solution)/shard_map/ppermute | solution.py:653
  6.1 0.0 copy-done
  6.1 0.2 collective-permute-start.5
  6.3 0.0 copy-done.9
  6.3 0.0 copy-done.10
  6.3 0.0 copy-done.11
  6.4 0.0 copy-done.12
  6.4 0.4 %collective-permute-start.2 = (f32[1,4608]{1,0:T(1,128)S(1)}, f32[1,4608]{1,0:T(1,128)S(1)}, u32[]{:S(2)}, u32[]{:S(2)}) collective-permute-start(f32[1,4608]{1,0:T(1,128)S(1)} %constant_dynamic-update-slice_fusion.refs_0_.refs_5_.refs_6_), channel_id=1, source_target_pairs={{1,0},{0,1},{3,2},{2,3},{5,4},{4,5},{7,6},{6,7},{9,8},{8,9},{11,10... | collective-permute-start | bytes 55304 | tf_op jit(solution)/shard_map/ppermute | solution.py:671
  6.8 0.0 copy-done.2
  6.8 4.1 %inner.1 = (f32[3,8,48,256]{3,2,1,0:T(8,128)S(1)}, f32[2,4,5,64,256]{4,3,2,1,0:T(8,128)S(1)}, f32[2,4,5,64,256]{4,3,2,1,0:T(8,128)S(1)}, f32[2,5,64,256]{3,2,1,0:T(8,128)S(1)}, f32[8,48,256]{2,1,0:T(8,128)S(1)}) custom-call(f32[3,8,48,256]{3,2,1,0:T(8,128)} %vel.3, f32[8,48,256]{2,1,0:T(8,128)} %pre.3, f32[8,48,256]{2,1,0:T(8,128)} %vis.3, ...), custom_call_target="tpu_custom_call" | custom-call | tf_op jit(solution)/shard_map/inner/pallas_call | solution.py:702
  10.9 0.0 collective-permute-done.2.refs_1_.refs_6_.refs_7_
  10.9 0.0 copy-done.3
  10.9 0.0 copy-done.1
  10.9 0.0 copy-done.4
  10.9 0.0 copy-done.7
  11.0 1.2 %prepare.1 = (bf16[2,2,128,128]{3,2,1,0:T(8,128)(2,1)S(1)}, f32[2,128]{1,0:T(2,128)S(1)}, bf16[2,256,96]{2,1,0:T(8,128)(2,1)S(1)}, f32[256,256]{1,0:T(8,128)S(1)...) custom-call(s32[1,256]{1,0:T(1,128)S(1)} %constant_dynamic-slice_fusion.own_ids, ...), custom_call_target="tpu_custom_call" | custom-call | tf_op jit(solution)/shard_map/prepare/pallas_call | solution.py:723
  12.1 0.0 collective-permute-done.4.refs_0_.refs_1_
  12.1 0.0 collective-permute-done.3.message
  12.1 1.0 %near.1 = (f32[3,8,48,256]{3,2,1,0:T(8,128)S(1)}, f32[8,48,256]{2,1,0:T(8,128)S(1)}, f32[256,256]{1,0:T(8,128)S(1)}, f32[2,4,5,64,256]{4,3,2,1,0:T(8,128)S(1)}, ...) custom-call(bf16[432,256]{1,0:T(8,128)(2,1)S(1)} %collective-permute, ...), custom_call_target="tpu_custom_call", output_to_operand_aliasing={{0}: (6, {}), {1}: (7, {}), {3}: (8, {}), {4}: (9, {}), {5}... | custom-call | tf_op jit(solution)/shard_map/near/pallas_call | solution.py:745
  13.1 0.0 collective-permute-done.1.message
  13.1 0.0 copy-start.5
  13.2 0.0 copy-start.6
  13.2 0.9 %far.1 = (f32[3,8,48,256]{3,2,1,0:T(8,128)S(1)}, f32[8,48,256]{2,1,0:T(8,128)S(1)}, f32[32,4,128]{2,1,0:T(4,128)S(1)}, f32[2,4,5,64,256]{4,3,2,1,0:T(8,128)S(1)}...) custom-call(bf16[448,256]{1,0:T(8,128)(2,1)S(1)} %collective-permute, ...), custom_call_target="tpu_custom_call", output_to_operand_aliasing={{0}: (6, {}), {1}: (7, {}), {3}: (8, {}), {4}: (9, {}), {5}... | custom-call | tf_op jit(solution)/shard_map/far/pallas_call | solution.py:745
  14.1 16.8 %all_to_all.10 = f32[32,4,128]{2,1,0:T(4,128)S(1)} all-to-all(f32[32,4,128]{2,1,0:T(4,128)S(1)} %get-tuple-element.78), channel_id=1, replica_groups=mesh['gx'=16,'gy'=2] {'gx','gy'}, dimensions={0} | all-to-all | bytes 131072 | tf_op jit(solution)/shard_map/all_to_all | solution.py:782
  30.9 0.0 collective-permute-done.5.refs_8_
  30.9 0.0 copy-done.5
  30.9 0.0 copy-done.6
  30.9 1.3 %first.1 = (f32[32,2,128]{2,1,0:T(2,128)S(1)}, f32[4,128]{1,0:T(4,128)S(1)}, f32[2,1,128]{2,1,0:T(1,128)S(1)}, f32[3,8,48,256]{3,2,1,0:T(8,128)}, f32[8,48,256]{2,1,0:T(8,128)}) custom-call(f32[16,2,4,128]{3,2,1,0:T(4,128)S(1)} %bitcast.15, bf16[2,2,128,128]{3,2,1,0:T(8,128)(2,1)S(1)} %get-tuple-element.79.refs_1_, f32[2,128]{1,0:T(2,128)S(1)} %copy-done.4, ...), custom_call_target="tpu_custom_call" | custom-call | tf_op jit(solution)/shard_map/first/pallas_call | solution.py:787
  32.2 8.9 %all_to_all.11 = f32[32,2,128]{2,1,0:T(2,128)S(1)} all-to-all(f32[32,2,128]{2,1,0:T(2,128)S(1)} %get-tuple-element.87), channel_id=1, replica_groups=mesh['gx'=16,'gy'=2] {'gx','gy'}, dimensions={0} | all-to-all | bytes 65536 | tf_op jit(solution)/shard_map/all_to_all | solution.py:805
  41.1 0.8 %second.1 = (f32[2,128]{1,0:T(2,128)}, f32[1,64]{1,0:T(1,128)}) custom-call(f32[16,2,2,128]{3,2,1,0:T(2,128)S(1)} %bitcast.16, bf16[2,2,128,128]{3,2,1,0:T(8,128)(2,1)S(1)} %get-tuple-element.79.refs_1_, f32[1,128]{1,0:T(1,128)S(1)} %bitcast.22, f32[1,128]{1,0:T(1,128)S(1)} %bitcast.24, f32[4,128]{1,0:T(4,128)S(1)} %get-tuple-element.88.refs_4_, ...), custom_call_target="tpu_custom_call" | custom-call | tf_op jit(solution)/shard_map/second/pallas_call | solution.py:808
  (8 shorter events, 0.1 us)
Async XLA Ops:
  0.6 10.3 %copy-start.3 = (f32[2048]{0:T(1024)S(1)}, f32[2048]{0:T(1024)}, u32[]{:S(2)}) copy-start(f32[2048]{0:T(1024)} %param.20) | copy-start | bytes 24580
  0.6 4.7 %copy-start.8 = (s32[1,4096]{1,0:T(1,128)S(1)}, s32[1,4096]{1,0:T(1,128)}, u32[]{:S(2)}) copy-start(s32[1,4096]{1,0:T(1,128)} %param.22) | copy-start | bytes 49156
  0.7 5.5 %copy-start = (bf16[2048,128]{1,0:T(8,128)(2,1)S(1)}, bf16[2048,128]{1,0:T(8,128)(2,1)}, u32[]{:S(2)}) copy-start(bf16[2048,128]{1,0:T(8,128)(2,1)} %refs_7_) | copy-start | bytes 1572868
  0.7 10.3 %copy-start.1 = (bf16[1024,128]{1,0:T(8,128)(2,1)S(1)}, bf16[1024,128]{1,0:T(8,128)(2,1)}, u32[]{:S(2)}) copy-start(bf16[1024,128]{1,0:T(8,128)(2,1)} %nodes) | copy-start | bytes 786436
  0.7 5.7 %copy-start.12 = (s32[64]{0:T(128)S(1)}, s32[64]{0:T(128)}, u32[]{:S(2)}) copy-start(s32[64]{0:T(128)} %param.25) | copy-start | bytes 772
  0.7 5.6 %copy-start.9 = (f32[64]{0:T(128)S(1)}, f32[64]{0:T(128)}, u32[]{:S(2)}) copy-start(f32[64]{0:T(128)} %param.26) | copy-start | bytes 772
  0.7 5.6 %copy-start.10 = (f32[64]{0:T(128)S(1)}, f32[64]{0:T(128)}, u32[]{:S(2)}) copy-start(f32[64]{0:T(128)} %param.27) | copy-start | bytes 772
  0.7 10.2 %copy-start.4 = (f32[2,128]{1,0:T(2,128)S(1)}, f32[2,128]{1,0:T(2,128)}, u32[]{:S(2)}) copy-start(f32[2,128]{1,0:T(2,128)} %refs_2_) | copy-start | bytes 3076
  0.7 5.6 %copy-start.11 = (f32[64]{0:T(128)S(1)}, f32[64]{0:T(128)}, u32[]{:S(2)}) copy-start(f32[64]{0:T(128)} %param.31) | copy-start | bytes 772
  0.7 6.1 %copy-start.2 = (f32[256]{0:T(256)S(1)}, f32[256]{0:T(256)}, u32[]{:S(2)}) copy-start(f32[256]{0:T(256)} %param.19) | copy-start | bytes 3076
  0.7 10.2 %copy-start.7 = (s32[1,256]{1,0:T(1,128)S(1)}, s32[1,256]{1,0:T(1,128)}, u32[]{:S(2)}) copy-start(s32[1,256]{1,0:T(1,128)} %cell.1) | copy-start | bytes 3076
  2.2 3.2 %collective-permute-start = (f32[5,8,8,256]{3,2,1,0:T(8,128)S(1)}, f32[5,8,8,256]{3,2,1,0:T(8,128)S(1)}, u32[]{:S(2)}, u32[]{:S(2)}) collective-permute-start(f32[5,8,8,256]{3,2,1,0:T(8,128)S(1)} %get-tuple-element.48), channel_id=1, source_target_pairs={{0,1},{1,0},{2,3},{3,2},{4,5},{5,4},{6,7},{7,6},{8,9},{9,8},{10,11... | collective-permute-start | bytes 983048 | tf_op jit(solution)/shard_map/ppermute | solution.py:608
  2.7 9.4 %collective-permute-start.3 = (bf16[432,256]{1,0:T(8,128)(2,1)S(1)}, bf16[432,256]{1,0:T(8,128)(2,1)S(1)}, u32[]{:S(2)}, u32[]{:S(2)}) collective-permute-start(bf16[432,256]{1,0:T(8,128)(2,1)S(1)} %get-tuple-element.63), channel_id=1, source_target_pairs={{0,2},{4,6},{8,10},{12,14},{16,18},{20,22},{24,26},{28,30},{2,0},{... | collective-permute-start | bytes 663560 | tf_op jit(solution)/shard_map/ppermute | solution.py:631
  5.3 6.8 %collective-permute-start.4 = (bf16[16,256]{1,0:T(8,128)(2,1)S(1)}, bf16[16,256]{1,0:T(8,128)(2,1)S(1)}, u32[]{:S(2)}, u32[]{:S(2)}) collective-permute-start(bf16[16,256]{1,0:T(8,128)(2,1)S(1)} %get-tuple-element.64), channel_id=1, source_target_pairs={{0,3},{4,7},{8,11},{12,15},{16,19},{20,23},{24,27},{28,31},{2,1},{... | collective-permute-start | bytes 24584 | tf_op jit(solution)/shard_map/ppermute | solution.py:664
  5.4 7.7 %collective-permute-start.1 = (bf16[448,256]{1,0:T(8,128)(2,1)S(1)}, bf16[448,256]{1,0:T(8,128)(2,1)S(1)}, u32[]{:S(2)}, u32[]{:S(2)}) collective-permute-start(bf16[448,256]{1,0:T(8,128)(2,1)S(1)} %corner.1), channel_id=1, source_target_pairs={{2,4},{6,8},{10,12},{14,16},{18,20},{22,24},{26,28},{4,2},{8,6},{1... | collective-permute-start | bytes 688136 | tf_op jit(solution)/shard_map/ppermute | solution.py:653
  6.1 24.7 %collective-permute-start.5 = (bf16[2048,128]{1,0:T(8,128)(2,1)S(1)}, bf16[2048,128]{1,0:T(8,128)(2,1)S(1)}, u32[]{:S(2)}, u32[]{:S(2)}) collective-permute-start(bf16[2048,128]{1,0:T(8,128)(2,1)S(1)} %copy-done), channel_id=1, source_target_pairs={{1,0},{0,1},{3,2},{2,3},{5,4},{4,5},{7,6},{6,7},{9,8},{8,9},{11,10... | collective-permute-start | bytes 1572872 | tf_op jit(solution)/shard_map/ppermute | solution.py:671
  6.4 4.5 %collective-permute-start.2 = (f32[1,4608]{1,0:T(1,128)S(1)}, f32[1,4608]{1,0:T(1,128)S(1)}, u32[]{:S(2)}, u32[]{:S(2)}) collective-permute-start(f32[1,4608]{1,0:T(1,128)S(1)} %constant_dynamic-update-slice_fusion.refs_0_.refs_5_.refs_6_), channel_id=1, source_target_pairs={{1,0},{0,1},{3,2},{2,3},{5,4},{4,5},{7,6},{6,7},{9,8},{8,9},{11,10... | collective-permute-start | bytes 55304 | tf_op jit(solution)/shard_map/ppermute | solution.py:671
  13.1 17.7 %copy-start.5 = (f32[128]{0:T(128)S(1)}, f32[128]{0:T(128)}, u32[]{:S(2)}) copy-start(f32[128]{0:T(128)} %param.28) | copy-start | bytes 1540
  13.2 17.7 %copy-start.6 = (f32[128]{0:T(128)S(1)}, f32[128]{0:T(128)}, u32[]{:S(2)}) copy-start(f32[128]{0:T(128)} %param.29) | copy-start | bytes 1540

commit v7 on v6

--- a/solution.py
+++ b/solution.py
@@ -187,8 +187,12 @@
 
     step = stepper(wind, height)
 
-    def advance(source, layer, row, edge=0):
+    nothing = jnp.zeros((8, height), f32)
+
+    def advance(source, layer, row, edge=0, missing=0):
         def get(f, offset, low):
+            if missing and offset == missing:
+                return nothing
             return source[f, layer + offset, pl.ds(low, 8), :]
 
         return step(get, visc[layer, pl.ds(row, 8), :], row, edge)
@@ -223,15 +227,38 @@
                 vel_out[i, layer, row - PAD : row - PAD + 8, :] = result[i]
             pre_out[layer, row - PAD : row - PAD + 8, :] = result[3]
 
-    for side, first_old, place_old, first_mid, place_mid in (
-        (0, 0, 2, 1, 3),
-        (1, layers - 2, 1, layers - 3, 0),
+    for side, own, inside, place, missing in (
+        (0, 0, 1, 3, -1),
+        (1, layers - 1, layers - 2, 1, 1),
     ):
-        for depth in range(2):
-            visc_edge[side, place_old + depth] = visc[first_old + depth]
+
+        def begin(row, edge, side=side, own=own, missing=missing):
+            result = advance(old, own, row, edge, missing)
             for f in range(4):
-                old_edge[side, f, place_old + depth] = old[f, first_old + depth]
-                mid_edge[side, f, place_mid + depth] = mid[f, first_mid + depth]
+                mid_edge[side, f, 2, row : row + 8, :] = result[f]
+
+        for row in range(PAD, last, 8):
+            begin(row, 0)
+            result = advance(mid, inside, row, 0, missing)
+            here = slice(row - PAD, row - PAD + 8)
+            for i in range(3):
+                vel_out[i, inside, here, :] = result[i]
+            pre_out[inside, here, :] = result[3]
+        for there, row, edge in ((has_left, 0, -1), (has_right, last, 1)):
+
+            @pl.when(there)
+            def _(begin=begin, row=row, edge=edge):
+                begin(row, edge)
+
+            @pl.when(jnp.logical_not(there))
+            def _(side=side, row=row):
+                mid_edge[side, :, 2, row : row + PAD, :] = jnp.zeros((4, PAD, height), f32)
+
+        visc_edge[side, 2] = visc[own]
+        visc_edge[side, place] = visc[inside]
+        for f in range(4):
+            old_edge[side, f, 2] = old[f, own]
+            mid_edge[side, f, place] = mid[f, inside]
 
 
 def edge_kernel(count_x, count_y, is_near, message, *refs):
@@ -277,48 +304,48 @@
 
         return step(get, visc[side, layer, pl.ds(row, 8), :], row, edge)
 
-    def first(layer, row, edge=0):
+    def first(layer, row, edge=0, keep=None):
         result = advance(old, layer, row, edge)
         for f in range(4):
-            mid[side, f, layer, pl.ds(row, 8), :] = result[f]
-
-    blank = jnp.zeros((4, PAD, height), f32)
+            value = result[f] if keep is None else jnp.where(keep, result[f], 0.0)
+            mid[side, f, layer, pl.ds(row, 8), :] = value
+
+    sign = 1.0 - 2.0 * side.astype(f32)
+    windy = jnp.broadcast_to(wind[...] * (0.5 * time_step), (8, height)) * sign
+    pull = sign * (0.5 * time_step)
+
+    def light(source, layer, other, row, write):
+        here = pl.ds(row, 8)
+        o = [source[side, f, other, here, :] for f in range(4)]
+        c = visc[side, layer, here, :] * time_step + windy
+        write(0, c * o[0] + pull * o[3])
+        write(1, c * o[1])
+        write(2, c * o[2])
+        write(3, pull * o[0])
+
+    for row in range(0, last + PAD, 8):
+        def write(f, value, row=row):
+            mid[side, f, 2, pl.ds(row, 8), :] += value
+        light(old, 2, outside, row, write)
     for row in range(PAD, last, 8):
-        first(2, row)
-
-    @pl.when(has_left)
-    def _():
-        first(2, 0, -1)
-
-    @pl.when(jnp.logical_not(has_left))
-    def _():
-        mid[side, :, 2, 0:PAD, :] = blank
-
-    @pl.when(has_right)
-    def _():
-        first(2, last, 1)
-
-    @pl.when(jnp.logical_not(has_right))
-    def _():
-        mid[side, :, 2, last : last + PAD, :] = blank
-
-    @pl.when(there)
-    def _():
-        for row in range(PAD, last, 8):
-            first(outside, row)
-
-    @pl.when(jnp.logical_not(there))
-    def _():
-        mid[side, :, outside, PAD:last, :] = jnp.zeros((4, rows, height), f32)
+        first(outside, row, 0, there)
 
     for row in range(PAD, last, 8):
-        for layer, place in ((2, side), (3 - 2 * side, 1 - side)):
-            result = advance(mid, layer, row)
-            here = pl.ds(row - PAD, 8)
-            target = side * (layers - 2) + place
-            for i in range(3):
-                vel_out[i, target, here, :] = result[i]
-            pre_out[target, here, :] = result[3]
+        result = advance(mid, 2, row)
+        here = pl.ds(row - PAD, 8)
+        target = side * (layers - 1)
+        for i in range(3):
+            vel_out[i, target, here, :] = result[i]
+        pre_out[target, here, :] = result[3]
+        target = 1 + side * (layers - 3)
+
+        def write(f, value, here=here, target=target):
+            if f < 3:
+                vel_out[f, target, here, :] += value
+            else:
+                pre_out[target, here, :] += value
+
+        light(mid, 3 - 2 * side, 2, row, write)
 
     flat = pre_out[pl.ds(side * (layers - 2), 2)].reshape(2 * rows, height)
     total = found[...]

time: 42.1 us -> 41.8 us (level)
  blocking collectives: 25.7 us -> 25.1 us
    pallas_call x1, Pallas kernels: 4.06 us -> 4.79 us  [body(): pl.pallas_call(functools.partial(inner_kernel, count_y), out_shape=(pltpu...]
    all_to_all x2, blocking collectives: 25.7 us -> 25.1 us  [body(): received = lax.all_to_all(payload, both, 0, 0, tiled=True)]
    pallas_call x2, Pallas kernels: 1.9 us -> 1.45 us  [edge(): pl.pallas_call(functools.partial(edge_kernel, count_x, count_y, is_near),...]
  transfers between devices with their start and end apart: 6 -> 6, of which waited for: 0 -> 0; matrix products, arithmetic and copies ran while one was open for 0% -> 0% of each run, Pallas kernels for 17% -> 18%
where the time goes in v7:
time: 41.8 us; the launch traced here: 41.5 us
  blocking collectives  25.1 us (60%)
  Pallas kernels  10.9 us (26%)
  starting transfers between devices  4.47 us (11%)
  between operations  0.92 us (2%)
    all_to_all x2, blocking collectives, body(): received = lax.all_to_all(payload, both, 0, 0, tiled=True)  25.1 us
    pallas_call x1, Pallas kernels, body(): pl.pallas_call(functools.partial(inner_kernel, count_y), out_shape=(pltpu...  4.79 us
    ppermute x1, starting transfers between devices, body(): near_message = lax.ppermute(near_message, 'gx', pairs(count_x, 0))  2.56 us
    pallas_call x1, Pallas kernels, body(): pl.pallas_call(functools.partial(pack_kernel, starts), out_shape=(pltpu.V...  1.46 us
    pallas_call x2, Pallas kernels, edge(): pl.pallas_call(functools.partial(edge_kernel, count_x, count_y, is_near),...  1.45 us
    pallas_call x1, Pallas kernels, body(): pl.pallas_call(functools.partial(first_kernel, count_x, count_y, load_row...  1.29 us
    pallas_call x1, Pallas kernels, body(): pl.pallas_call(functools.partial(prepare_kernel, slot_count, damper_padde...  1.16 us
  transfers between devices with their start and end apart: 6, of which 0 were waited for; matrix products, arithmetic and copies ran while one was open for 0% of the time, Pallas kernels for 18%

profile of v7, /device:TPU:0, one launch (start us, length us, event | category | flops | bytes accessed | tf_op | source)
XLA Modules:
  0.0 41.5 jit_solution(5433388567543192959)
XLA Ops:
  0.6 0.0 copy-start.3
  0.6 0.0 copy-start.8
  0.7 0.0 copy-start
  0.7 0.0 copy-start.1
  0.7 0.0 copy-start.12
  0.7 0.0 copy-start.9
  0.7 0.0 copy-start.10
  0.7 0.0 copy-start.4
  0.7 0.0 copy-start.11
  0.7 0.0 copy-start.2
  0.7 0.0 copy-start.7
  0.7 1.5 %pack.1 = (bf16[432,256]{1,0:T(8,128)(2,1)S(1)}, bf16[448,256]{1,0:T(8,128)(2,1)S(1)}, f32[5,8,8,256]{3,2,1,0:T(8,128)S(1)}, bf16[16,256]{1,0:T(8,128)(2,1)S(1)}) custom-call(f32[3,8,48,256]{3,2,1,0:T(8,128)} %vel.3, f32[8,48,256]{2,1,0:T(8,128)} %pre.3, f32[8,48,256]{2,1,0:T(8,128)} %vis.3), custom_call_target="tpu_custom_call" | custom-call | tf_op jit(solution)/shard_map/pack/pallas_call | solution.py:643
  2.2 0.5 %collective-permute-start = (f32[5,8,8,256]{3,2,1,0:T(8,128)S(1)}, f32[5,8,8,256]{3,2,1,0:T(8,128)S(1)}, u32[]{:S(2)}, u32[]{:S(2)}) collective-permute-start(f32[5,8,8,256]{3,2,1,0:T(8,128)S(1)} %get-tuple-element.48), channel_id=1, source_target_pairs={{0,1},{1,0},{2,3},{3,2},{4,5},{5,4},{6,7},{7,6},{8,9},{9,8},{10,11... | collective-permute-start | bytes 983048 | tf_op jit(solution)/shard_map/ppermute | solution.py:635
  2.7 2.6 %collective-permute-start.3 = (bf16[432,256]{1,0:T(8,128)(2,1)S(1)}, bf16[432,256]{1,0:T(8,128)(2,1)S(1)}, u32[]{:S(2)}, u32[]{:S(2)}) collective-permute-start(bf16[432,256]{1,0:T(8,128)(2,1)S(1)} %get-tuple-element.63), channel_id=1, source_target_pairs={{0,2},{4,6},{8,10},{12,14},{16,18},{20,22},{24,26},{28,30},{2,0},{... | collective-permute-start | bytes 663560 | tf_op jit(solution)/shard_map/ppermute | solution.py:658
  5.3 0.1 collective-permute-start.4
  5.4 0.0 collective-permute-done.left.right
  5.4 0.0 copy-done.8
  5.4 0.7 %collective-permute-start.1 = (bf16[448,256]{1,0:T(8,128)(2,1)S(1)}, bf16[448,256]{1,0:T(8,128)(2,1)S(1)}, u32[]{:S(2)}, u32[]{:S(2)}) collective-permute-start(bf16[448,256]{1,0:T(8,128)(2,1)S(1)} %corner.1), channel_id=1, source_target_pairs={{2,4},{6,8},{10,12},{14,16},{18,20},{22,24},{26,28},{4,2},{8,6},{1... | collective-permute-start | bytes 688136 | tf_op jit(solution)/shard_map/ppermute | solution.py:680
  6.1 0.0 copy-done
  6.1 0.2 collective-permute-start.5
  6.3 0.0 copy-done.9
  6.3 0.0 copy-done.10
  6.3 0.0 copy-done.11
  6.4 0.0 copy-done.12
  6.4 0.4 %collective-permute-start.2 = (f32[1,4608]{1,0:T(1,128)S(1)}, f32[1,4608]{1,0:T(1,128)S(1)}, u32[]{:S(2)}, u32[]{:S(2)}) collective-permute-start(f32[1,4608]{1,0:T(1,128)S(1)} %constant_dynamic-update-slice_fusion.refs_0_.refs_5_.refs_6_), channel_id=1, source_target_pairs={{1,0},{0,1},{3,2},{2,3},{5,4},{4,5},{7,6},{6,7},{9,8},{8,9},{11,10... | collective-permute-start | bytes 55304 | tf_op jit(solution)/shard_map/ppermute | solution.py:698
  6.8 0.0 copy-done.2
  6.8 4.8 %inner.1 = (f32[3,8,48,256]{3,2,1,0:T(8,128)S(1)}, f32[2,4,5,64,256]{4,3,2,1,0:T(8,128)S(1)}, f32[2,4,5,64,256]{4,3,2,1,0:T(8,128)S(1)}, f32[2,5,64,256]{3,2,1,0:T(8,128)S(1)}, f32[8,48,256]{2,1,0:T(8,128)S(1)}) custom-call(f32[3,8,48,256]{3,2,1,0:T(8,128)} %vel.3, f32[8,48,256]{2,1,0:T(8,128)} %pre.3, f32[8,48,256]{2,1,0:T(8,128)} %vis.3, ...), custom_call_target="tpu_custom_call" | custom-call | tf_op jit(solution)/shard_map/inner/pallas_call | solution.py:729
  11.6 0.0 collective-permute-done.2.refs_1_.refs_6_.refs_7_
  11.7 0.0 copy-done.3
  11.7 0.0 copy-done.1
  11.7 0.0 copy-done.4
  11.7 0.0 copy-done.7
  11.7 1.2 %prepare.1 = (bf16[2,2,128,128]{3,2,1,0:T(8,128)(2,1)S(1)}, f32[2,128]{1,0:T(2,128)S(1)}, bf16[2,256,96]{2,1,0:T(8,128)(2,1)S(1)}, f32[256,256]{1,0:T(8,128)S(1)...) custom-call(s32[1,256]{1,0:T(1,128)S(1)} %constant_dynamic-slice_fusion.own_ids, ...), custom_call_target="tpu_custom_call" | custom-call | tf_op jit(solution)/shard_map/prepare/pallas_call | solution.py:750
  12.9 0.0 collective-permute-done.4.refs_0_.refs_1_
  12.9 0.0 collective-permute-done.3.message
  12.9 0.7 %near.1 = (f32[3,8,48,256]{3,2,1,0:T(8,128)S(1)}, f32[8,48,256]{2,1,0:T(8,128)S(1)}, f32[256,256]{1,0:T(8,128)S(1)}, f32[2,4,5,64,256]{4,3,2,1,0:T(8,128)S(1)}, ...) custom-call(bf16[432,256]{1,0:T(8,128)(2,1)S(1)} %collective-permute, ...), custom_call_target="tpu_custom_call", output_to_operand_aliasing={{0}: (6, {}), {1}: (7, {}), {3}: (8, {}), {4}: (9, {}), {5}... | custom-call | tf_op jit(solution)/shard_map/near/pallas_call | solution.py:772
  13.6 0.0 collective-permute-done.1.message
  13.6 0.0 copy-start.5
  13.6 0.0 copy-start.6
  13.6 0.8 %far.1 = (f32[3,8,48,256]{3,2,1,0:T(8,128)S(1)}, f32[8,48,256]{2,1,0:T(8,128)S(1)}, f32[32,4,128]{2,1,0:T(4,128)S(1)}, f32[2,4,5,64,256]{4,3,2,1,0:T(8,128)S(1)}...) custom-call(bf16[448,256]{1,0:T(8,128)(2,1)S(1)} %collective-permute, ...), custom_call_target="tpu_custom_call", output_to_operand_aliasing={{0}: (6, {}), {1}: (7, {}), {3}: (8, {}), {4}: (9, {}), {5}... | custom-call | tf_op jit(solution)/shard_map/far/pallas_call | solution.py:772
  14.4 16.1 %all_to_all.10 = f32[32,4,128]{2,1,0:T(4,128)S(1)} all-to-all(f32[32,4,128]{2,1,0:T(4,128)S(1)} %get-tuple-element.78), channel_id=1, replica_groups=mesh['gx'=16,'gy'=2] {'gx','gy'}, dimensions={0} | all-to-all | bytes 131072 | tf_op jit(solution)/shard_map/all_to_all | solution.py:809
  30.5 0.0 collective-permute-done.5.refs_8_
  30.5 0.0 copy-done.5
  30.5 0.0 copy-done.6
  30.5 1.3 %first.1 = (f32[32,2,128]{2,1,0:T(2,128)S(1)}, f32[4,128]{1,0:T(4,128)S(1)}, f32[2,1,128]{2,1,0:T(1,128)S(1)}, f32[3,8,48,256]{3,2,1,0:T(8,128)}, f32[8,48,256]{2,1,0:T(8,128)}) custom-call(f32[16,2,4,128]{3,2,1,0:T(4,128)S(1)} %bitcast.15, bf16[2,2,128,128]{3,2,1,0:T(8,128)(2,1)S(1)} %get-tuple-element.79.refs_1_, f32[2,128]{1,0:T(2,128)S(1)} %copy-done.4, ...), custom_call_target="tpu_custom_call" | custom-call | tf_op jit(solution)/shard_map/first/pallas_call | solution.py:814
  31.8 8.9 %all_to_all.11 = f32[32,2,128]{2,1,0:T(2,128)S(1)} all-to-all(f32[32,2,128]{2,1,0:T(2,128)S(1)} %get-tuple-element.87), channel_id=1, replica_groups=mesh['gx'=16,'gy'=2] {'gx','gy'}, dimensions={0} | all-to-all | bytes 65536 | tf_op jit(solution)/shard_map/all_to_all | solution.py:832
  40.8 0.8 %second.1 = (f32[2,128]{1,0:T(2,128)}, f32[1,64]{1,0:T(1,128)}) custom-call(f32[16,2,2,128]{3,2,1,0:T(2,128)S(1)} %bitcast.16, bf16[2,2,128,128]{3,2,1,0:T(8,128)(2,1)S(1)} %get-tuple-element.79.refs_1_, f32[1,128]{1,0:T(1,128)S(1)} %bitcast.22, f32[1,128]{1,0:T(1,128)S(1)} %bitcast.24, f32[4,128]{1,0:T(4,128)S(1)} %get-tuple-element.88.refs_4_, ...), custom_call_target="tpu_custom_call" | custom-call | tf_op jit(solution)/shard_map/second/pallas_call | solution.py:835
  (8 shorter events, 0.1 us)
Async XLA Ops:
  0.6 11.0 %copy-start.3 = (f32[2048]{0:T(1024)S(1)}, f32[2048]{0:T(1024)}, u32[]{:S(2)}) copy-start(f32[2048]{0:T(1024)} %param.20) | copy-start | bytes 24580
  0.6 4.7 %copy-start.8 = (s32[1,4096]{1,0:T(1,128)S(1)}, s32[1,4096]{1,0:T(1,128)}, u32[]{:S(2)}) copy-start(s32[1,4096]{1,0:T(1,128)} %param.22) | copy-start | bytes 49156
  0.7 5.5 %copy-start = (bf16[2048,128]{1,0:T(8,128)(2,1)S(1)}, bf16[2048,128]{1,0:T(8,128)(2,1)}, u32[]{:S(2)}) copy-start(bf16[2048,128]{1,0:T(8,128)(2,1)} %refs_7_) | copy-start | bytes 1572868
  0.7 11.0 %copy-start.1 = (bf16[1024,128]{1,0:T(8,128)(2,1)S(1)}, bf16[1024,128]{1,0:T(8,128)(2,1)}, u32[]{:S(2)}) copy-start(bf16[1024,128]{1,0:T(8,128)(2,1)} %nodes) | copy-start | bytes 786436
  0.7 5.7 %copy-start.12 = (s32[64]{0:T(128)S(1)}, s32[64]{0:T(128)}, u32[]{:S(2)}) copy-start(s32[64]{0:T(128)} %param.25) | copy-start | bytes 772
  0.7 5.6 %copy-start.9 = (f32[64]{0:T(128)S(1)}, f32[64]{0:T(128)}, u32[]{:S(2)}) copy-start(f32[64]{0:T(128)} %param.26) | copy-start | bytes 772
  0.7 5.6 %copy-start.10 = (f32[64]{0:T(128)S(1)}, f32[64]{0:T(128)}, u32[]{:S(2)}) copy-start(f32[64]{0:T(128)} %param.27) | copy-start | bytes 772
  0.7 11.0 %copy-start.4 = (f32[2,128]{1,0:T(2,128)S(1)}, f32[2,128]{1,0:T(2,128)}, u32[]{:S(2)}) copy-start(f32[2,128]{1,0:T(2,128)} %refs_2_) | copy-start | bytes 3076
  0.7 5.6 %copy-start.11 = (f32[64]{0:T(128)S(1)}, f32[64]{0:T(128)}, u32[]{:S(2)}) copy-start(f32[64]{0:T(128)} %param.31) | copy-start | bytes 772
  0.7 6.1 %copy-start.2 = (f32[256]{0:T(256)S(1)}, f32[256]{0:T(256)}, u32[]{:S(2)}) copy-start(f32[256]{0:T(256)} %param.19) | copy-start | bytes 3076
  0.7 11.0 %copy-start.7 = (s32[1,256]{1,0:T(1,128)S(1)}, s32[1,256]{1,0:T(1,128)}, u32[]{:S(2)}) copy-start(s32[1,256]{1,0:T(1,128)} %cell.1) | copy-start | bytes 3076
  2.2 3.2 %collective-permute-start = (f32[5,8,8,256]{3,2,1,0:T(8,128)S(1)}, f32[5,8,8,256]{3,2,1,0:T(8,128)S(1)}, u32[]{:S(2)}, u32[]{:S(2)}) collective-permute-start(f32[5,8,8,256]{3,2,1,0:T(8,128)S(1)} %get-tuple-element.48), channel_id=1, source_target_pairs={{0,1},{1,0},{2,3},{3,2},{4,5},{5,4},{6,7},{7,6},{8,9},{9,8},{10,11... | collective-permute-start | bytes 983048 | tf_op jit(solution)/shard_map/ppermute | solution.py:635
  2.7 10.1 %collective-permute-start.3 = (bf16[432,256]{1,0:T(8,128)(2,1)S(1)}, bf16[432,256]{1,0:T(8,128)(2,1)S(1)}, u32[]{:S(2)}, u32[]{:S(2)}) collective-permute-start(bf16[432,256]{1,0:T(8,128)(2,1)S(1)} %get-tuple-element.63), channel_id=1, source_target_pairs={{0,2},{4,6},{8,10},{12,14},{16,18},{20,22},{24,26},{28,30},{2,0},{... | collective-permute-start | bytes 663560 | tf_op jit(solution)/shard_map/ppermute | solution.py:658
  5.3 7.6 %collective-permute-start.4 = (bf16[16,256]{1,0:T(8,128)(2,1)S(1)}, bf16[16,256]{1,0:T(8,128)(2,1)S(1)}, u32[]{:S(2)}, u32[]{:S(2)}) collective-permute-start(bf16[16,256]{1,0:T(8,128)(2,1)S(1)} %get-tuple-element.64), channel_id=1, source_target_pairs={{0,3},{4,7},{8,11},{12,15},{16,19},{20,23},{24,27},{28,31},{2,1},{... | collective-permute-start | bytes 24584 | tf_op jit(solution)/shard_map/ppermute | solution.py:691
  5.4 8.1 %collective-permute-start.1 = (bf16[448,256]{1,0:T(8,128)(2,1)S(1)}, bf16[448,256]{1,0:T(8,128)(2,1)S(1)}, u32[]{:S(2)}, u32[]{:S(2)}) collective-permute-start(bf16[448,256]{1,0:T(8,128)(2,1)S(1)} %corner.1), channel_id=1, source_target_pairs={{2,4},{6,8},{10,12},{14,16},{18,20},{22,24},{26,28},{4,2},{8,6},{1... | collective-permute-start | bytes 688136 | tf_op jit(solution)/shard_map/ppermute | solution.py:680
  6.1 24.4 %collective-permute-start.5 = (bf16[2048,128]{1,0:T(8,128)(2,1)S(1)}, bf16[2048,128]{1,0:T(8,128)(2,1)S(1)}, u32[]{:S(2)}, u32[]{:S(2)}) collective-permute-start(bf16[2048,128]{1,0:T(8,128)(2,1)S(1)} %copy-done), channel_id=1, source_target_pairs={{1,0},{0,1},{3,2},{2,3},{5,4},{4,5},{7,6},{6,7},{9,8},{8,9},{11,10... | collective-permute-start | bytes 1572872 | tf_op jit(solution)/shard_map/ppermute | solution.py:698
  6.4 5.2 %collective-permute-start.2 = (f32[1,4608]{1,0:T(1,128)S(1)}, f32[1,4608]{1,0:T(1,128)S(1)}, u32[]{:S(2)}, u32[]{:S(2)}) collective-permute-start(f32[1,4608]{1,0:T(1,128)S(1)} %constant_dynamic-update-slice_fusion.refs_0_.refs_5_.refs_6_), channel_id=1, source_target_pairs={{1,0},{0,1},{3,2},{2,3},{5,4},{4,5},{7,6},{6,7},{9,8},{8,9},{11,10... | collective-permute-start | bytes 55304 | tf_op jit(solution)/shard_map/ppermute | solution.py:698
  13.6 17.0 %copy-start.5 = (f32[128]{0:T(128)S(1)}, f32[128]{0:T(128)}, u32[]{:S(2)}) copy-start(f32[128]{0:T(128)} %param.28) | copy-start | bytes 1540
  13.6 16.9 %copy-start.6 = (f32[128]{0:T(128)S(1)}, f32[128]{0:T(128)}, u32[]{:S(2)}) copy-start(f32[128]{0:T(128)} %param.29) | copy-start | bytes 1540

commit v8 on v7

--- a/solution.py
+++ b/solution.py
@@ -261,7 +261,7 @@
             mid_edge[side, f, place] = mid[f, inside]
 
 
-def edge_kernel(count_x, count_y, is_near, message, *refs):
+def edge_kernel(count_x, count_y, damper_count, is_near, message, *refs):
     if is_near:
         left_lines, right_lines = refs[:2]
         wind, pick, found = refs[2:5]
@@ -363,7 +363,9 @@
     for start in range(0, slots, LANES):
         chosen = jnp.where(same, loads[start : start + LANES], 0.0)
         lines.append(jnp.sum(chosen, axis=0, keepdims=True))
-    message = jnp.concatenate(lines + [partial[...]], axis=0)
+    pair = folded(partial[...], damper_count)
+    high = pair.astype(bf16).astype(f32)
+    message = jnp.concatenate(lines + [high, pair - high], axis=0).astype(bf16)
     payload[...] = jnp.broadcast_to(message[None], payload.shape)
 
 
@@ -437,6 +439,21 @@
     partial[...] = drift_times(state[0:1], state[1:2], shapes)
 
 
+def folded(pair, count):
+    width = pair.shape[1]
+    if 2 * count > width:
+        return pair
+    return pair[0:1] + pltpu.roll(pair[1:2], count, 1)
+
+
+def unfolded(rows, count):
+    width = rows.shape[1]
+    if 2 * count > width:
+        return rows[0:1], rows[1:2]
+    low = lax.broadcasted_iota(jnp.int32, rows.shape, 1) < count
+    return jnp.where(low, rows, 0.0), jnp.where(low, pltpu.roll(rows, width - count, 1), 0.0)
+
+
 def respond(stretch, rate, hysteresis, viscous, hysteretic):
     hysteresis = hysteresis + modal_step * (
         rate
@@ -489,12 +506,12 @@
     return [small[:, slot_count + k * width : slot_count + (k + 1) * width] for k in range(3)]
 
 
-def first_kernel(count_x, count_y, load_rows, *refs):
-    received, shapes, modal, frequency, ratio = refs[:5]
+def first_kernel(count_x, count_y, load_rows, damper_count, *refs):
+    arrived, shapes, modal, frequency, ratio = refs[:5]
     smalls = refs[5 : 5 + count_y]
     tables = refs[5 + count_y : 5 + 2 * count_y]
     spreads = refs[5 + 2 * count_y : 5 + 3 * count_y]
-    vel, pre, payload, state, hysteresis_out, vel_out, pre_out, sem = refs[5 + 3 * count_y :]
+    vel, pre, payload, state, hysteresis_out, vel_out, pre_out, received, sem = refs[5 + 3 * count_y :]
     writes = [
         pltpu.make_async_copy(vel, vel_out, sem.at[0]),
         pltpu.make_async_copy(pre, pre_out, sem.at[1]),
@@ -502,6 +519,8 @@
     for write in writes:
         write.start()
     iy = lax.axis_index("gy")
+    received[...] = arrived[...].astype(f32)
+    kept = (arrived.shape[2] - load_rows) // 2
     panel_count = tables[0].shape[0]
     high_count = panel_count // LANES
     slot_count = count_x * load_rows * LANES
@@ -533,11 +552,10 @@
                 axis=1,
             )
         )
-        stretch = received[0, piece, load_rows : load_rows + 1, :]
-        rate = received[0, piece, load_rows + 1 : load_rows + 2, :]
+        sums = received[0, piece, load_rows:, :]
         for i in range(1, count_x):
-            stretch = stretch + received[i, piece, load_rows : load_rows + 1, :]
-            rate = rate + received[i, piece, load_rows + 1 : load_rows + 2, :]
+            sums = sums + received[i, piece, load_rows:, :]
+        stretch, rate = unfolded(sums[:kept] + sums[kept:], damper_count)
         viscous, hysteretic, held_state = damper_rows(smalls[q], slot_count, width)
         hysteresis, force = respond(stretch, rate, held_state, viscous, hysteretic)
         hysteresis_out[q] = hysteresis
@@ -554,13 +572,13 @@
     state[1:2, :] = velocity
     state[2:3, :] = panel_modal
     state[3:4, :] = panel_modal
-    message = drift_times(displacement, velocity, shapes)
+    message = folded(drift_times(displacement, velocity, shapes), damper_count)
     payload[...] = jnp.broadcast_to(message[None], payload.shape)
     for write in writes:
         write.wait()
 
 
-def second_kernel(count_x, count_y, slot_count, *refs):
+def second_kernel(count_x, count_y, slot_count, damper_count, *refs):
     received, shapes, frequency, ratio, state, held = refs[:6]
     smalls = refs[6 : 6 + count_y]
     modal, damper = refs[6 + count_y :]
@@ -568,11 +586,10 @@
     forces = []
     for q in range(count_y):
         piece = lax.rem(iy + q, count_y)
-        stretch = received[0, piece, 0:1, :]
-        rate = received[0, piece, 1:2, :]
+        sums = received[0, piece]
         for i in range(1, count_x):
-            stretch = stretch + received[i, piece, 0:1, :]
-            rate = rate + received[i, piece, 1:2, :]
+            sums = sums + received[i, piece]
+        stretch, rate = unfolded(sums, damper_count)
         viscous, hysteretic, _ = damper_rows(smalls[q], slot_count, stretch.shape[1])
         hysteresis, force = respond(stretch, rate, held[q], viscous, hysteretic)
         if q == 0:
@@ -766,11 +783,13 @@
         pressure_next, *smalls,
     )
 
+    kept = 1 if 2 * damper_count <= damper_padded else 2
+
     def edge(is_near, result, *operands):
         kept = (velocity_next, pressure_next, old, mid, visc)
         base = len(operands)
         return pl.pallas_call(
-            functools.partial(edge_kernel, count_x, count_y, is_near),
+            functools.partial(edge_kernel, count_x, count_y, damper_count, is_near),
             out_shape=(
                 pltpu.VMEM(velocity.shape, f32),
                 pltpu.VMEM(pressure.shape, f32),
@@ -798,7 +817,7 @@
     )
     velocity_next, pressure_next, payload, *_ = edge(
         False,
-        shape((total, load_rows + 2, LANES), f32),
+        shape((total, load_rows + 2 * kept, LANES), bf16),
         far_message,
         wind,
         pick,
@@ -807,14 +826,14 @@
         partial,
     )
     received = lax.all_to_all(payload, both, 0, 0, tiled=True)
-    received = received.reshape(count_x, count_y, load_rows + 2, LANES)
+    received = received.reshape(count_x, count_y, load_rows + 2 * kept, LANES)
 
     frequency = frequency[None]
     damping_ratio = damping_ratio[None]
     payload, state, hysteresis, velocity_next, pressure_next = pl.pallas_call(
-        functools.partial(first_kernel, count_x, count_y, load_rows),
+        functools.partial(first_kernel, count_x, count_y, load_rows, damper_count),
         out_shape=(
-            shape((total, 2, damper_padded), f32),
+            shape((total, kept, damper_padded), f32),
             shape((4, mode_count), f32),
             shape((count_y, 1, damper_padded), f32),
             shape(velocity.shape, f32),
@@ -822,7 +841,10 @@
         ),
         in_specs=[whole()] * (7 + 3 * count_y),
         out_specs=(whole(),) * 3 + (whole(pl.ANY),) * 2,
-        scratch_shapes=[pltpu.SemaphoreType.DMA((2,))],
+        scratch_shapes=[
+            pltpu.VMEM((count_x, count_y, load_rows + 2 * kept, LANES), f32),
+            pltpu.SemaphoreType.DMA((2,)),
+        ],
         compiler_params=params,
         name="first",
     )(
@@ -830,10 +852,10 @@
         *smalls, *tables, *spreads, velocity_next, pressure_next,
     )
     received = lax.all_to_all(payload, both, 0, 0, tiled=True)
-    received = received.reshape(count_x, count_y, 2, damper_padded)
+    received = received.reshape(count_x, count_y, kept, damper_padded)
 
     modal_next, damper_next = pl.pallas_call(
-        functools.partial(second_kernel, count_x, count_y, slot_count),
+        functools.partial(second_kernel, count_x, count_y, slot_count, damper_count),
         out_shape=(
             shape((2, mode_count), f32),
             shape((1, damper_count), f32),

time: 41.8 us -> 41.5 us (level)
  no operation moved by 1% of the time
where the time goes in v8:
time: 41.5 us; the launch traced here: 41.3 us
  blocking collectives  24.8 us (60%)
  Pallas kernels  11 us (27%)
  starting transfers between devices  4.47 us (11%)
  between operations  0.92 us (2%)
    all_to_all x2, blocking collectives, body(): received = lax.all_to_all(payload, both, 0, 0, tiled=True)  24.8 us
    pallas_call x1, Pallas kernels, body(): pl.pallas_call(functools.partial(inner_kernel, count_y), out_shape=(pltpu...  4.79 us
    ppermute x1, starting transfers between devices, body(): near_message = lax.ppermute(near_message, 'gx', pairs(count_x, 0))  2.56 us
    pallas_call x1, Pallas kernels, body(): pl.pallas_call(functools.partial(pack_kernel, starts), out_shape=(pltpu.V...  1.46 us
    pallas_call x2, Pallas kernels, edge(): pl.pallas_call(functools.partial(edge_kernel, count_x, count_y, damper_co...  1.45 us
    pallas_call x1, Pallas kernels, body(): pl.pallas_call(functools.partial(first_kernel, count_x, count_y, load_row...  1.3 us
    pallas_call x1, Pallas kernels, body(): pl.pallas_call(functools.partial(prepare_kernel, slot_count, damper_padde...  1.16 us
  transfers between devices with their start and end apart: 6, of which 0 were waited for; matrix products, arithmetic and copies ran while one was open for 0% of the time, Pallas kernels for 18%

profile of v8, /device:TPU:0, one launch (start us, length us, event | category | flops | bytes accessed | tf_op | source)
XLA Modules:
  0.0 41.3 jit_solution(9721852117751615630)
XLA Ops:
  0.6 0.0 copy-start.3
  0.6 0.0 copy-start.8
  0.7 0.0 copy-start
  0.7 0.0 copy-start.1
  0.7 0.0 copy-start.12
  0.7 0.0 copy-start.9
  0.7 0.0 copy-start.10
  0.7 0.0 copy-start.4
  0.7 0.0 copy-start.11
  0.7 0.0 copy-start.2
  0.7 0.0 copy-start.7
  0.7 1.5 %pack.1 = (bf16[432,256]{1,0:T(8,128)(2,1)S(1)}, bf16[448,256]{1,0:T(8,128)(2,1)S(1)}, f32[5,8,8,256]{3,2,1,0:T(8,128)S(1)}, bf16[16,256]{1,0:T(8,128)(2,1)S(1)}) custom-call(f32[3,8,48,256]{3,2,1,0:T(8,128)} %vel.3, f32[8,48,256]{2,1,0:T(8,128)} %pre.3, f32[8,48,256]{2,1,0:T(8,128)} %vis.3), custom_call_target="tpu_custom_call" | custom-call | tf_op jit(solution)/shard_map/pack/pallas_call | solution.py:660
  2.2 0.5 %collective-permute-start = (f32[5,8,8,256]{3,2,1,0:T(8,128)S(1)}, f32[5,8,8,256]{3,2,1,0:T(8,128)S(1)}, u32[]{:S(2)}, u32[]{:S(2)}) collective-permute-start(f32[5,8,8,256]{3,2,1,0:T(8,128)S(1)} %get-tuple-element.48), channel_id=1, source_target_pairs={{0,1},{1,0},{2,3},{3,2},{4,5},{5,4},{6,7},{7,6},{8,9},{9,8},{10,11... | collective-permute-start | bytes 983048 | tf_op jit(solution)/shard_map/ppermute | solution.py:652
  2.7 2.6 %collective-permute-start.3 = (bf16[432,256]{1,0:T(8,128)(2,1)S(1)}, bf16[432,256]{1,0:T(8,128)(2,1)S(1)}, u32[]{:S(2)}, u32[]{:S(2)}) collective-permute-start(bf16[432,256]{1,0:T(8,128)(2,1)S(1)} %get-tuple-element.63), channel_id=1, source_target_pairs={{0,2},{4,6},{8,10},{12,14},{16,18},{20,22},{24,26},{28,30},{2,0},{... | collective-permute-start | bytes 663560 | tf_op jit(solution)/shard_map/ppermute | solution.py:675
  5.3 0.1 collective-permute-start.4
  5.4 0.0 collective-permute-done.left.right
  5.4 0.0 copy-done.8
  5.4 0.7 %collective-permute-start.1 = (bf16[448,256]{1,0:T(8,128)(2,1)S(1)}, bf16[448,256]{1,0:T(8,128)(2,1)S(1)}, u32[]{:S(2)}, u32[]{:S(2)}) collective-permute-start(bf16[448,256]{1,0:T(8,128)(2,1)S(1)} %corner.1), channel_id=1, source_target_pairs={{2,4},{6,8},{10,12},{14,16},{18,20},{22,24},{26,28},{4,2},{8,6},{1... | collective-permute-start | bytes 688136 | tf_op jit(solution)/shard_map/ppermute | solution.py:697
  6.1 0.0 copy-done
  6.1 0.2 collective-permute-start.5
  6.3 0.0 copy-done.9
  6.3 0.0 copy-done.10
  6.3 0.0 copy-done.11
  6.4 0.0 copy-done.12
  6.4 0.4 %collective-permute-start.2 = (f32[1,4608]{1,0:T(1,128)S(1)}, f32[1,4608]{1,0:T(1,128)S(1)}, u32[]{:S(2)}, u32[]{:S(2)}) collective-permute-start(f32[1,4608]{1,0:T(1,128)S(1)} %constant_dynamic-update-slice_fusion.refs_0_.refs_5_.refs_6_), channel_id=1, source_target_pairs={{1,0},{0,1},{3,2},{2,3},{5,4},{4,5},{7,6},{6,7},{9,8},{8,9},{11,10... | collective-permute-start | bytes 55304 | tf_op jit(solution)/shard_map/ppermute | solution.py:715
  6.8 0.0 copy-done.2
  6.8 4.8 %inner.1 = (f32[3,8,48,256]{3,2,1,0:T(8,128)S(1)}, f32[2,4,5,64,256]{4,3,2,1,0:T(8,128)S(1)}, f32[2,4,5,64,256]{4,3,2,1,0:T(8,128)S(1)}, f32[2,5,64,256]{3,2,1,0:T(8,128)S(1)}, f32[8,48,256]{2,1,0:T(8,128)S(1)}) custom-call(f32[3,8,48,256]{3,2,1,0:T(8,128)} %vel.3, f32[8,48,256]{2,1,0:T(8,128)} %pre.3, f32[8,48,256]{2,1,0:T(8,128)} %vis.3, ...), custom_call_target="tpu_custom_call" | custom-call | tf_op jit(solution)/shard_map/inner/pallas_call | solution.py:746
  11.6 0.0 collective-permute-done.2.refs_1_.refs_6_.refs_7_
  11.7 0.0 copy-done.3
  11.7 0.0 copy-done.1
  11.7 0.0 copy-done.4
  11.7 0.0 copy-done.7
  11.7 1.2 %prepare.1 = (bf16[2,2,128,128]{3,2,1,0:T(8,128)(2,1)S(1)}, f32[2,128]{1,0:T(2,128)S(1)}, bf16[2,256,96]{2,1,0:T(8,128)(2,1)S(1)}, f32[256,256]{1,0:T(8,128)S(1)...) custom-call(s32[1,256]{1,0:T(1,128)S(1)} %constant_dynamic-slice_fusion.own_ids, ...), custom_call_target="tpu_custom_call" | custom-call | tf_op jit(solution)/shard_map/prepare/pallas_call | solution.py:767
  12.9 0.0 collective-permute-done.4.refs_0_.refs_1_
  12.9 0.0 collective-permute-done.3.message
  12.9 0.7 %near.1 = (f32[3,8,48,256]{3,2,1,0:T(8,128)S(1)}, f32[8,48,256]{2,1,0:T(8,128)S(1)}, f32[256,256]{1,0:T(8,128)S(1)}, f32[2,4,5,64,256]{4,3,2,1,0:T(8,128)S(1)}, ...) custom-call(bf16[432,256]{1,0:T(8,128)(2,1)S(1)} %collective-permute, ...), custom_call_target="tpu_custom_call", output_to_operand_aliasing={{0}: (6, {}), {1}: (7, {}), {3}: (8, {}), {4}: (9, {}), {5}... | custom-call | tf_op jit(solution)/shard_map/near/pallas_call | solution.py:791
  13.6 0.0 collective-permute-done.1.message
  13.6 0.0 copy-start.5
  13.6 0.0 copy-start.6
  13.6 0.8 %far.1 = (f32[3,8,48,256]{3,2,1,0:T(8,128)S(1)}, f32[8,48,256]{2,1,0:T(8,128)S(1)}, bf16[32,4,128]{2,1,0:T(4,128)(2,1)S(1)}, f32[2,4,5,64,256]{4,3,2,1,0:T(8,128...) custom-call(bf16[448,256]{1,0:T(8,128)(2,1)S(1)} %collective-permute, ...), custom_call_target="tpu_custom_call", output_to_operand_aliasing={{0}: (6, {}), {1}: (7, {}), {3}: (8, {}), {4}: (9, {}), {5}... | custom-call | tf_op jit(solution)/shard_map/far/pallas_call | solution.py:791
  14.4 16.0 %all_to_all.10 = bf16[32,4,128]{2,1,0:T(4,128)(2,1)S(1)} all-to-all(bf16[32,4,128]{2,1,0:T(4,128)(2,1)S(1)} %get-tuple-element.78), channel_id=1, replica_groups=mesh['gx'=16,'gy'=2] {'gx','gy'}, dimensions={0} | all-to-all | bytes 65536 | tf_op jit(solution)/shard_map/all_to_all | solution.py:828
  30.4 0.0 collective-permute-done.5.refs_8_
  30.4 0.0 copy-done.5
  30.4 0.0 copy-done.6
  30.4 1.3 %first.1 = (f32[32,1,128]{2,1,0:T(1,128)S(1)}, f32[4,128]{1,0:T(4,128)S(1)}, f32[2,1,128]{2,1,0:T(1,128)S(1)}, f32[3,8,48,256]{3,2,1,0:T(8,128)}, f32[8,48,256]{2,1,0:T(8,128)}) custom-call(bf16[16,2,4,128]{3,2,1,0:T(4,128)(2,1)S(1)} %bitcast.15, bf16[2,2,128,128]{3,2,1,0:T(8,128)(2,1)S(1)} %get-tuple-element.79.refs_1_, f32[2,128]{1,0:T(2,128)S(1)} %copy-done.4, ...), custom_call_target="tpu_custom_call" | custom-call | tf_op jit(solution)/shard_map/first/pallas_call | solution.py:833
  31.7 8.8 %all_to_all.11 = f32[32,1,128]{2,1,0:T(1,128)S(1)} all-to-all(f32[32,1,128]{2,1,0:T(1,128)S(1)} %get-tuple-element.87), channel_id=1, replica_groups=mesh['gx'=16,'gy'=2] {'gx','gy'}, dimensions={0} | all-to-all | bytes 32768 | tf_op jit(solution)/shard_map/all_to_all | solution.py:854
  40.5 0.8 %second.1 = (f32[2,128]{1,0:T(2,128)}, f32[1,64]{1,0:T(1,128)}) custom-call(f32[16,2,1,128]{3,2,1,0:T(1,128)S(1)} %bitcast.16, bf16[2,2,128,128]{3,2,1,0:T(8,128)(2,1)S(1)} %get-tuple-element.79.refs_1_, f32[1,128]{1,0:T(1,128)S(1)} %bitcast.22, f32[1,128]{1,0:T(1,128)S(1)} %bitcast.24, f32[4,128]{1,0:T(4,128)S(1)} %get-tuple-element.88.refs_4_, ...), custom_call_target="tpu_custom_call" | custom-call | tf_op jit(solution)/shard_map/second/pallas_call | solution.py:857
  (8 shorter events, 0.1 us)
Async XLA Ops:
  0.6 11.0 %copy-start.3 = (f32[2048]{0:T(1024)S(1)}, f32[2048]{0:T(1024)}, u32[]{:S(2)}) copy-start(f32[2048]{0:T(1024)} %param.20) | copy-start | bytes 24580
  0.6 4.7 %copy-start.8 = (s32[1,4096]{1,0:T(1,128)S(1)}, s32[1,4096]{1,0:T(1,128)}, u32[]{:S(2)}) copy-start(s32[1,4096]{1,0:T(1,128)} %param.22) | copy-start | bytes 49156
  0.7 5.5 %copy-start = (bf16[2048,128]{1,0:T(8,128)(2,1)S(1)}, bf16[2048,128]{1,0:T(8,128)(2,1)}, u32[]{:S(2)}) copy-start(bf16[2048,128]{1,0:T(8,128)(2,1)} %refs_7_) | copy-start | bytes 1572868
  0.7 11.0 %copy-start.1 = (bf16[1024,128]{1,0:T(8,128)(2,1)S(1)}, bf16[1024,128]{1,0:T(8,128)(2,1)}, u32[]{:S(2)}) copy-start(bf16[1024,128]{1,0:T(8,128)(2,1)} %nodes) | copy-start | bytes 786436
  0.7 5.7 %copy-start.12 = (s32[64]{0:T(128)S(1)}, s32[64]{0:T(128)}, u32[]{:S(2)}) copy-start(s32[64]{0:T(128)} %param.25) | copy-start | bytes 772
  0.7 5.6 %copy-start.9 = (f32[64]{0:T(128)S(1)}, f32[64]{0:T(128)}, u32[]{:S(2)}) copy-start(f32[64]{0:T(128)} %param.26) | copy-start | bytes 772
  0.7 5.6 %copy-start.10 = (f32[64]{0:T(128)S(1)}, f32[64]{0:T(128)}, u32[]{:S(2)}) copy-start(f32[64]{0:T(128)} %param.27) | copy-start | bytes 772
  0.7 11.0 %copy-start.4 = (f32[2,128]{1,0:T(2,128)S(1)}, f32[2,128]{1,0:T(2,128)}, u32[]{:S(2)}) copy-start(f32[2,128]{1,0:T(2,128)} %refs_2_) | copy-start | bytes 3076
  0.7 5.6 %copy-start.11 = (f32[64]{0:T(128)S(1)}, f32[64]{0:T(128)}, u32[]{:S(2)}) copy-start(f32[64]{0:T(128)} %param.31) | copy-start | bytes 772
  0.7 6.1 %copy-start.2 = (f32[256]{0:T(256)S(1)}, f32[256]{0:T(256)}, u32[]{:S(2)}) copy-start(f32[256]{0:T(256)} %param.19) | copy-start | bytes 3076
  0.7 11.0 %copy-start.7 = (s32[1,256]{1,0:T(1,128)S(1)}, s32[1,256]{1,0:T(1,128)}, u32[]{:S(2)}) copy-start(s32[1,256]{1,0:T(1,128)} %cell.1) | copy-start | bytes 3076
  2.2 3.2 %collective-permute-start = (f32[5,8,8,256]{3,2,1,0:T(8,128)S(1)}, f32[5,8,8,256]{3,2,1,0:T(8,128)S(1)}, u32[]{:S(2)}, u32[]{:S(2)}) collective-permute-start(f32[5,8,8,256]{3,2,1,0:T(8,128)S(1)} %get-tuple-element.48), channel_id=1, source_target_pairs={{0,1},{1,0},{2,3},{3,2},{4,5},{5,4},{6,7},{7,6},{8,9},{9,8},{10,11... | collective-permute-start | bytes 983048 | tf_op jit(solution)/shard_map/ppermute | solution.py:652
  2.7 10.1 %collective-permute-start.3 = (bf16[432,256]{1,0:T(8,128)(2,1)S(1)}, bf16[432,256]{1,0:T(8,128)(2,1)S(1)}, u32[]{:S(2)}, u32[]{:S(2)}) collective-permute-start(bf16[432,256]{1,0:T(8,128)(2,1)S(1)} %get-tuple-element.63), channel_id=1, source_target_pairs={{0,2},{4,6},{8,10},{12,14},{16,18},{20,22},{24,26},{28,30},{2,0},{... | collective-permute-start | bytes 663560 | tf_op jit(solution)/shard_map/ppermute | solution.py:675
  5.3 7.6 %collective-permute-start.4 = (bf16[16,256]{1,0:T(8,128)(2,1)S(1)}, bf16[16,256]{1,0:T(8,128)(2,1)S(1)}, u32[]{:S(2)}, u32[]{:S(2)}) collective-permute-start(bf16[16,256]{1,0:T(8,128)(2,1)S(1)} %get-tuple-element.64), channel_id=1, source_target_pairs={{0,3},{4,7},{8,11},{12,15},{16,19},{20,23},{24,27},{28,31},{2,1},{... | collective-permute-start | bytes 24584 | tf_op jit(solution)/shard_map/ppermute | solution.py:708
  5.4 8.1 %collective-permute-start.1 = (bf16[448,256]{1,0:T(8,128)(2,1)S(1)}, bf16[448,256]{1,0:T(8,128)(2,1)S(1)}, u32[]{:S(2)}, u32[]{:S(2)}) collective-permute-start(bf16[448,256]{1,0:T(8,128)(2,1)S(1)} %corner.1), channel_id=1, source_target_pairs={{2,4},{6,8},{10,12},{14,16},{18,20},{22,24},{26,28},{4,2},{8,6},{1... | collective-permute-start | bytes 688136 | tf_op jit(solution)/shard_map/ppermute | solution.py:697
  6.1 24.3 %collective-permute-start.5 = (bf16[2048,128]{1,0:T(8,128)(2,1)S(1)}, bf16[2048,128]{1,0:T(8,128)(2,1)S(1)}, u32[]{:S(2)}, u32[]{:S(2)}) collective-permute-start(bf16[2048,128]{1,0:T(8,128)(2,1)S(1)} %copy-done), channel_id=1, source_target_pairs={{1,0},{0,1},{3,2},{2,3},{5,4},{4,5},{7,6},{6,7},{9,8},{8,9},{11,10... | collective-permute-start | bytes 1572872 | tf_op jit(solution)/shard_map/ppermute | solution.py:715
  6.4 5.2 %collective-permute-start.2 = (f32[1,4608]{1,0:T(1,128)S(1)}, f32[1,4608]{1,0:T(1,128)S(1)}, u32[]{:S(2)}, u32[]{:S(2)}) collective-permute-start(f32[1,4608]{1,0:T(1,128)S(1)} %constant_dynamic-update-slice_fusion.refs_0_.refs_5_.refs_6_), channel_id=1, source_target_pairs={{1,0},{0,1},{3,2},{2,3},{5,4},{4,5},{7,6},{6,7},{9,8},{8,9},{11,10... | collective-permute-start | bytes 55304 | tf_op jit(solution)/shard_map/ppermute | solution.py:715
  13.6 16.8 %copy-start.5 = (f32[128]{0:T(128)S(1)}, f32[128]{0:T(128)}, u32[]{:S(2)}) copy-start(f32[128]{0:T(128)} %param.28) | copy-start | bytes 1540
  13.6 16.8 %copy-start.6 = (f32[128]{0:T(128)S(1)}, f32[128]{0:T(128)}, u32[]{:S(2)}) copy-start(f32[128]{0:T(128)} %param.29) | copy-start | bytes 1540

commit v9 on v8

--- a/solution.py
+++ b/solution.py
@@ -349,7 +349,7 @@
 
     flat = pre_out[pl.ds(side * (layers - 2), 2)].reshape(2 * rows, height)
     total = found[...]
-    for part in parts_of(flat):
+    for part in parts_of(flat)[:2]:
         total = total + jnp.dot(pick[side], part.astype(bf16), preferred_element_type=f32)
     if is_near:
         found_out[...] = total

time: 41.5 us -> 41.5 us (level)
  no operation moved by 1% of the time
where the time goes in v9:
time: 41.5 us; the launch traced here: 41.3 us
  blocking collectives  24.9 us (60%)
  Pallas kernels  10.9 us (26%)
  starting transfers between devices  4.47 us (11%)
  between operations  0.92 us (2%)
    all_to_all x2, blocking collectives, body(): received = lax.all_to_all(payload, both, 0, 0, tiled=True)  24.9 us
    pallas_call x1, Pallas kernels, body(): pl.pallas_call(functools.partial(inner_kernel, count_y), out_shape=(pltpu...  4.79 us
    ppermute x1, starting transfers between devices, body(): near_message = lax.ppermute(near_message, 'gx', pairs(count_x, 0))  2.56 us
    pallas_call x1, Pallas kernels, body(): pl.pallas_call(functools.partial(pack_kernel, starts), out_shape=(pltpu.V...  1.46 us
    pallas_call x2, Pallas kernels, edge(): pl.pallas_call(functools.partial(edge_kernel, count_x, count_y, damper_co...  1.38 us
    pallas_call x1, Pallas kernels, body(): pl.pallas_call(functools.partial(first_kernel, count_x, count_y, load_row...  1.3 us
    pallas_call x1, Pallas kernels, body(): pl.pallas_call(functools.partial(prepare_kernel, slot_count, damper_padde...  1.16 us
  transfers between devices with their start and end apart: 6, of which 0 were waited for; matrix products, arithmetic and copies ran while one was open for 0% of the time, Pallas kernels for 18%

profile of v9, /device:TPU:0, one launch (start us, length us, event | category | flops | bytes accessed | tf_op | source)
XLA Modules:
  0.0 41.3 jit_solution(6164196374142123290)
XLA Ops:
  0.6 0.0 copy-start.3
  0.6 0.0 copy-start.8
  0.7 0.0 copy-start
  0.7 0.0 copy-start.1
  0.7 0.0 copy-start.12
  0.7 0.0 copy-start.9
  0.7 0.0 copy-start.10
  0.7 0.0 copy-start.4
  0.7 0.0 copy-start.11
  0.7 0.0 copy-start.2
  0.7 0.0 copy-start.7
  0.7 1.5 %pack.1 = (bf16[432,256]{1,0:T(8,128)(2,1)S(1)}, bf16[448,256]{1,0:T(8,128)(2,1)S(1)}, f32[5,8,8,256]{3,2,1,0:T(8,128)S(1)}, bf16[16,256]{1,0:T(8,128)(2,1)S(1)}) custom-call(f32[3,8,48,256]{3,2,1,0:T(8,128)} %vel.3, f32[8,48,256]{2,1,0:T(8,128)} %pre.3, f32[8,48,256]{2,1,0:T(8,128)} %vis.3), custom_call_target="tpu_custom_call" | custom-call | tf_op jit(solution)/shard_map/pack/pallas_call | solution.py:660
  2.2 0.5 %collective-permute-start = (f32[5,8,8,256]{3,2,1,0:T(8,128)S(1)}, f32[5,8,8,256]{3,2,1,0:T(8,128)S(1)}, u32[]{:S(2)}, u32[]{:S(2)}) collective-permute-start(f32[5,8,8,256]{3,2,1,0:T(8,128)S(1)} %get-tuple-element.48), channel_id=1, source_target_pairs={{0,1},{1,0},{2,3},{3,2},{4,5},{5,4},{6,7},{7,6},{8,9},{9,8},{10,11... | collective-permute-start | bytes 983048 | tf_op jit(solution)/shard_map/ppermute | solution.py:652
  2.7 2.6 %collective-permute-start.3 = (bf16[432,256]{1,0:T(8,128)(2,1)S(1)}, bf16[432,256]{1,0:T(8,128)(2,1)S(1)}, u32[]{:S(2)}, u32[]{:S(2)}) collective-permute-start(bf16[432,256]{1,0:T(8,128)(2,1)S(1)} %get-tuple-element.63), channel_id=1, source_target_pairs={{0,2},{4,6},{8,10},{12,14},{16,18},{20,22},{24,26},{28,30},{2,0},{... | collective-permute-start | bytes 663560 | tf_op jit(solution)/shard_map/ppermute | solution.py:675
  5.3 0.1 collective-permute-start.4
  5.4 0.0 collective-permute-done.left.right
  5.4 0.0 copy-done.8
  5.4 0.7 %collective-permute-start.1 = (bf16[448,256]{1,0:T(8,128)(2,1)S(1)}, bf16[448,256]{1,0:T(8,128)(2,1)S(1)}, u32[]{:S(2)}, u32[]{:S(2)}) collective-permute-start(bf16[448,256]{1,0:T(8,128)(2,1)S(1)} %corner.1), channel_id=1, source_target_pairs={{2,4},{6,8},{10,12},{14,16},{18,20},{22,24},{26,28},{4,2},{8,6},{1... | collective-permute-start | bytes 688136 | tf_op jit(solution)/shard_map/ppermute | solution.py:697
  6.1 0.0 copy-done
  6.1 0.2 collective-permute-start.5
  6.3 0.0 copy-done.9
  6.3 0.0 copy-done.10
  6.3 0.0 copy-done.11
  6.4 0.0 copy-done.12
  6.4 0.4 %collective-permute-start.2 = (f32[1,4608]{1,0:T(1,128)S(1)}, f32[1,4608]{1,0:T(1,128)S(1)}, u32[]{:S(2)}, u32[]{:S(2)}) collective-permute-start(f32[1,4608]{1,0:T(1,128)S(1)} %constant_dynamic-update-slice_fusion.refs_0_.refs_5_.refs_6_), channel_id=1, source_target_pairs={{1,0},{0,1},{3,2},{2,3},{5,4},{4,5},{7,6},{6,7},{9,8},{8,9},{11,10... | collective-permute-start | bytes 55304 | tf_op jit(solution)/shard_map/ppermute | solution.py:715
  6.8 0.0 copy-done.2
  6.8 4.8 %inner.1 = (f32[3,8,48,256]{3,2,1,0:T(8,128)S(1)}, f32[2,4,5,64,256]{4,3,2,1,0:T(8,128)S(1)}, f32[2,4,5,64,256]{4,3,2,1,0:T(8,128)S(1)}, f32[2,5,64,256]{3,2,1,0:T(8,128)S(1)}, f32[8,48,256]{2,1,0:T(8,128)S(1)}) custom-call(f32[3,8,48,256]{3,2,1,0:T(8,128)} %vel.3, f32[8,48,256]{2,1,0:T(8,128)} %pre.3, f32[8,48,256]{2,1,0:T(8,128)} %vis.3, ...), custom_call_target="tpu_custom_call" | custom-call | tf_op jit(solution)/shard_map/inner/pallas_call | solution.py:746
  11.6 0.0 collective-permute-done.2.refs_1_.refs_6_.refs_7_
  11.7 0.0 copy-done.3
  11.7 0.0 copy-done.1
  11.7 0.0 copy-done.4
  11.7 0.0 copy-done.7
  11.7 1.2 %prepare.1 = (bf16[2,2,128,128]{3,2,1,0:T(8,128)(2,1)S(1)}, f32[2,128]{1,0:T(2,128)S(1)}, bf16[2,256,96]{2,1,0:T(8,128)(2,1)S(1)}, f32[256,256]{1,0:T(8,128)S(1)...) custom-call(s32[1,256]{1,0:T(1,128)S(1)} %constant_dynamic-slice_fusion.own_ids, ...), custom_call_target="tpu_custom_call" | custom-call | tf_op jit(solution)/shard_map/prepare/pallas_call | solution.py:767
  12.9 0.0 collective-permute-done.4.refs_0_.refs_1_
  12.9 0.0 collective-permute-done.3.message
  12.9 0.6 %near.1 = (f32[3,8,48,256]{3,2,1,0:T(8,128)S(1)}, f32[8,48,256]{2,1,0:T(8,128)S(1)}, f32[256,256]{1,0:T(8,128)S(1)}, f32[2,4,5,64,256]{4,3,2,1,0:T(8,128)S(1)}, ...) custom-call(bf16[432,256]{1,0:T(8,128)(2,1)S(1)} %collective-permute, ...), custom_call_target="tpu_custom_call", output_to_operand_aliasing={{0}: (6, {}), {1}: (7, {}), {3}: (8, {}), {4}: (9, {}), {5}... | custom-call | tf_op jit(solution)/shard_map/near/pallas_call | solution.py:791
  13.5 0.0 collective-permute-done.1.message
  13.5 0.0 copy-start.5
  13.5 0.0 copy-start.6
  13.6 0.7 %far.1 = (f32[3,8,48,256]{3,2,1,0:T(8,128)S(1)}, f32[8,48,256]{2,1,0:T(8,128)S(1)}, bf16[32,4,128]{2,1,0:T(4,128)(2,1)S(1)}, f32[2,4,5,64,256]{4,3,2,1,0:T(8,128...) custom-call(bf16[448,256]{1,0:T(8,128)(2,1)S(1)} %collective-permute, ...), custom_call_target="tpu_custom_call", output_to_operand_aliasing={{0}: (6, {}), {1}: (7, {}), {3}: (8, {}), {4}: (9, {}), {5}... | custom-call | tf_op jit(solution)/shard_map/far/pallas_call | solution.py:791
  14.3 16.0 %all_to_all.10 = bf16[32,4,128]{2,1,0:T(4,128)(2,1)S(1)} all-to-all(bf16[32,4,128]{2,1,0:T(4,128)(2,1)S(1)} %get-tuple-element.78), channel_id=1, replica_groups=mesh['gx'=16,'gy'=2] {'gx','gy'}, dimensions={0} | all-to-all | bytes 65536 | tf_op jit(solution)/shard_map/all_to_all | solution.py:828
  30.3 0.0 collective-permute-done.5.refs_8_
  30.3 0.0 copy-done.5
  30.3 0.0 copy-done.6
  30.3 1.3 %first.1 = (f32[32,1,128]{2,1,0:T(1,128)S(1)}, f32[4,128]{1,0:T(4,128)S(1)}, f32[2,1,128]{2,1,0:T(1,128)S(1)}, f32[3,8,48,256]{3,2,1,0:T(8,128)}, f32[8,48,256]{2,1,0:T(8,128)}) custom-call(bf16[16,2,4,128]{3,2,1,0:T(4,128)(2,1)S(1)} %bitcast.15, bf16[2,2,128,128]{3,2,1,0:T(8,128)(2,1)S(1)} %get-tuple-element.79.refs_1_, f32[2,128]{1,0:T(2,128)S(1)} %copy-done.4, ...), custom_call_target="tpu_custom_call" | custom-call | tf_op jit(solution)/shard_map/first/pallas_call | solution.py:833
  31.6 8.8 %all_to_all.11 = f32[32,1,128]{2,1,0:T(1,128)S(1)} all-to-all(f32[32,1,128]{2,1,0:T(1,128)S(1)} %get-tuple-element.87), channel_id=1, replica_groups=mesh['gx'=16,'gy'=2] {'gx','gy'}, dimensions={0} | all-to-all | bytes 32768 | tf_op jit(solution)/shard_map/all_to_all | solution.py:854
  40.5 0.8 %second.1 = (f32[2,128]{1,0:T(2,128)}, f32[1,64]{1,0:T(1,128)}) custom-call(f32[16,2,1,128]{3,2,1,0:T(1,128)S(1)} %bitcast.16, bf16[2,2,128,128]{3,2,1,0:T(8,128)(2,1)S(1)} %get-tuple-element.79.refs_1_, f32[1,128]{1,0:T(1,128)S(1)} %bitcast.22, f32[1,128]{1,0:T(1,128)S(1)} %bitcast.24, f32[4,128]{1,0:T(4,128)S(1)} %get-tuple-element.88.refs_4_, ...), custom_call_target="tpu_custom_call" | custom-call | tf_op jit(solution)/shard_map/second/pallas_call | solution.py:857
  (8 shorter events, 0.1 us)
Async XLA Ops:
  0.6 11.0 %copy-start.3 = (f32[2048]{0:T(1024)S(1)}, f32[2048]{0:T(1024)}, u32[]{:S(2)}) copy-start(f32[2048]{0:T(1024)} %param.20) | copy-start | bytes 24580
  0.6 4.7 %copy-start.8 = (s32[1,4096]{1,0:T(1,128)S(1)}, s32[1,4096]{1,0:T(1,128)}, u32[]{:S(2)}) copy-start(s32[1,4096]{1,0:T(1,128)} %param.22) | copy-start | bytes 49156
  0.7 5.5 %copy-start = (bf16[2048,128]{1,0:T(8,128)(2,1)S(1)}, bf16[2048,128]{1,0:T(8,128)(2,1)}, u32[]{:S(2)}) copy-start(bf16[2048,128]{1,0:T(8,128)(2,1)} %refs_7_) | copy-start | bytes 1572868
  0.7 11.0 %copy-start.1 = (bf16[1024,128]{1,0:T(8,128)(2,1)S(1)}, bf16[1024,128]{1,0:T(8,128)(2,1)}, u32[]{:S(2)}) copy-start(bf16[1024,128]{1,0:T(8,128)(2,1)} %nodes) | copy-start | bytes 786436
  0.7 5.7 %copy-start.12 = (s32[64]{0:T(128)S(1)}, s32[64]{0:T(128)}, u32[]{:S(2)}) copy-start(s32[64]{0:T(128)} %param.25) | copy-start | bytes 772
  0.7 5.6 %copy-start.9 = (f32[64]{0:T(128)S(1)}, f32[64]{0:T(128)}, u32[]{:S(2)}) copy-start(f32[64]{0:T(128)} %param.26) | copy-start | bytes 772
  0.7 5.6 %copy-start.10 = (f32[64]{0:T(128)S(1)}, f32[64]{0:T(128)}, u32[]{:S(2)}) copy-start(f32[64]{0:T(128)} %param.27) | copy-start | bytes 772
  0.7 11.0 %copy-start.4 = (f32[2,128]{1,0:T(2,128)S(1)}, f32[2,128]{1,0:T(2,128)}, u32[]{:S(2)}) copy-start(f32[2,128]{1,0:T(2,128)} %refs_2_) | copy-start | bytes 3076
  0.7 5.6 %copy-start.11 = (f32[64]{0:T(128)S(1)}, f32[64]{0:T(128)}, u32[]{:S(2)}) copy-start(f32[64]{0:T(128)} %param.31) | copy-start | bytes 772
  0.7 6.1 %copy-start.2 = (f32[256]{0:T(256)S(1)}, f32[256]{0:T(256)}, u32[]{:S(2)}) copy-start(f32[256]{0:T(256)} %param.19) | copy-start | bytes 3076
  0.7 11.0 %copy-start.7 = (s32[1,256]{1,0:T(1,128)S(1)}, s32[1,256]{1,0:T(1,128)}, u32[]{:S(2)}) copy-start(s32[1,256]{1,0:T(1,128)} %cell.1) | copy-start | bytes 3076
  2.2 3.2 %collective-permute-start = (f32[5,8,8,256]{3,2,1,0:T(8,128)S(1)}, f32[5,8,8,256]{3,2,1,0:T(8,128)S(1)}, u32[]{:S(2)}, u32[]{:S(2)}) collective-permute-start(f32[5,8,8,256]{3,2,1,0:T(8,128)S(1)} %get-tuple-element.48), channel_id=1, source_target_pairs={{0,1},{1,0},{2,3},{3,2},{4,5},{5,4},{6,7},{7,6},{8,9},{9,8},{10,11... | collective-permute-start | bytes 983048 | tf_op jit(solution)/shard_map/ppermute | solution.py:652
  2.7 10.1 %collective-permute-start.3 = (bf16[432,256]{1,0:T(8,128)(2,1)S(1)}, bf16[432,256]{1,0:T(8,128)(2,1)S(1)}, u32[]{:S(2)}, u32[]{:S(2)}) collective-permute-start(bf16[432,256]{1,0:T(8,128)(2,1)S(1)} %get-tuple-element.63), channel_id=1, source_target_pairs={{0,2},{4,6},{8,10},{12,14},{16,18},{20,22},{24,26},{28,30},{2,0},{... | collective-permute-start | bytes 663560 | tf_op jit(solution)/shard_map/ppermute | solution.py:675
  5.3 7.6 %collective-permute-start.4 = (bf16[16,256]{1,0:T(8,128)(2,1)S(1)}, bf16[16,256]{1,0:T(8,128)(2,1)S(1)}, u32[]{:S(2)}, u32[]{:S(2)}) collective-permute-start(bf16[16,256]{1,0:T(8,128)(2,1)S(1)} %get-tuple-element.64), channel_id=1, source_target_pairs={{0,3},{4,7},{8,11},{12,15},{16,19},{20,23},{24,27},{28,31},{2,1},{... | collective-permute-start | bytes 24584 | tf_op jit(solution)/shard_map/ppermute | solution.py:708
  5.4 8.1 %collective-permute-start.1 = (bf16[448,256]{1,0:T(8,128)(2,1)S(1)}, bf16[448,256]{1,0:T(8,128)(2,1)S(1)}, u32[]{:S(2)}, u32[]{:S(2)}) collective-permute-start(bf16[448,256]{1,0:T(8,128)(2,1)S(1)} %corner.1), channel_id=1, source_target_pairs={{2,4},{6,8},{10,12},{14,16},{18,20},{22,24},{26,28},{4,2},{8,6},{1... | collective-permute-start | bytes 688136 | tf_op jit(solution)/shard_map/ppermute | solution.py:697
  6.1 24.2 %collective-permute-start.5 = (bf16[2048,128]{1,0:T(8,128)(2,1)S(1)}, bf16[2048,128]{1,0:T(8,128)(2,1)S(1)}, u32[]{:S(2)}, u32[]{:S(2)}) collective-permute-start(bf16[2048,128]{1,0:T(8,128)(2,1)S(1)} %copy-done), channel_id=1, source_target_pairs={{1,0},{0,1},{3,2},{2,3},{5,4},{4,5},{7,6},{6,7},{9,8},{8,9},{11,10... | collective-permute-start | bytes 1572872 | tf_op jit(solution)/shard_map/ppermute | solution.py:715
  6.4 5.2 %collective-permute-start.2 = (f32[1,4608]{1,0:T(1,128)S(1)}, f32[1,4608]{1,0:T(1,128)S(1)}, u32[]{:S(2)}, u32[]{:S(2)}) collective-permute-start(f32[1,4608]{1,0:T(1,128)S(1)} %constant_dynamic-update-slice_fusion.refs_0_.refs_5_.refs_6_), channel_id=1, source_target_pairs={{1,0},{0,1},{3,2},{2,3},{5,4},{4,5},{7,6},{6,7},{9,8},{8,9},{11,10... | collective-permute-start | bytes 55304 | tf_op jit(solution)/shard_map/ppermute | solution.py:715
  13.5 16.8 %copy-start.5 = (f32[128]{0:T(128)S(1)}, f32[128]{0:T(128)}, u32[]{:S(2)}) copy-start(f32[128]{0:T(128)} %param.28) | copy-start | bytes 1540
  13.5 16.8 %copy-start.6 = (f32[128]{0:T(128)S(1)}, f32[128]{0:T(128)}, u32[]{:S(2)}) copy-start(f32[128]{0:T(128)} %param.29) | copy-start | bytes 1540
